TPU v7x, 32 devices: a whole 2x2x4 slice. The times are simulated.
32 devices in a mesh: dp: 4 (over z), row: 4 (over y, core), col: 2 (over x).
Axes of the slice: x: 2, y: 2, z: 4, core: 2. Of those that a mesh axis runs over, the one named last changes fastest.
Arguments:
- tokens: bfloat16 [8192, 1152], P('dp', ('row', 'col')), may hold values from -6 to 6
- cotangent: bfloat16 [8192, 1152], P('dp', ('row', 'col')), may hold values from -6 to 6
- weight_query: bfloat16 [1152, 1024], P('row', 'col'), may hold values from -0.1875 to 0.1875
- weight_key: bfloat16 [1152, 256], P('row', 'col'), may hold values from -0.1875 to 0.1875
- weight_value: bfloat16 [1152, 256], P('row', 'col'), may hold values from -0.1875 to 0.1875
- weight_out: bfloat16 [1024, 1152], P('col', 'row'), may hold values from -0.1875 to 0.1875
- weight_gate: bfloat16 [1152, 6912], P('row', 'col'), may hold values from -0.1875 to 0.1875
- weight_up: bfloat16 [1152, 6912], P('row', 'col'), may hold values from -0.1875 to 0.1875
- weight_down: bfloat16 [6912, 1152], P('col', 'row'), may hold values from -0.078125 to 0.078125
- gain_input: float32 [1152], P(('row', 'col')), may hold values from -0.5 to 1
- gain_attn: float32 [1152], P(('row', 'col')), may hold values from -0.5 to 1
- gain_pre: float32 [1152], P(('row', 'col')), may hold values from -0.5 to 1
- gain_post: float32 [1152], P(('row', 'col')), may hold values from -0.5 to 1
- gain_query: float32 [256], replicated, may hold values from -0.5 to 1
- gain_key: float32 [256], replicated, may hold values from -0.5 to 1
- doc_lengths: int32 [4, 3], P('dp'), may hold values from 1 to 1792, 2048 in all within a row
- block_size: int32 [1], replicated, may hold values from 128 to 512
Outputs:
- layer_out: bfloat16 [8192, 1152], P('dp', ('row', 'col'))
- grad_tokens: float32 [8192, 1152], P('dp', ('row', 'col'))
- grad_weight_query: float32 [1152, 1024], P('row', 'col')
- grad_weight_key: float32 [1152, 256], P('row', 'col')
- grad_weight_value: float32 [1152, 256], P('row', 'col')
- grad_weight_out: float32 [1024, 1152], P('col', 'row')
- grad_weight_gate: float32 [1152, 6912], P('row', 'col')
- grad_weight_up: float32 [1152, 6912], P('row', 'col')
- grad_weight_down: float32 [6912, 1152], P('col', 'row')
- grad_gain_input: float32 [1152], P(('row', 'col'))
- grad_gain_attn: float32 [1152], P(('row', 'col'))
- grad_gain_pre: float32 [1152], P(('row', 'col'))
- grad_gain_post: float32 [1152], P(('row', 'col'))
- grad_gain_query: float32 [256], replicated
- grad_gain_key: float32 [256], replicated
Inputs may be any that keep to these rules, and one draw needn't show every extreme that they name: `doc_lengths`: each row sums to 2048; its longest document has exactly 1792 tokens. `block_size`: one block size for all documents.
All inputs are finite; a program needn't handle non-finite values.
Results may differ from a plain program's by a relative error of at most 0.017.
Values may be sent and summed in bfloat16 or wider, within the bound.
A program may use at most 192 MiB of HBM per device.

v0:
```python
import math

import jax
import jax.numpy as jnp
from jax import lax
from jax.sharding import PartitionSpec as P

D = 1152
HD = 256


EPS = 1e-06
ROPE_BASE = 1000000.0
GELU_C = 0.7978845608028654


def gelu_tanh(values):
    return 0.5 * values * (1.0 + jnp.tanh(GELU_C * (values + 0.044715 * values * values * values)))


def rotate(values, cos_table, sin_table):
    half_width = values.shape[-1] // 2
    first_half = values[..., :half_width]
    second_half = values[..., half_width:]
    return jnp.concatenate(
        [
            first_half * cos_table - second_half * sin_table,
            second_half * cos_table + first_half * sin_table,
        ],
        axis=-1,
    )


def head_norm(values, scales, cos_table, sin_table):
    mean_square = jnp.mean(values * values, axis=-1, keepdims=True)
    return rotate(values * lax.rsqrt(mean_square + EPS) * (1.0 + scales), cos_table, sin_table)


def positions(lengths, tok_count):
    doc_ends = jnp.cumsum(lengths, dtype=jnp.int32)
    doc_starts = doc_ends - lengths
    token_ids = jnp.arange(tok_count, dtype=jnp.int32)
    document = jnp.sum(
        (token_ids[:, None] >= doc_ends[None, :]).astype(jnp.int32), axis=1, dtype=jnp.int32
    )
    doc_ids = jnp.arange(lengths.shape[0], dtype=jnp.int32)
    doc_first = jnp.sum(
        jnp.where(doc_ids[None, :] == document[:, None], doc_starts[None, :], 0),
        axis=1,
        dtype=jnp.int32,
    )
    return (document, token_ids - doc_first)


def angles(places):
    half_width = HD // 2
    frequency = jnp.exp(
        jnp.arange(half_width, dtype=jnp.float32) * (-2.0 * math.log(ROPE_BASE) / HD)
    )
    phases = places.astype(jnp.float32)[:, None] * frequency[None, :]
    return (jnp.cos(phases), jnp.sin(phases))


def feature_sum(values):
    return lax.psum(jnp.sum(values, axis=1), ("row", "col"))


def wide_norm(values, scales):
    inverse = lax.rsqrt(feature_sum(values * values) / D + EPS)[:, None]
    return (values * inverse * (1.0 + scales), inverse)


def wide_norm_back(values, scales, inverse, upstream):
    scaled = upstream * (1.0 + scales)
    inner = feature_sum(scaled * values)[:, None] / D
    grad_values = scaled * inverse - values * inverse * inverse * inverse * inner
    return (grad_values, jnp.sum(upstream * values * inverse, axis=0))


def column_gather(values):
    return lax.all_gather(values, "col", axis=1, tiled=True)


def column_sums(values):
    return lax.psum_scatter(values, "col", scatter_dimension=1, tiled=True)


def row_gather(values):
    return lax.all_gather(values, "row", axis=2, tiled=True)


def row_sums(values):
    return lax.psum_scatter(values, "row", scatter_dimension=2, tiled=True)


def token_sums(term_fn, tok_count):
    return lax.psum_scatter(
        term_fn(jnp.int32(0), tok_count * lax.axis_size("row")),
        "row",
        scatter_dimension=0,
        tiled=True,
    )


def token_gather(values):
    return lax.all_gather(values, "row", axis=0, tiled=True)


def body(
    tokens,
    cotangent,
    weight_query,
    weight_key,
    weight_value,
    weight_out,
    weight_gate,
    weight_up,
    weight_down,
    gain_input,
    gain_attn,
    gain_pre,
    gain_post,
    gain_query,
    gain_key,
    doc_lengths,
    block_size,
):
    tok_count = tokens.shape[0]
    local_rows = tok_count // lax.axis_size("row")
    head_count = weight_query.shape[1] // HD
    kv_width = weight_key.shape[1]
    row_start = lax.axis_index("row") * local_rows
    col_start = lax.axis_index("col") * kv_width
    query_scale = 1.0 / math.sqrt(HD)
    document, places = positions(doc_lengths[0], tok_count)
    block_span = block_size[0]
    cos_table, sin_table = angles(places)
    my_document = lax.dynamic_slice_in_dim(document, row_start, local_rows, 0)
    my_places = lax.dynamic_slice_in_dim(places, row_start, local_rows, 0)
    cos_local = lax.dynamic_slice_in_dim(cos_table, row_start, local_rows, 0)[:, None, :]
    sin_local = lax.dynamic_slice_in_dim(sin_table, row_start, local_rows, 0)[:, None, :]
    allowed = (my_document[:, None] == document[None, :]) & (
        places[None, :] // block_span <= my_places[:, None] // block_span
    )
    inputs = tokens.astype(jnp.float32)
    normed, inverse_in = wide_norm(inputs, gain_input)
    normed_cols = column_gather(normed.astype(jnp.bfloat16))

    def query_term(first_row, row_count):
        return jnp.dot(normed_cols, weight_query, preferred_element_type=jnp.float32)

    query_pre = token_sums(query_term, local_rows).reshape(local_rows, head_count, HD)
    key_part = jnp.dot(normed_cols, weight_key, preferred_element_type=jnp.float32)
    value_part = jnp.dot(normed_cols, weight_value, preferred_element_type=jnp.float32)
    key_half, value_half = lax.psum((key_part, value_part), "row")
    key_pre, value_pre = (
        lax.all_gather(key_half, "col", axis=1, tiled=True),
        lax.all_gather(value_half, "col", axis=1, tiled=True),
    )
    query_bf = (head_norm(query_pre, gain_query, cos_local, sin_local) * query_scale).astype(
        jnp.bfloat16
    )
    keys_bf = head_norm(key_pre, gain_key, cos_table, sin_table).astype(jnp.bfloat16)
    values_bf = value_pre.astype(jnp.bfloat16)

    def attention_scores():
        raw_scores = jnp.einsum(
            "thd,sd->hts", query_bf, keys_bf, preferred_element_type=jnp.float32
        )
        return jnp.where(allowed[None, :, :], raw_scores, -1e30)

    scores = attention_scores()
    row_peak = jnp.max(scores, axis=-1, keepdims=True)
    exp_scores = jnp.exp(scores - row_peak)
    totals = jnp.sum(exp_scores, axis=-1, keepdims=True)
    log_total = row_peak + jnp.log(totals)
    probs_bf = (exp_scores / totals).astype(jnp.bfloat16)
    head_out = jnp.einsum("hts,sd->thd", probs_bf, values_bf, preferred_element_type=jnp.float32)
    head_bf = head_out.astype(jnp.bfloat16).reshape(local_rows, head_count * HD)
    heads_all = token_gather(head_bf)
    attn_out = column_sums(jnp.dot(heads_all, weight_out, preferred_element_type=jnp.float32))
    attn_normed, inverse_attn = wide_norm(attn_out, gain_attn)
    residual = inputs + attn_normed
    pre_normed, inverse_pre = wide_norm(residual, gain_pre)
    pre_cols = column_gather(pre_normed.astype(jnp.bfloat16))
    stacked = jnp.stack([weight_gate, weight_up], axis=1)
    gate_up = row_sums(
        jnp.einsum("td,dgf->tgf", pre_cols, stacked, preferred_element_type=jnp.float32)
    )
    gate_rows = gate_up[:, 0, :]
    up_rows = gate_up[:, 1, :]
    hidden_bf = (gelu_tanh(gate_rows) * up_rows).astype(jnp.bfloat16)
    hidden_all = row_gather(hidden_bf[:, None, :])[:, 0, :]
    mlp_out = column_sums(jnp.dot(hidden_all, weight_down, preferred_element_type=jnp.float32))
    mlp_normed, inverse_post = wide_norm(mlp_out, gain_post)
    layer_out = residual + mlp_normed
    upstream = cotangent.astype(jnp.float32)
    grad_mlp, grad_gain_post = wide_norm_back(mlp_out, gain_post, inverse_post, upstream)
    grad_mlp_cols = column_gather(grad_mlp.astype(jnp.bfloat16))
    grad_weight_down = jnp.einsum(
        "tf,td->fd", hidden_all, grad_mlp_cols, preferred_element_type=jnp.float32
    )
    hidden_part = jnp.einsum(
        "td,fd->tf", grad_mlp_cols, weight_down, preferred_element_type=jnp.float32
    )
    grad_hidden = row_sums(hidden_part[:, None, :])[:, 0, :]
    unused_gelu, pull_gelu = jax.vjp(
        lambda gate_in, up_in: gelu_tanh(gate_in) * up_in, gate_rows, up_rows
    )
    grad_gate, grad_up = pull_gelu(grad_hidden)
    grad_gate_up = jnp.stack([grad_gate, grad_up], axis=1).astype(jnp.bfloat16)
    grad_gate_all = row_gather(grad_gate_up)
    grad_stacked = jnp.einsum(
        "td,tgf->dgf", pre_cols, grad_gate_all, preferred_element_type=jnp.float32
    )
    grad_pre_part = jnp.einsum(
        "tgf,dgf->td", grad_gate_all, stacked, preferred_element_type=jnp.float32
    )
    grad_pre = column_sums(grad_pre_part)
    grad_resid, grad_gain_pre = wide_norm_back(residual, gain_pre, inverse_pre, grad_pre)
    grad_resid = grad_resid + upstream
    grad_attn, grad_gain_attn = wide_norm_back(attn_out, gain_attn, inverse_attn, grad_resid)
    grad_attn_cols = column_gather(grad_attn.astype(jnp.bfloat16))
    grad_weight_out = jnp.einsum(
        "te,td->ed", heads_all, grad_attn_cols, preferred_element_type=jnp.float32
    )

    def head_term(first_row, row_count):
        return jnp.einsum(
            "td,ed->te", grad_attn_cols, weight_out, preferred_element_type=jnp.float32
        )

    grad_head_bf = (
        token_sums(head_term, local_rows).astype(jnp.bfloat16).reshape(local_rows, head_count, HD)
    )
    scores = attention_scores()
    probs = jnp.exp(scores - log_total)
    probs_bf = probs.astype(jnp.bfloat16)
    grad_probs = jnp.einsum(
        "thd,sd->hts", grad_head_bf, values_bf, preferred_element_type=jnp.float32
    )
    grad_values = jnp.einsum(
        "hts,thd->sd", probs_bf, grad_head_bf, preferred_element_type=jnp.float32
    )
    row_inner = jnp.sum(probs * grad_probs, axis=-1, keepdims=True)
    grad_scores = (probs * (grad_probs - row_inner)).astype(jnp.bfloat16)
    grad_query = (
        jnp.einsum("hts,sd->thd", grad_scores, keys_bf, preferred_element_type=jnp.float32)
        * query_scale
    )
    grad_keys = jnp.einsum("hts,thd->sd", grad_scores, query_bf, preferred_element_type=jnp.float32)
    unused_query, pull_query = jax.vjp(
        lambda rows_in, scales_in: head_norm(rows_in, scales_in, cos_local, sin_local),
        query_pre,
        gain_query,
    )
    grad_query_pre, grad_gain_query = pull_query(grad_query)
    grad_keys, grad_values, grad_gain_query = lax.psum(
        (grad_keys, grad_values, grad_gain_query), ("row", "col")
    )
    unused_key, pull_key = jax.vjp(
        lambda rows_in, scales_in: head_norm(rows_in, scales_in, cos_table, sin_table),
        key_pre,
        gain_key,
    )
    grad_key_pre, grad_gain_key = pull_key(grad_keys)
    grad_key_bf = lax.dynamic_slice_in_dim(grad_key_pre, col_start, kv_width, 1).astype(
        jnp.bfloat16
    )
    grad_value_bf = lax.dynamic_slice_in_dim(grad_values, col_start, kv_width, 1).astype(
        jnp.bfloat16
    )
    grad_query_all = token_gather(
        grad_query_pre.astype(jnp.bfloat16).reshape(local_rows, head_count * HD)
    )
    grad_in_part = jnp.einsum(
        "te,de->td", grad_query_all, weight_query, preferred_element_type=jnp.float32
    )
    grad_in_part = grad_in_part + jnp.einsum(
        "tk,dk->td", grad_key_bf, weight_key, preferred_element_type=jnp.float32
    )
    grad_in_part = grad_in_part + jnp.einsum(
        "tk,dk->td", grad_value_bf, weight_value, preferred_element_type=jnp.float32
    )
    grad_weight_query = jnp.einsum(
        "td,te->de", normed_cols, grad_query_all, preferred_element_type=jnp.float32
    )
    grad_weight_key = jnp.einsum(
        "td,tk->dk", normed_cols, grad_key_bf, preferred_element_type=jnp.float32
    )
    grad_weight_value = jnp.einsum(
        "td,tk->dk", normed_cols, grad_value_bf, preferred_element_type=jnp.float32
    )
    grad_normed = column_sums(grad_in_part)
    grad_in_norm, grad_gain_input = wide_norm_back(inputs, gain_input, inverse_in, grad_normed)
    grad_tokens = grad_in_norm + grad_resid
    summed = lax.psum(
        (
            grad_weight_query,
            grad_weight_key,
            grad_weight_value,
            grad_weight_out,
            grad_stacked,
            grad_weight_down,
            grad_gain_input,
            grad_gain_attn,
            grad_gain_pre,
            grad_gain_post,
            grad_gain_query,
            grad_gain_key,
        ),
        "dp",
    )
    return (
        layer_out.astype(jnp.bfloat16),
        grad_tokens,
        summed[0],
        summed[1],
        summed[2],
        summed[3],
        summed[4][:, 0, :],
        summed[4][:, 1, :],
        summed[5],
        summed[6],
        summed[7],
        summed[8],
        summed[9],
        summed[10],
        summed[11],
    )


def solution(mesh):
    in_specs = (
        P("dp", ("row", "col")),
        P("dp", ("row", "col")),
        P("row", "col"),
        P("row", "col"),
        P("row", "col"),
        P("col", "row"),
        P("row", "col"),
        P("row", "col"),
        P("col", "row"),
        P(("row", "col")),
        P(("row", "col")),
        P(("row", "col")),
        P(("row", "col")),
        P(),
        P(),
        P("dp", None),
        P(),
    )
    out_specs = (
        P("dp", ("row", "col")),
        P("dp", ("row", "col")),
        P("row", "col"),
        P("row", "col"),
        P("row", "col"),
        P("col", "row"),
        P("row", "col"),
        P("row", "col"),
        P("col", "row"),
        P(("row", "col")),
        P(("row", "col")),
        P(("row", "col")),
        P(("row", "col")),
        P(),
        P(),
    )
    return jax.shard_map(body, mesh=mesh, in_specs=in_specs, out_specs=out_specs, check_vma=False)
```

profile of v0, /device:TPU:0, one launch (start us, length us, event | category | flops | bytes accessed | tf_op | source)
XLA Modules:
  0.0 2147.9 jit_solution(2866870271570644720)
XLA Ops:
  9.3 15.5 psum.175
  27.6 23.0 %all-gather.11.cloned.1.call-done = bf16[2048,288]{0,1:T(8,128)(2,1)} async-done(((bf16[2048,144]{0,1:T(8,128)(2,1)}), bf16[2048,288]{0,1:T(8,128)(2,1)}) %all-gather.11.cloned.1.call-update) | async-done | bytes 1179664 | tf_op jit(solution)/shard_map/all_gather | solution.py:81
  53.6 36.2 %all-reduce.13.cloned.1.call-done = f32[2048,128]{1,0:T(8,128)} async-done(((f32[2048,128]{1,0:T(8,128)}), f32[2048,128]{1,0:T(8,128)}) %all-reduce.13.cloned.1.call-update) | async-done | bytes 1048592 | tf_op jit(solution)/shard_map/psum | solution.py:155
  98.9 27.2 %all-reduce.18 = bf16[2048,128]{1,0:T(8,128)(2,1)} all-reduce(f32[2048,128]{1,0:T(8,128)} %fusion.103), channel_id=1, replica_groups=mesh['dp'=4,'row'=4,'col'=2] {'row'}, use_global_device_ids=true, to_apply=%region_2.3 | all-reduce | flops 262144 | bytes 1572864 | tf_op jit(solution)/shard_map/psum | solution.py:155
  136.0 36.0 %reduce-scatter.9.cloned.1.call-done = f32[512,512]{1,0:T(8,128)} async-done(((f32[2048,512]{1,0:T(8,128)}), f32[512,512]{1,0:T(8,128)}) %reduce-scatter.9.cloned.1.call-update) | async-done | bytes 1048592 | tf_op jit(solution)/shard_map/reduce_scatter | solution.py:97
  202.6 22.7 %all-gather.17.cloned.1.call-done = bf16[2048,512]{0,1:T(8,128)(2,1)} async-done(((bf16[512,512]{0,1:T(8,128)(2,1)}), bf16[2048,512]{0,1:T(8,128)(2,1)}) %all-gather.17.cloned.1.call-update) | async-done | bytes 2097168 | tf_op jit(solution)/shard_map/all_gather | solution.py:106
  229.7 34.2 %reduce-scatter.11.cloned.1.call-done = f32[2048,144]{0,1:T(8,128)} async-done(((f32[2048,288]{0,1:T(8,128)}), f32[2048,144]{0,1:T(8,128)}) %reduce-scatter.11.cloned.1.call-update) | async-done | bytes 1179664 | tf_op jit(solution)/shard_map/reduce_scatter | solution.py:85
  265.3 13.1 psum.178
  280.2 13.6 psum.179
  295.0 22.7 %all-gather.19.cloned.1.call-done = bf16[2048,288]{0,1:T(8,128)(2,1)} async-done(((bf16[2048,144]{0,1:T(8,128)(2,1)}), bf16[2048,288]{0,1:T(8,128)(2,1)}) %all-gather.19.cloned.1.call-update) | async-done | bytes 1179664 | tf_op jit(solution)/shard_map/all_gather | solution.py:81
  317.8 25.1 %fusion.26 = f32[2048,2,3456]{0,2,1:T(8,128)} fusion(bf16[288,1,3456]{2,0,1:T(8,128)(2,1)} %bitcast.147, bf16[288,1,3456]{2,0,1:T(8,128)(2,1)} %bitcast.149, bf16[2048,288]{0,1:T(8,128)(2,1)} %all-gather.19.cloned.1.call-done), kind=kOutput, calls=%fused_computation.45 | convolution fusion | flops 8161689600 | bytes 61784064 | tf_op jit(solution)/shard_map/td,dgf->tgf/dot_general | solution.py:188
  343.0 384.3 %reduce-scatter.13.cloned.1.call-done = f32[2048,2,864]{0,2,1:T(8,128)} async-done(((f32[2048,2,3456]{0,2,1:T(8,128)}), f32[2048,2,864]{0,2,1:T(8,128)}) %reduce-scatter.13.cloned.1.call-update) | async-done | bytes 14155792 | tf_op jit(solution)/shard_map/reduce_scatter | solution.py:93
  734.8 91.2 %all-gather.21.cloned.1.call-done = bf16[2048,1,3456]{0,2,1:T(8,128)(2,1)} async-done(((bf16[2048,1,864]{0,2,1:T(8,128)(2,1)}), bf16[2048,1,3456]{0,2,1:T(8,128)(2,1)}) %all-gather.21.cloned.1.call-update) | async-done | bytes 14155792 | tf_op jit(solution)/shard_map/all_gather | solution.py:89
  835.9 34.2 %reduce-scatter.15.cloned.1.call-done = f32[2048,144]{0,1:T(8,128)} async-done(((f32[2048,288]{0,1:T(8,128)}), f32[2048,144]{0,1:T(8,128)}) %reduce-scatter.15.cloned.1.call-update) | async-done | bytes 1179664 | tf_op jit(solution)/shard_map/reduce_scatter | solution.py:85
  871.5 13.1 psum.180
  886.5 13.6 psum.181
  903.2 22.9 %all-gather.23.cloned.1.call-done = bf16[2048,288]{0,1:T(8,128)(2,1)} async-done(((bf16[2048,144]{0,1:T(8,128)(2,1)}), bf16[2048,288]{0,1:T(8,128)(2,1)}) %all-gather.23.cloned.1.call-update) | async-done | bytes 1179664 | tf_op jit(solution)/shard_map/all_gather | solution.py:81
  926.1 14.0 convolution_bitcast_fusion
  940.5 200.8 %reduce-scatter.17.cloned.1.call-done = f32[2048,1,864]{0,2,1:T(8,128)} async-done(((f32[2048,1,3456]{0,2,1:T(8,128)}), f32[2048,1,864]{0,2,1:T(8,128)}) %reduce-scatter.17.cloned.1.call-update) | async-done | bytes 7077904 | tf_op jit(solution)/shard_map/reduce_scatter | solution.py:93
  1155.5 171.8 %all-gather.25.cloned.1.call-done = bf16[2048,2,3456]{0,2,1:T(8,128)(2,1)} async-done(((bf16[2048,2,864]{0,2,1:T(8,128)(2,1)}), bf16[2048,2,3456]{0,2,1:T(8,128)(2,1)}) %all-gather.25.cloned.1.call-update) | async-done | bytes 28311568 | tf_op jit(solution)/shard_map/all_gather | solution.py:89
  1327.3 15.2 convolution_bitcast_fusion.1
  1342.6 34.8 %reduce-scatter.19.cloned.1.call-done = f32[2048,144]{0,1:T(8,128)} async-done(((f32[2048,288]{0,1:T(8,128)}), f32[2048,144]{0,1:T(8,128)}) %reduce-scatter.19.cloned.1.call-update) | async-done | bytes 1179664 | tf_op jit(solution)/shard_map/reduce_scatter | solution.py:85
  1379.1 13.1 psum.182
  1395.2 13.5 psum.183
  1411.2 23.0 %all-gather.27.cloned.1.call-done = bf16[2048,288]{0,1:T(8,128)(2,1)} async-done(((bf16[2048,144]{0,1:T(8,128)(2,1)}), bf16[2048,288]{0,1:T(8,128)(2,1)}) %all-gather.27.cloned.1.call-update) | async-done | bytes 1179664 | tf_op jit(solution)/shard_map/all_gather | solution.py:81
  1439.1 44.4 %reduce-scatter.21.cloned.1.call-done = f32[512,512]{1,0:T(8,128)} async-done(((f32[2048,512]{1,0:T(8,128)}), f32[512,512]{1,0:T(8,128)}) %reduce-scatter.21.cloned.1.call-update) | async-done | bytes 1048592 | tf_op jit(solution)/shard_map/reduce_scatter | solution.py:97
  1512.3 101.8 %all-reduce.19 = bf16[2048,256]{1,0:T(8,128)(2,1)S(1)} all-reduce(f32[2048,256]{1,0:T(8,128)} %fusion.23), channel_id=1, replica_groups=mesh['dp'=4,'row'=4,'col'=2] {'row','col'}, use_global_device_ids=true, to_apply=%region_34.35 | all-reduce | flops 524288 | bytes 3145728 | tf_op jit(solution)/shard_map/psum | solution.py:258
  1632.2 11.8 fusion
  1644.0 16.4 fusion.56
  1668.8 13.9 all-reduce.4
  1682.7 13.4 all-reduce.5
  1698.8 429.9 %all-reduce.17.cloned.1.call-done = (f32[288,512]{1,0:T(8,128)}, f32[288,128]{1,0:T(8,128)}, f32[288,128]{1,0:T(8,128)}, f32[512,288]{0,1:T(8,128)}, f32[288,2,3456]{2,0,1:T(8,128)}, /*index=5*/f32[3456,288]{0,1:T(8,128)}) async-done(((f32[288,512]{1,0:T(8,128)}, f32[288,128]{1,0:T(8,128)}, f32[288,128]{1,0:T(8,128)}, f32[512,288]{0,1:T(8,128)}, f32[288,2,3456]{2,0,1:T(8,128)}, ...) | async-done | bytes 13418512 | tf_op jit(solution)/shard_map/psum | solution.py:297
  (282 shorter events, 185.3 us)
Async XLA Ops:
  7.2 818.8 %copy-start = (bf16[3456,288]{0,1:T(8,128)(2,1)S(1)}, bf16[3456,288]{0,1:T(8,128)(2,1)}, u32[]{:S(2)}) copy-start(bf16[3456,288]{0,1:T(8,128)(2,1)} %param.25) | copy-start | bytes 5971972
  7.2 43.4 %copy-start.41 = (bf16[288,128]{1,0:T(8,128)(2,1)S(1)}, bf16[288,128]{1,0:T(8,128)(2,1)}, u32[]{:S(2)}) copy-start(bf16[288,128]{1,0:T(8,128)(2,1)} %param.20) | copy-start | bytes 221188
  7.2 43.3 %all-gather.11.cloned.1.call-start = ((), (), s32[]{:S(2)}) async-start(), calls=%async_computation.8 | async-start | bytes 1769472 | tf_op jit(solution)/shard_map/all_gather | solution.py:81
  27.5 62.4 %copy-start.22 = (bf16[288,512]{1,0:T(8,128)(2,1)S(1)}, bf16[288,512]{1,0:T(8,128)(2,1)}, u32[]{:S(2)}) copy-start(bf16[288,512]{1,0:T(8,128)(2,1)} %param.19) | copy-start | bytes 884740
  27.5 62.3 %all-reduce.13.cloned.1.call-start = ((), (), s32[]{:S(2)}) async-start(), calls=%async_computation.10 | async-start | bytes 2097152 | tf_op jit(solution)/shard_map/psum | solution.py:155
  53.6 72.9 %all-gather.15.cloned.1.call-start = ((), (), s32[]{:S(2)}) async-start(), calls=%async_computation.11 | async-start | bytes 3145728 | tf_op jit(solution)/shard_map/all_gather | solution.py:157
  89.9 82.2 %reduce-scatter.9.cloned.1.call-start = ((), (), s32[]{:S(2)}) async-start(), calls=%async_computation.12 | async-start | bytes 5242880 | tf_op jit(solution)/shard_map/reduce_scatter | solution.py:97
  93.2 102.1 %all-gather.13.cloned.1.call-start = ((), (), s32[]{:S(2)}) async-start(), calls=%async_computation.9 | async-start | bytes 1572864 | tf_op jit(solution)/shard_map/all_gather | solution.py:158
  94.8 82.1 %copy-start.57 = (f32[256]{0:T(256)}, f32[256]{0:T(256)S(1)}, u32[]{:S(2)}) copy-start(f32[256]{0:T(256)S(1)} %broadcast_add_fusion) | copy-start | bytes 3076
  126.2 99.1 %all-gather.17.cloned.1.call-start = ((), (), s32[]{:S(2)}) async-start(), calls=%async_computation.13 | async-start | bytes 2621440 | tf_op jit(solution)/shard_map/all_gather | solution.py:106
  136.0 42.5 %copy-start.18 = (f32[512,128]{1,0:T(8,128)}, f32[512,128]{1,0:T(8,128)S(1)}, u32[]{:S(2)}) copy-start(f32[512,128]{1,0:T(8,128)S(1)} %get-tuple-element.70) | copy-start | bytes 786436
  185.3 40.0 %copy-start.27 = (bf16[512,288]{0,1:T(8,128)(2,1)S(1)}, bf16[512,288]{0,1:T(8,128)(2,1)}, u32[]{:S(2)}) copy-start(bf16[512,288]{0,1:T(8,128)(2,1)} %param.22) | copy-start | bytes 884740
  202.5 61.4 %reduce-scatter.11.cloned.1.call-start = ((), (), s32[]{:S(2)}) async-start(), calls=%async_computation.14 | async-start | bytes 3538944 | tf_op jit(solution)/shard_map/reduce_scatter | solution.py:85
  229.1 88.7 %all-gather.19.cloned.1.call-start = ((), (), s32[]{:S(2)}) async-start(), calls=%async_computation.15 | async-start | bytes 1769472 | tf_op jit(solution)/shard_map/all_gather | solution.py:81
  294.8 432.4 %reduce-scatter.13.cloned.1.call-start = ((), (), s32[]{:S(2)}) async-start(), calls=%async_computation.16 | async-start | bytes 70778880 | tf_op jit(solution)/shard_map/reduce_scatter | solution.py:93
  342.9 483.1 %all-gather.21.cloned.1.call-start = ((), (), s32[]{:S(2)}) async-start(), calls=%async_computation.17 | async-start | bytes 17694720 | tf_op jit(solution)/shard_map/all_gather | solution.py:89
  734.8 135.3 %reduce-scatter.15.cloned.1.call-start = ((), (), s32[]{:S(2)}) async-start(), calls=%async_computation.18 | async-start | bytes 3538944 | tf_op jit(solution)/shard_map/reduce_scatter | solution.py:85
  835.2 90.9 %all-gather.23.cloned.1.call-start = ((), (), s32[]{:S(2)}) async-start(), calls=%async_computation.19 | async-start | bytes 1769472 | tf_op jit(solution)/shard_map/all_gather | solution.py:81
  903.1 238.2 %reduce-scatter.17.cloned.1.call-start = ((), (), s32[]{:S(2)}) async-start(), calls=%async_computation.20 | async-start | bytes 35389440 | tf_op jit(solution)/shard_map/reduce_scatter | solution.py:93
  940.1 387.2 %all-gather.25.cloned.1.call-start = ((), (), s32[]{:S(2)}) async-start(), calls=%async_computation.21 | async-start | bytes 35389440 | tf_op jit(solution)/shard_map/all_gather | solution.py:89
  1155.5 171.9 %copy-start.26 = (bf16[288,3456]{1,0:T(8,128)(2,1)S(1)}, bf16[288,3456]{1,0:T(8,128)(2,1)}, u32[]{:S(2)}) copy-start(bf16[288,3456]{1,0:T(8,128)(2,1)} %param.24) | copy-start | bytes 5971972
  1155.5 221.9 %reduce-scatter.19.cloned.1.call-start = ((), (), s32[]{:S(2)}) async-start(), calls=%async_computation.22 | async-start | bytes 3538944 | tf_op jit(solution)/shard_map/reduce_scatter | solution.py:85
  1342.5 49.7 %copy-start.9 = (f32[2048,144]{0,1:T(8,128)S(1)}, f32[2048,144]{0,1:T(8,128)}, u32[]{:S(2)}) copy-start(f32[2048,144]{0,1:T(8,128)} %reduce-scatter.11.cloned.1.call-done) | copy-start | bytes 3538948
  1342.5 49.7 %copy-start.14 = (bf16[2048,144]{0,1:T(8,128)(2,1)S(1)}, bf16[2048,144]{0,1:T(8,128)(2,1)}, u32[]{:S(2)}) copy-start(bf16[2048,144]{0,1:T(8,128)(2,1)} %param.18) | copy-start | bytes 1769476
  1342.5 91.7 %all-gather.27.cloned.1.call-start = ((), (), s32[]{:S(2)}) async-start(), calls=%async_computation.23 | async-start | bytes 1769472 | tf_op jit(solution)/shard_map/all_gather | solution.py:81
  1411.2 72.3 %reduce-scatter.21.cloned.1.call-start = ((), (), s32[]{:S(2)}) async-start(), calls=%async_computation.24 | async-start | bytes 5242880 | tf_op jit(solution)/shard_map/reduce_scatter | solution.py:97
  1438.8 46.0 %copy-start.6 = (pred[512,2048]{0,1:T(8,128)(4,1)S(1)}, pred[512,2048]{0,1:T(8,128)(4,1)}, u32[]{:S(2)}) copy-start(pred[512,2048]{0,1:T(8,128)(4,1)} %compare_and_fusion) | copy-start | bytes 3145732
  1438.8 177.2 %all-reduce.15.cloned.1.call-start = ((), (), s32[]{:S(2)}) async-start(), calls=%async_computation.26 | async-start | bytes 4194304 | tf_op jit(solution)/shard_map/psum | solution.py:258
  1504.0 122.7 %all-gather.29.cloned.1.call-start = ((), (), s32[]{:S(2)}) async-start(), calls=%async_computation.25 | async-start | bytes 2621440 | tf_op jit(solution)/shard_map/all_gather | solution.py:106
  1512.2 101.8 %copy-start.40 = (bf16[288,128]{1,0:T(8,128)(2,1)S(1)}, bf16[288,128]{1,0:T(8,128)(2,1)}, u32[]{:S(2)}) copy-start(bf16[288,128]{1,0:T(8,128)(2,1)} %param.21) | copy-start | bytes 221188
  1512.3 154.5 %reduce-scatter.23.cloned.1.call-start = ((), (), s32[]{:S(2)}) async-start(), calls=%async_computation.27 | async-start | bytes 3538944 | tf_op jit(solution)/shard_map/reduce_scatter | solution.py:85
  1632.0 496.7 %all-reduce.17.cloned.1.call-start = ((), (), s32[]{:S(2)}) async-start(), calls=%async_computation.28 | async-start | bytes 26836992 | tf_op jit(solution)/shard_map/psum | solution.py:297
  (62 other events, 398.0 us)
Sparse Core Ops, SparseCore 0:
  27.6 22.8 all-gather.10
  53.7 36.1 all-reduce.12
  91.4 33.4 all-gather.14
  127.5 44.5 reduce-scatter.8
  174.0 21.2 all-gather.12
  202.6 22.5 all-gather.16
  229.2 34.7 reduce-scatter.10
  294.9 22.8 all-gather.18
  343.0 384.1 reduce-scatter.12
  734.9 91.0 all-gather.20
  835.4 34.7 reduce-scatter.14
  903.2 22.8 all-gather.22
  940.2 201.0 reduce-scatter.16
  1155.6 171.6 all-gather.24
  1342.6 34.6 reduce-scatter.18
  1411.3 22.8 all-gather.26
  1438.9 44.5 reduce-scatter.20
  1504.1 74.0 all-reduce.14
  1580.3 27.7 all-gather.28
  1632.1 34.5 reduce-scatter.22
  1671.5 457.0 all-reduce.16
where the time goes:
time: 2150 us
  waiting for transfers between devices  1620 us (75%)
  blocking collectives  252 us (12%)
  matrix products  149 us (7%)
  other arithmetic  76.9 us (4%)
  local copies, waits for them, and re-layouts  28.3 us (1%)
    reduce_scatter x2, waiting for transfers between devices, row_sums(): return lax.psum_scatter(values, 'row', scatter_dimension=2, tiled=True)  585 us
    psum x1, waiting for transfers between devices, body(): lax.psum((grad_weight_query, grad_weight_key, grad_weight_value, grad_wei...  430 us
    all_gather x2, waiting for transfers between devices, row_gather(): return lax.all_gather(values, 'row', axis=2, tiled=True)  263 us
    psum x8, blocking collectives, feature_sum(): return lax.psum(jnp.sum(values, axis=1), ('row', 'col'))  109 us
    reduce_scatter x4, waiting for transfers between devices, column_sums(): return lax.psum_scatter(values, 'col', scatter_dimension=1, tiled=True)  104 us
    psum x1, blocking collectives, body(): lax.psum((grad_keys, grad_values, grad_gain_query), ('row', 'col'))  102 us
    all_gather x4, waiting for transfers between devices, column_gather(): return lax.all_gather(values, 'col', axis=1, tiled=True)  91.7 us
    reduce_scatter x2, waiting for transfers between devices, token_sums(): lax.psum_scatter(term_fn(jnp.int32(0), tok_count * lax.axis_size('row')),...  80.5 us
  transfers between devices with their start and end apart: 21, of which 18 were waited for; matrix products, arithmetic and copies ran while one was open for 4% of the time, Pallas kernels for 0%

commit v1 on v0

v1 whole, which is shorter than its diff:
```python
import math

import jax
import jax.numpy as jnp
from jax import lax
from jax.experimental import pallas as pl
from jax.experimental.pallas import tpu as pltpu
from jax.sharding import PartitionSpec as P

HD = 256
EPS = 1e-06
ROPE_BASE = 1000000.0
GELU_C = 0.7978845608028654
BF = jnp.bfloat16
F32 = jnp.float32
PLANE = ("row", "col")


def dot(left, right, dims):
    return lax.dot_general(left, right, (dims, ((), ())), preferred_element_type=F32)


def nn(left, right):
    return dot(left, right, ((1,), (0,)))


def nt(left, right):
    return dot(left, right, ((1,), (1,)))


def tn(left, right):
    return dot(left, right, ((0,), (0,)))


def gelu_tanh(values):
    return 0.5 * values * (1.0 + jnp.tanh(GELU_C * (values + 0.044715 * values * values * values)))


def rotate(values, cos_table, sin_table):
    half_width = values.shape[-1] // 2
    first_half = values[..., :half_width]
    second_half = values[..., half_width:]
    return jnp.concatenate(
        [
            first_half * cos_table - second_half * sin_table,
            second_half * cos_table + first_half * sin_table,
        ],
        axis=-1,
    )


def head_norm(values, scales, cos_table, sin_table):
    mean_square = jnp.mean(values * values, axis=-1, keepdims=True)
    return rotate(values * lax.rsqrt(mean_square + EPS) * (1.0 + scales), cos_table, sin_table)


def positions(lengths, token_ids):
    doc_ends = jnp.cumsum(lengths, dtype=jnp.int32)
    doc_starts = doc_ends - lengths
    document = jnp.sum(
        (token_ids[:, None] >= doc_ends[None, :]).astype(jnp.int32), axis=1, dtype=jnp.int32
    )
    doc_ids = jnp.arange(lengths.shape[0], dtype=jnp.int32)
    doc_first = jnp.sum(
        jnp.where(doc_ids[None, :] == document[:, None], doc_starts[None, :], 0),
        axis=1,
        dtype=jnp.int32,
    )
    return (document, token_ids - doc_first)


def angles(places):
    half_width = HD // 2
    frequency = jnp.exp(
        jnp.arange(half_width, dtype=jnp.float32) * (-2.0 * math.log(ROPE_BASE) / HD)
    )
    phases = places.astype(jnp.float32)[:, None] * frequency[None, :]
    return (jnp.cos(phases), jnp.sin(phases))


def norm(values, scales):
    inverse = lax.rsqrt(jnp.mean(values * values, axis=1, keepdims=True) + EPS)
    return (values * inverse * (1.0 + scales), inverse)


def norm_back(values, scales, inverse, upstream):
    scaled = upstream * (1.0 + scales)
    inner = jnp.mean(scaled * values, axis=1, keepdims=True)
    grad_values = scaled * inverse - values * inverse * inverse * inverse * inner
    return (grad_values, jnp.sum(upstream * values * inverse, axis=0))


MESH = pl.DeviceIdType.MESH
TILE = 256
VMEM_LIMIT = 64 * 1024 * 1024 - 512 * 1024


def whereabouts():
    place, row, col = lax.axis_index("dp"), lax.axis_index("row"), lax.axis_index("col")
    return place, row, col, row // 2, row % 2


def peers():
    place, row, col, high, core = whereabouts()
    far = row + 2 - 4 * high
    return (
        (place, row, 1 - col),
        (place, far, col),
        (place, far, 1 - col),
        (place, row + 1 - 2 * core, col),
    )


def remote(src, dst, send, recv, device):
    return pltpu.make_async_remote_copy(
        src_ref=src, dst_ref=dst, send_sem=send, recv_sem=recv, device_id=device, device_id_type=MESH
    )


def greet(devices):
    barrier = pltpu.get_barrier_semaphore()
    for device in devices:
        pl.semaphore_signal(barrier, inc=1, device_id=device, device_id_type=MESH)
    pl.semaphore_wait(barrier, len(devices))


def any_spec():
    return pl.BlockSpec(memory_space=pl.ANY)


def vmem_spec():
    return pl.BlockSpec(memory_space=pltpu.VMEM)


def params(number):
    return pltpu.CompilerParams(
        collective_id=number, has_side_effects=True, vmem_limit_bytes=VMEM_LIMIT
    )


def entry_kernel(tk, ct, wa, wm, tk_out, ct_out, wa_out, wm_out, tk_s, tk_r, ct_s, ct_r, wa_s, wa_r, wm_s, wm_r, loc):
    place, row, col, high, core = whereabouts()
    depth = wa.shape[0]
    slab = wm_out.shape[2]
    me = 2 * row + col
    px, py, pd, pc = peers()
    others = []
    for step in range(1, 8):
        r2, c2 = (row + step // 2) % 4, (col + step) % 2
        others.append((2 * r2 + c2, (place, r2, c2)))
    greet([device for _, device in others])
    copies = []

    def start(copy):
        copy.start()
        copies.append(copy)
        return copy

    for i, (index, device) in enumerate(others):
        start(remote(tk.at[index], tk_out.at[me], tk_s.at[i], tk_r.at[i], device))
    local = [
        pltpu.make_async_copy(tk.at[me], tk_out.at[me], loc.at[0]),
        pltpu.make_async_copy(ct.at[me], ct_out.at[me], loc.at[1]),
        pltpu.make_async_copy(wa, wa_out.at[col, pl.ds(row * depth, depth)], loc.at[2]),
        pltpu.make_async_copy(
            wm.at[:, :, pl.ds(high * slab, slab)], wm_out.at[:, pl.ds(row * depth, depth)], loc.at[3]
        ),
    ]
    for copy in local:
        copy.start()
    slot = wa_out.at[col, pl.ds(row * depth, depth)]
    first = [start(remote(wa, slot, wa_s.at[i], wa_r.at[i], p)) for i, p in enumerate((px, py, pd, pc))]
    mine = pl.ds(high * slab, slab)
    away = pl.ds((1 - high) * slab, slab)
    rows = pl.ds(row * depth, depth)
    far_row = row + 2 - 4 * high
    far_rows = pl.ds(far_row * depth, depth)
    over = []
    for m in range(3):
        over.append(start(remote(wm.at[m, :, away], wm_out.at[m, rows], wm_s.at[m, 0], wm_r.at[m, 0], py)))
        start(remote(wm.at[m, :, mine], wm_out.at[m, rows], wm_s.at[m, 1], wm_r.at[m, 1], pc))
    for i, (index, device) in enumerate(others):
        start(remote(ct.at[index], ct_out.at[me], ct_s.at[i], ct_r.at[i], device))
    relay = []
    for i, (r2, c2) in enumerate(((row, 1 - col), (far_row, col), (far_row, 1 - col))):
        first[i].wait_recv()
        part = wa_out.at[c2, pl.ds(r2 * depth, depth)]
        relay.append(remote(part, part, wa_s.at[4 + i], wa_r.at[4 + i], pc))
        relay[-1].start()
    for m in range(3):
        over[m].wait_recv()
        part = wm_out.at[m, far_rows]
        relay.append(remote(part, part, wm_s.at[m, 2], wm_r.at[m, 2], pc))
        relay[-1].start()
    waited = first[:3] + over
    for copy in copies:
        copy.wait_send()
        if not any(copy is other for other in waited):
            copy.wait_recv()
    for copy in relay:
        copy.wait()
    for copy in local:
        copy.wait()


def entry(tk, ct, wa, wm):
    depth, feats = wa.shape
    slab = wm.shape[2] // 2
    dma = pltpu.SemaphoreType.DMA
    return pl.pallas_call(
        entry_kernel,
        out_shape=(
            jax.ShapeDtypeStruct(tk.shape, BF),
            jax.ShapeDtypeStruct(ct.shape, BF),
            jax.ShapeDtypeStruct((2, 4 * depth, feats), BF),
            jax.ShapeDtypeStruct((3, 4 * depth, slab), BF),
        ),
        in_specs=[any_spec()] * 4,
        out_specs=[any_spec()] * 4,
        scratch_shapes=[
            dma((7,)), dma((7,)), dma((7,)), dma((7,)), dma((7,)), dma((7,)),
            dma((3, 3)), dma((3, 3)), dma((4,)),
        ],
        compiler_params=params(1),
        name="entry",
    )(tk, ct, wa, wm)


KV_SLOTS = (0, 1, 4, 5)


def kv_kernel(kv, out, send, recv, loc):
    px, py, pd, pc = peers()
    greet((px, py, pd, pc))
    own = pltpu.make_async_copy(kv, out.at[0], loc)
    own.start()
    first = [
        remote(kv, out.at[slot], send.at[i], recv.at[i], device)
        for i, (slot, device) in enumerate(((1, px), (4, py), (5, pd), (2, pc)))
    ]
    for copy in first:
        copy.start()
    relay = []
    for i, slot in enumerate((1, 4, 5)):
        first[i].wait_recv()
        copy = remote(out.at[slot], out.at[slot + 2], send.at[4 + i], recv.at[4 + i], pc)
        copy.start()
        relay.append(copy)
    for copy in first:
        copy.wait_send()
    first[3].wait_recv()
    for copy in relay:
        copy.wait()
    own.wait()


def kv_gather(kv):
    dma = pltpu.SemaphoreType.DMA
    return pl.pallas_call(
        kv_kernel,
        out_shape=jax.ShapeDtypeStruct((8,) + kv.shape, BF),
        in_specs=[any_spec()],
        out_specs=any_spec(),
        scratch_shapes=[dma((7,)), dma((7,)), dma(())],
        compiler_params=params(2),
        name="kv_gather",
    )(kv)


def mlp_kernel(
    pre, res, ct, gpost, wg_h, wu_h, wd_h,
    lo, dgpost, dpre, grads,
    wg, wu, wd, pre_all, pre_t, gm_all, gm_t, aa, bb, hh, acc, own, parts, prc, prc2, dwb, crecv,
    w_sem, ag_s, ag_r, rs_s, rs_r, gs_s, gs_r, bs_s, bs_r, c_s, c_r, y_s, y_r, l_s,
):
    place, row, col, high, core = whereabouts()
    px, py, pd, pc = peers()
    quad = (px, py, pd)
    loc, width = pre.shape
    slab = wg.shape[1]
    tiles = slab // TILE
    depth = crecv.shape[3]
    loads = [
        pltpu.make_async_copy(src, dst, w_sem.at[i])
        for i, (src, dst) in enumerate(((wg_h, wg), (wu_h, wu), (wd_h, wd)))
    ]
    for copy in loads:
        copy.start()
    greet((px, py, pd, pc))

    def spread(src, buffer, send, recv):
        copies = [remote(src, buffer.at[i + 1], send.at[i], recv.at[i], p) for i, p in enumerate(quad)]
        for copy in copies:
            copy.start()
        return copies

    def lanes(n):
        return pl.ds(pl.multiple_of(n * TILE, TILE), TILE)

    gathers = spread(pre, pre_all, ag_s, ag_r)
    pre_all[0] = pre[...]
    for copy in loads:
        copy.wait()

    scatters = []
    for j in range(4):
        if j:
            gathers[j - 1].wait_recv()
        acc[...] = jnp.zeros_like(acc)
        rows = pl.ds(j * loc, loc)

        def forward(n, carry, j=j, rows=rows):
            x = pre_all[j]
            gate = nn(x, wg[:, lanes(n)])
            up = nn(x, wu[:, lanes(n)])
            square = gate * gate
            bend = jnp.tanh(GELU_C * gate * (1.0 + 0.044715 * square))
            half = 0.5 * (1.0 + bend)
            gelu = gate * half
            slope = half + 0.5 * gate * (1.0 - bend * bend) * (GELU_C * (1.0 + 0.134145 * square))
            hidden = (gelu * up).astype(BF)
            aa[rows, lanes(n)] = gelu.astype(BF)
            bb[rows, lanes(n)] = (up * slope).astype(BF)
            hh[rows, lanes(n)] = hidden
            acc[...] += nt(hidden, wd[:, lanes(n)])
            return carry

        lax.fori_loop(0, tiles, forward, 0)
        if j:
            parts[j - 1] = acc[...].astype(BF)
            copy = remote(parts.at[j - 1], prc.at[j - 1], rs_s.at[j - 1], rs_r.at[j - 1], quad[j - 1])
            copy.start()
            scatters.append(copy)
        else:
            own[...] = acc[...]
    for j in range(4):
        pre_t[:, j * loc : (j + 1) * loc] = pre_all[j].T
    for copy in scatters:
        copy.wait()
    out = own[...] + prc[0].astype(F32) + prc[1].astype(F32) + prc[2].astype(F32)
    scale = 1.0 + gpost[...]
    inverse = lax.rsqrt(jnp.mean(out * out, axis=1, keepdims=True) + EPS)
    lo[...] = (res[...] + out * inverse * scale).astype(BF)
    upstream = ct[...].astype(F32)
    scaled = upstream * scale
    inner = jnp.mean(scaled * out, axis=1, keepdims=True)
    gm_all[0] = (scaled * inverse - out * (inverse * inverse * inverse * inner)).astype(BF)
    dgpost[...] = jnp.sum(upstream * out * inverse, axis=0, keepdims=True)

    gathers2 = spread(gm_all.at[0], gm_all, gs_s, gs_r)
    scatters2 = []
    for j in range(4):
        if j:
            gathers2[j - 1].wait_recv()
        acc[...] = jnp.zeros_like(acc)
        rows = pl.ds(j * loc, loc)

        def backward(n, carry, j=j, rows=rows):
            grad_hidden = nn(gm_all[j], wd[:, lanes(n)])
            grad_gate = (grad_hidden * bb[rows, lanes(n)].astype(F32)).astype(BF)
            grad_up = (grad_hidden * aa[rows, lanes(n)].astype(F32)).astype(BF)
            bb[rows, lanes(n)] = grad_gate
            aa[rows, lanes(n)] = grad_up
            acc[...] += nt(grad_gate, wg[:, lanes(n)]) + nt(grad_up, wu[:, lanes(n)])
            return carry

        lax.fori_loop(0, tiles, backward, 0)
        gm_t[:, j * loc : (j + 1) * loc] = gm_all[j].T
        if j:
            parts[j - 1] = acc[...].astype(BF)
            copy = remote(parts.at[j - 1], prc2.at[j - 1], bs_s.at[j - 1], bs_r.at[j - 1], quad[j - 1])
            copy.start()
            scatters2.append(copy)
        else:
            own[...] = acc[...]

    def to_core(n, m, y2):
        return remote(
            dwb.at[n % 2, m, 2 * y2 + 1 - core], crecv.at[m, n, y2], c_s.at[n % 2, m, y2], c_r.at[m, n, y2], pc
        )

    def to_far(n, m):
        return remote(crecv.at[m, n, 1 - high], grads.at[m, n, 1], y_s.at[m, n], y_r.at[m, n], py)

    def to_out(n, m):
        return pltpu.make_async_copy(crecv.at[m, n, high], grads.at[m, n, 0], l_s.at[m, n])

    def produce(n):
        for m, (left, right) in enumerate(((pre_t, bb), (pre_t, aa), (gm_t, hh))):
            product = nn(left[...], right[:, lanes(n)]).astype(BF)
            dwb[n % 2, m] = product.reshape(4, depth, TILE)
            for y2 in range(2):
                to_core(n, m, y2).start()

    def settle(n):
        for m in range(3):
            for y2 in range(2):
                to_core(n, m, y2).wait()
                crecv[m, n, y2] = (
                    crecv[m, n, y2].astype(F32) + dwb[n % 2, m, 2 * y2 + core].astype(F32)
                ).astype(BF)
            to_far(n, m).start()
            to_out(n, m).start()

    produce(0)

    def step(n, carry):
        produce(n)
        settle(n - 1)
        return carry

    lax.fori_loop(1, tiles, step, 0)
    settle(tiles - 1)
    for copy in scatters2:
        copy.wait()
    dpre[...] = own[...] + prc2[0].astype(F32) + prc2[1].astype(F32) + prc2[2].astype(F32)

    def finish(n, carry):
        for m in range(3):
            to_far(n, m).wait()
            to_out(n, m).wait()
        return carry

    lax.fori_loop(0, tiles, finish, 0)
    for copy in gathers + gathers2:
        copy.wait_send()


def mlp(pre, res, ct, gpost, w_gate, w_up, w_down):
    loc, width = pre.shape
    slab = w_gate.shape[1]
    tiles = slab // TILE
    depth = width // 4
    dma = pltpu.SemaphoreType.DMA
    return pl.pallas_call(
        mlp_kernel,
        out_shape=(
            jax.ShapeDtypeStruct((loc, width), BF),
            jax.ShapeDtypeStruct((1, width), F32),
            jax.ShapeDtypeStruct((loc, width), F32),
            jax.ShapeDtypeStruct((3, tiles, 2, depth, TILE), BF),
        ),
        in_specs=[vmem_spec()] * 4 + [any_spec()] * 3,
        out_specs=[vmem_spec()] * 3 + [any_spec()],
        scratch_shapes=[
            pltpu.VMEM((width, slab), BF),
            pltpu.VMEM((width, slab), BF),
            pltpu.VMEM((width, slab), BF),
            pltpu.VMEM((4, loc, width), BF),
            pltpu.VMEM((width, 4 * loc), BF),
            pltpu.VMEM((4, loc, width), BF),
            pltpu.VMEM((width, 4 * loc), BF),
            pltpu.VMEM((4 * loc, slab), BF),
            pltpu.VMEM((4 * loc, slab), BF),
            pltpu.VMEM((4 * loc, slab), BF),
            pltpu.VMEM((loc, width), F32),
            pltpu.VMEM((loc, width), F32),
            pltpu.VMEM((3, loc, width), BF),
            pltpu.VMEM((3, loc, width), BF),
            pltpu.VMEM((3, loc, width), BF),
            pltpu.VMEM((2, 3, 4, depth, TILE), BF),
            pltpu.VMEM((3, tiles, 2, depth, TILE), BF),
            dma((3,)),
            dma((3,)), dma((3,)), dma((3,)), dma((3,)), dma((3,)), dma((3,)), dma((3,)), dma((3,)),
            dma((2, 3, 2)), dma((3, tiles, 2)), dma((3, tiles)), dma((3, tiles)), dma((3, tiles)),
        ],
        compiler_params=params(3),
        name="feed_forward",
    )(pre, res, ct, gpost, w_gate, w_up, w_down)


def kv_sum_kernel(parts, out, cr, summed, qr, c_s, c_r, q_s, q_r):
    px, py, pd, pc = peers()
    greet((px, py, pd, pc))
    core = [
        remote(parts.at[slot + 2], cr.at[i], c_s.at[i], c_r.at[i], pc) for i, slot in enumerate(KV_SLOTS)
    ]
    for copy in core:
        copy.start()
    sends = []
    for i, device in ((3, pd), (1, px), (2, py), (0, None)):
        core[i].wait_recv()
        total = parts[KV_SLOTS[i]].astype(F32) + cr[i].astype(F32)
        if device is None:
            out[...] = total
        else:
            summed[i - 1] = total.astype(BF)
            copy = remote(summed.at[i - 1], qr.at[i - 1], q_s.at[i - 1], q_r.at[i - 1], device)
            copy.start()
            sends.append(copy)
    for copy in sends:
        copy.wait()
    out[...] += qr[0].astype(F32) + qr[1].astype(F32) + qr[2].astype(F32)
    for copy in core:
        copy.wait_send()


def kv_sum(parts):
    shape = parts.shape[1:]
    dma = pltpu.SemaphoreType.DMA
    return pl.pallas_call(
        kv_sum_kernel,
        out_shape=jax.ShapeDtypeStruct(shape, F32),
        in_specs=[vmem_spec()],
        out_specs=vmem_spec(),
        scratch_shapes=[
            pltpu.VMEM((4,) + shape, BF),
            pltpu.VMEM((3,) + shape, BF),
            pltpu.VMEM((3,) + shape, BF),
            dma((4,)), dma((4,)), dma((3,)), dma((3,)),
        ],
        compiler_params=params(4),
        name="kv_sum",
    )(parts)


def attn_sum_kernel(parts, out, cr, summed, qr, c_s, c_r, q_s, q_r):
    place, row, col, high, core = whereabouts()
    px, py, pd, pc = peers()
    greet((px, py, pd, pc))
    wanted = ((1 - col, 1 - high, pd), (1 - col, high, px), (col, 1 - high, py), (col, high, None))
    copies = [
        remote(parts.at[c2, 2 * y2 + 1 - core], cr.at[c2, y2], c_s.at[i], c_r.at[c2, y2], pc)
        for i, (c2, y2, _) in enumerate(wanted)
    ]
    for copy in copies:
        copy.start()
    sends = []
    for i, (c2, y2, device) in enumerate(wanted):
        copies[i].wait_recv()
        total = parts[c2, 2 * y2 + core].astype(F32) + cr[c2, y2].astype(F32)
        if device is None:
            own = total
        else:
            summed[i] = total.astype(BF)
            copy = remote(summed.at[i], qr.at[i], q_s.at[i], q_r.at[i], device)
            copy.start()
            sends.append(copy)
    for copy in sends:
        copy.wait()
    out[...] = (own + qr[0].astype(F32) + qr[1].astype(F32) + qr[2].astype(F32)).astype(BF)
    for copy in copies:
        copy.wait_send()


def attn_sum(parts):
    shape = parts.shape[2:]
    dma = pltpu.SemaphoreType.DMA
    return pl.pallas_call(
        attn_sum_kernel,
        out_shape=jax.ShapeDtypeStruct(shape, BF),
        in_specs=[vmem_spec()],
        out_specs=vmem_spec(),
        scratch_shapes=[
            pltpu.VMEM((2, 2) + shape, BF),
            pltpu.VMEM((3,) + shape, BF),
            pltpu.VMEM((3,) + shape, BF),
            dma((4,)), dma((2, 2)), dma((3,)), dma((3,)),
        ],
        compiler_params=params(5),
        name="attn_sum",
    )(parts)


class Line:
    def __init__(self, mine, inbox, middle, out, sems):
        self.mine, self.inbox, self.middle, self.out = mine, inbox, middle, out
        self.in_s, self.in_r, self.mid_s, self.mid_r, self.x_s, self.x_r, self.o_s, self.o_r, self.l_s = sems
        place, row, col = lax.axis_index("dp"), lax.axis_index("row"), lax.axis_index("col")
        self.end = (place % 3) == 0
        inner = jnp.where(place == 0, 1, 2)
        self.inner = (inner, row, col)
        self.outer = ((place - 1) * 3 % 6, row, col)
        self.across = (3 - place, row, col)
        self.root = jnp.where(place == 1, 0, 1)
        self.place = place

    def inward(self, k, h):
        return remote(self.mine.at[k, h], self.inbox.at[k, h], self.in_s.at[k, h], self.in_r.at[k, h], self.inner)

    def partial(self, k):
        return remote(
            self.mine.at[k, 1 - self.root], self.middle.at[k], self.mid_s.at[k], self.mid_r.at[k], self.across
        )

    def exchange(self, k):
        return remote(
            self.mine.at[k, self.root], self.out.at[k, self.root], self.x_s.at[k], self.x_r.at[k], self.across
        )

    def exchanged(self, k):
        return remote(
            self.mine.at[k, 1 - self.root], self.out.at[k, 1 - self.root], self.x_s.at[k], self.x_r.at[k], self.across
        )

    def outward(self, k, h, source):
        return remote(source.at[k, h], self.out.at[k, h], self.o_s.at[k, h], self.o_r.at[k, h], self.outer)

    def keep(self, k):
        return pltpu.make_async_copy(self.mine.at[k, self.root], self.out.at[k, self.root], self.l_s.at[k])

    def send(self, k):
        @pl.when(self.end)
        def _():
            for h in range(2):
                self.inward(k, h).start()

    def add(self, k):
        @pl.when(jnp.logical_not(self.end))
        def _():
            other = 1 - self.root
            self.inward(k, other).wait_recv()
            self.mine[k, other] = (
                self.mine[k, other].astype(F32) + self.inbox[k, other].astype(F32)
            ).astype(BF)
            self.partial(k).start()

    def total(self, k):
        @pl.when(jnp.logical_not(self.end))
        def _():
            root = self.root
            self.inward(k, root).wait_recv()
            self.partial(k).wait_recv()
            self.mine[k, root] = (
                self.mine[k, root].astype(F32) + self.inbox[k, root].astype(F32) + self.middle[k].astype(F32)
            ).astype(BF)
            self.outward(k, root, self.mine).start()
            self.exchange(k).start()
            self.keep(k).start()

    def forward(self, k):
        @pl.when(jnp.logical_not(self.end))
        def _():
            other = 1 - self.root
            self.exchanged(k).wait_recv()
            self.outward(k, other, self.out).start()

    def drain(self, k):
        @pl.when(self.end)
        def _():
            for h in range(2):
                self.inward(k, h).wait_send()
                self.outward(k, h, self.out).wait_recv()

        @pl.when(jnp.logical_not(self.end))
        def _():
            self.partial(k).wait_send()
            self.exchange(k).wait_send()
            self.keep(k).wait()
            for h in range(2):
                self.outward(k, h, self.out).wait_send()

    def greet(self):
        barrier = pltpu.get_barrier_semaphore()

        @pl.when(self.end)
        def _():
            pl.semaphore_signal(barrier, inc=1, device_id=self.inner, device_id_type=MESH)
            pl.semaphore_wait(barrier, 1)

        @pl.when(jnp.logical_not(self.end))
        def _():
            pl.semaphore_signal(barrier, inc=1, device_id=self.outer, device_id_type=MESH)
            pl.semaphore_signal(barrier, inc=1, device_id=self.across, device_id_type=MESH)
            pl.semaphore_wait(barrier, 2)


def line_sems(count):
    dma = pltpu.SemaphoreType.DMA
    return [
        dma((count, 2)), dma((count, 2)), dma((count,)), dma((count,)), dma((count,)), dma((count,)),
        dma((count, 2)), dma((count, 2)), dma((count,)),
    ]


def line_kernel(g, a, g_out, a_out, g_mine, g_in, g_mid, a_mine, a_in, a_mid, load, *sems):
    big = Line(g_mine, g_in, g_mid, g_out, sems[:9])
    small = Line(a_mine, a_in, a_mid, a_out, sems[9:])
    count = g_mine.shape[0]
    fetch = [pltpu.make_async_copy(g, g_mine, load.at[0]), pltpu.make_async_copy(a, a_mine, load.at[1])]
    for copy in fetch:
        copy.start()
    big.greet()
    for copy in fetch:
        copy.wait()

    def send(k, carry):
        big.send(k)
        return carry

    lax.fori_loop(0, count, send, 0)
    small.send(0)
    big.add(0)
    big.add(1)
    big.total(0)

    def step(k, carry):
        big.add(k)
        big.total(k - 1)
        big.forward(k - 2)
        return carry

    lax.fori_loop(2, count, step, 0)
    small.add(0)
    big.total(count - 1)
    big.forward(count - 2)
    small.total(0)
    big.forward(count - 1)
    small.forward(0)

    def drain(k, carry):
        big.drain(k)
        return carry

    lax.fori_loop(0, count, drain, 0)
    small.drain(0)


def line_sum(g, a):
    count = g.shape[0]
    shape, small = g.shape[2:], a.shape[2:]
    dma = pltpu.SemaphoreType.DMA
    return pl.pallas_call(
        line_kernel,
        out_shape=(jax.ShapeDtypeStruct(g.shape, BF), jax.ShapeDtypeStruct(a.shape, BF)),
        in_specs=[any_spec()] * 2,
        out_specs=[any_spec()] * 2,
        scratch_shapes=[
            pltpu.VMEM(g.shape, BF), pltpu.VMEM(g.shape, BF), pltpu.VMEM((count,) + shape, BF),
            pltpu.VMEM(a.shape, BF), pltpu.VMEM(a.shape, BF), pltpu.VMEM((1,) + small, BF),
            dma((2,)),
        ] + line_sems(count) + line_sems(1),
        compiler_params=params(6),
        name="line_sum",
    )(g, a)


def swap(values, d_row, d_col):
    n_row, n_col = lax.axis_size("row"), lax.axis_size("col")
    pairs = [
        (i * n_col + j, (i ^ d_row) * n_col + (j ^ d_col))
        for i in range(n_row)
        for j in range(n_col)
    ]
    return lax.ppermute(values, ("row", "col"), pairs)


def all_sum(values):
    for d_row, d_col in ((1, 0), (0, 1), (2, 0)):
        values = values + swap(values, d_row, d_col)
    if lax.axis_size("dp") != 4:
        return lax.psum(values, "dp")
    for step in (1, 2):
        values = values + lax.ppermute(values, "dp", [(i, i ^ step) for i in range(4)])
    return values


def cut_low(values):
    return lax.reduce_precision(values, 8, 7)


def split3(values):
    high = cut_low(values)
    middle = cut_low(values - high)
    low = cut_low(values - high - middle)
    return jnp.stack([high, middle, low]).astype(BF)


def dp_sums(grads, attn):
    if lax.axis_size("dp") != 4:
        return lax.psum(grads.astype(F32), "dp"), lax.psum(attn.astype(F32), "dp")
    return line_sum(grads, attn)


def body(
    tokens,
    cotangent,
    weight_query,
    weight_key,
    weight_value,
    weight_out,
    weight_gate,
    weight_up,
    weight_down,
    gain_input,
    gain_attn,
    gain_pre,
    gain_post,
    gain_query,
    gain_key,
    doc_lengths,
    block_size,
):
    n_row, n_col = lax.axis_size("row"), lax.axis_size("col")
    members = n_row * n_col
    tok_count, cut = tokens.shape
    width = cut * members
    local = tok_count // members
    row, col = lax.axis_index("row"), lax.axis_index("col")
    high, core = row // 2, row % 2
    me = row * n_col + col
    depth = weight_query.shape[0]
    q_half = weight_query.shape[1]
    kv_half = weight_key.shape[1]
    qkv_half = q_half + 2 * kv_half
    head_count = n_col * q_half // HD
    hidden_half = weight_gate.shape[1]
    slab = -(-hidden_half // 512) * 256
    query_scale = 1.0 / math.sqrt(HD)

    gains = jnp.concatenate([split3(g) for g in (gain_input, gain_attn, gain_pre, gain_post)])
    gains = jnp.broadcast_to(jnp.pad(gains, ((0, 4), (0, 0)))[None], (members, 16, cut))
    token_blocks = jnp.concatenate([tokens.reshape(members, local, cut), gains], axis=1)
    attn_block = jnp.concatenate([weight_query, weight_key, weight_value, weight_out.T], axis=1)
    hidden_block = jnp.pad(
        jnp.stack([weight_gate, weight_up, weight_down.T]),
        ((0, 0), (0, 0), (0, 2 * slab - hidden_half)),
    )
    got_tokens, got_cotangent, w_attn, w_hidden = entry(
        token_blocks, cotangent.reshape(members, local, cut), attn_block, hidden_block
    )
    with_gains = got_tokens.transpose(1, 0, 2).reshape(-1, width)
    inputs = with_gains[:local].astype(F32)
    upstream_bf = got_cotangent.transpose(1, 0, 2).reshape(local, width)
    upstream = upstream_bf.astype(F32)
    gain_rows = with_gains[local : local + 12].astype(F32).reshape(4, 3, width).sum(axis=1)
    g_input, g_attn, g_pre, g_post = (gain_rows[i] for i in range(4))
    w_qkv = w_attn[:, :, :qkv_half]
    w_out = jnp.concatenate([w_attn[j, :, qkv_half:] for j in range(n_col)], axis=1)

    lengths = doc_lengths[0]
    span = block_size[0]
    slots = [
        ((row + 2 * (s // 4)) % 4 // 2 * 2 + (core + (s // 2) % 2) % 2) * n_col + (col + s) % 2
        for s in range(members)
    ]
    my_tokens = me * local + jnp.arange(local, dtype=jnp.int32)
    key_tokens = jnp.concatenate([s * local + jnp.arange(local, dtype=jnp.int32) for s in slots])
    my_document, my_places = positions(lengths, my_tokens)
    key_document, key_places = positions(lengths, key_tokens)
    allowed = (my_document[:, None] == key_document[None, :]) & (
        key_places[None, :] // span <= my_places[:, None] // span
    )
    cos_table, sin_table = angles(my_places)
    cos_heads, sin_heads = cos_table[:, None, :], sin_table[:, None, :]

    normed, inverse_in = norm(inputs, g_input)
    normed_bf = normed.astype(BF)
    projected = [nn(normed_bf, w_qkv[j]) for j in range(n_col)]
    query_pre = jnp.concatenate([p[:, :q_half] for p in projected], axis=1).reshape(
        local, head_count, HD
    )
    key_pre = jnp.concatenate([p[:, q_half : q_half + kv_half] for p in projected], axis=1)
    value_pre = jnp.concatenate([p[:, q_half + kv_half :] for p in projected], axis=1)
    query_bf = (head_norm(query_pre, gain_query, cos_heads, sin_heads) * query_scale).astype(BF)
    key_bf = head_norm(key_pre, gain_key, cos_table, sin_table).astype(BF)
    kv_all = kv_gather(jnp.concatenate([key_bf, value_pre.astype(BF)], axis=1))
    kv_all = kv_all.reshape(tok_count, 2 * HD)
    keys_bf, values_bf = kv_all[:, :HD], kv_all[:, HD:]

    def attention_scores():
        raw = jnp.einsum("thd,sd->hts", query_bf, keys_bf, preferred_element_type=F32)
        return jnp.where(allowed[None, :, :], raw, -1e30)

    scores = attention_scores()
    row_peak = jnp.max(scores, axis=-1, keepdims=True)
    exp_scores = jnp.exp(scores - row_peak)
    totals = jnp.sum(exp_scores, axis=-1, keepdims=True)
    log_total = row_peak + jnp.log(totals)
    probs_bf = (exp_scores / totals).astype(BF)
    head_out = jnp.einsum("hts,sd->thd", probs_bf, values_bf, preferred_element_type=F32)
    head_bf = head_out.astype(BF).reshape(local, head_count * HD)
    attn_out = nt(head_bf, w_out)
    attn_normed, inverse_attn = norm(attn_out, g_attn)
    residual = inputs + attn_normed
    pre_normed, inverse_pre = norm(residual, g_pre)

    layer_rows, grad_g_post, grad_pre, hidden_grads = mlp(
        pre_normed.astype(BF), residual, upstream_bf, g_post[None], w_hidden[0], w_hidden[1], w_hidden[2]
    )

    grad_resid, grad_g_pre = norm_back(residual, g_pre, inverse_pre, grad_pre)
    grad_resid = grad_resid + upstream
    grad_attn, grad_g_attn = norm_back(attn_out, g_attn, inverse_attn, grad_resid)
    grad_attn_bf = grad_attn.astype(BF)
    grad_w_out = tn(grad_attn_bf, head_bf)
    grad_head_bf = nn(grad_attn_bf, w_out).astype(BF).reshape(local, head_count, HD)

    scores = attention_scores()
    probs = jnp.exp(scores - log_total)
    probs_bf = probs.astype(BF)
    grad_probs = jnp.einsum("thd,sd->hts", grad_head_bf, values_bf, preferred_element_type=F32)
    grad_values = jnp.einsum("hts,thd->sd", probs_bf, grad_head_bf, preferred_element_type=F32)
    row_inner = jnp.sum(probs * grad_probs, axis=-1, keepdims=True)
    grad_scores = (probs * (grad_probs - row_inner)).astype(BF)
    grad_query = (
        jnp.einsum("hts,sd->thd", grad_scores, keys_bf, preferred_element_type=F32) * query_scale
    )
    grad_keys = jnp.einsum("hts,thd->sd", grad_scores, query_bf, preferred_element_type=F32)
    grad_kv = kv_sum(
        jnp.concatenate([grad_keys, grad_values], axis=1).astype(BF).reshape(members, local, 2 * HD)
    )
    grad_key, grad_value = grad_kv[:, :HD], grad_kv[:, HD:]

    unused, pull = jax.vjp(
        lambda rows_in, scales_in: head_norm(rows_in, scales_in, cos_heads, sin_heads),
        query_pre,
        gain_query,
    )
    grad_query_pre, grad_g_query = pull(grad_query)
    unused, pull = jax.vjp(
        lambda rows_in, scales_in: head_norm(rows_in, scales_in, cos_table, sin_table),
        key_pre,
        gain_key,
    )
    grad_key_pre, grad_g_key = pull(grad_key)
    grad_query_bf = grad_query_pre.astype(BF).reshape(local, head_count * HD)
    grad_key_bf = grad_key_pre.astype(BF)
    grad_value_bf = grad_value.astype(BF)
    grad_halves = [
        jnp.concatenate(
            [
                grad_query_bf[:, j * q_half : (j + 1) * q_half],
                grad_key_bf[:, j * kv_half : (j + 1) * kv_half],
                grad_value_bf[:, j * kv_half : (j + 1) * kv_half],
            ],
            axis=1,
        )
        for j in range(n_col)
    ]
    grad_normed = sum(nt(grad_halves[j], w_qkv[j]) for j in range(n_col))
    grad_in, grad_g_input = norm_back(inputs, g_input, inverse_in, grad_normed)

    out_half = grad_w_out.shape[1] // n_col
    attn_grads = jnp.stack(
        [
            jnp.concatenate(
                [tn(normed_bf, grad_halves[j]), grad_w_out[:, j * out_half : (j + 1) * out_half]], axis=1
            ).astype(BF)
            for j in range(n_col)
        ]
    ).reshape(n_col, n_row, depth, -1)
    attn_mine = attn_sum(attn_grads)
    feats = attn_mine.shape[1]
    attn_pair = jnp.stack([attn_mine[:, : feats // 2], attn_mine[:, feats // 2 :]])[None]
    tiles = hidden_grads.shape[1]
    hidden_sum, attn_pair = dp_sums(
        hidden_grads.reshape((3 * tiles, 2, depth, TILE)), attn_pair
    )
    attn_mine = jnp.concatenate([attn_pair[0, 0], attn_pair[0, 1]], axis=1).astype(F32)
    hidden_sum = hidden_sum.reshape(3, tiles, 2, depth, TILE)
    hidden_sum = jnp.where(high == 0, hidden_sum, hidden_sum[:, :, ::-1])
    hidden_sum = hidden_sum.transpose(0, 3, 2, 1, 4).reshape(3, depth, 2 * slab)
    hidden_sum = hidden_sum[:, :, :hidden_half].astype(F32)

    def from_tokens(values):
        cubes = values.astype(BF).reshape(local, members, cut).transpose(1, 0, 2)
        return lax.all_to_all(cubes, ("row", "col"), split_axis=0, concat_axis=0, tiled=True).reshape(
            tok_count, cut
        )

    grad_tokens = from_tokens(grad_in + grad_resid).astype(F32)
    layer_out = from_tokens(layer_rows)

    def my_gain(values):
        return lax.dynamic_slice_in_dim(values, me * cut, cut, 0)

    sums = all_sum(
        jnp.concatenate([grad_g_input, grad_g_attn, grad_g_pre, grad_g_post[0], grad_g_query, grad_g_key])
    )
    return (
        layer_out,
        grad_tokens,
        attn_mine[:, :q_half],
        attn_mine[:, q_half : q_half + kv_half],
        attn_mine[:, q_half + kv_half : qkv_half],
        attn_mine[:, qkv_half:].T,
        hidden_sum[0],
        hidden_sum[1],
        hidden_sum[2].T,
        my_gain(sums[:width]),
        my_gain(sums[width : 2 * width]),
        my_gain(sums[2 * width : 3 * width]),
        my_gain(sums[3 * width : 4 * width]),
        sums[4 * width : 4 * width + HD],
        sums[4 * width + HD :],
    )


def solution(mesh):
    in_specs = (
        P("dp", ("row", "col")),
        P("dp", ("row", "col")),
        P("row", "col"),
        P("row", "col"),
        P("row", "col"),
        P("col", "row"),
        P("row", "col"),
        P("row", "col"),
        P("col", "row"),
        P(("row", "col")),
        P(("row", "col")),
        P(("row", "col")),
        P(("row", "col")),
        P(),
        P(),
        P("dp", None),
        P(),
    )
    out_specs = (
        P("dp", ("row", "col")),
        P("dp", ("row", "col")),
        P("row", "col"),
        P("row", "col"),
        P("row", "col"),
        P("col", "row"),
        P("row", "col"),
        P("row", "col"),
        P("col", "row"),
        P(("row", "col")),
        P(("row", "col")),
        P(("row", "col")),
        P(("row", "col")),
        P(),
        P(),
    )
    return jax.shard_map(body, mesh=mesh, in_specs=in_specs, out_specs=out_specs, check_vma=False)
```

time: 2150 us -> 801 us (0.37)
  waiting for transfers between devices: 1620 us -> 9.39 us
  Pallas kernels: 0 us -> 573 us
  blocking collectives: 252 us -> 0 us
  matrix products: 149 us -> 34.4 us
  local copies, waits for them, and re-layouts: 28.3 us -> 91.6 us
    reduce_scatter x8 -> x0, waiting for transfers between devices: 769 us -> none  [the longest x2 585 us: row_sums(): return lax.psum_scatter(values, 'row', scatter_dimension=2, tiled=True)]
    pallas_call x0 -> x6, Pallas kernels: none -> 573 us  [the longest x1 183 us: line_sum(): pl.pallas_call(line_kernel, out_shape=(jax.ShapeDtypeStruct(g.shape, BF),...]
    psum x3 -> x0, waiting for transfers between devices: 466 us -> none  [the longest x1 430 us: body(): lax.psum((grad_weight_query, grad_weight_key, grad_weight_value, grad_wei...]
    all_gather x10 -> x0, waiting for transfers between devices: 387 us -> none  [the longest x2 263 us: row_gather(): return lax.all_gather(values, 'row', axis=2, tiled=True)]
    psum x11 -> x0, blocking collectives: 252 us -> none  [the longest x8 109 us: feature_sum(): return lax.psum(jnp.sum(values, axis=1), ('row', 'col'))]
    dot_general x22 -> x13, matrix products: 138 us -> 28.2 us  [the longest x9 17.6 us: dot(): lax.dot_general(left, right, (dims, ((), ())), preferred_element_type=F32)]
    reshape x1 -> x7, local copies, waits for them, and re-layouts: 1.88 us -> 25.9 us  [the longest x1 12.4 us: body(): hidden_sum = hidden_sum.transpose(0, 3, 2, 1, 4).reshape(3, depth, 2 * slab)]
  transfers between devices with their start and end apart: 21 -> 7, of which waited for: 18 -> 4; matrix products, arithmetic and copies ran while one was open for 4% -> 15% of each run, Pallas kernels for 0% -> 31%
where the time goes in v1:
time: 801 us; the launch traced here: 793 us
  Pallas kernels  573 us (72%)
  local copies, waits for them, and re-layouts  91.6 us (11%)
  other arithmetic  66.9 us (8%)
  matrix products  34.4 us (4%)
  starting transfers between devices  14.4 us (2%)
  waiting for transfers between devices  9.39 us (1%)
    pallas_call x1, Pallas kernels, line_sum(): pl.pallas_call(line_kernel, out_shape=(jax.ShapeDtypeStruct(g.shape, BF),...  183 us
    pallas_call x1, Pallas kernels, mlp(): pl.pallas_call(mlp_kernel, out_shape=(jax.ShapeDtypeStruct((loc, width),...  180 us
    pallas_call x1, Pallas kernels, entry(): pl.pallas_call(entry_kernel, out_shape=(jax.ShapeDtypeStruct(tk.shape, BF...  130 us
    pallas_call x1, Pallas kernels, attn_sum(): pl.pallas_call(attn_sum_kernel, out_shape=jax.ShapeDtypeStruct(shape, BF)...  41.9 us
    unnamed x177, local copies, waits for them, and re-layouts  22.2 us
    pallas_call x1, Pallas kernels, kv_sum(): pl.pallas_call(kv_sum_kernel, out_shape=jax.ShapeDtypeStruct(shape, F32),...  20.9 us
    dot_general x9, matrix products, dot(): lax.dot_general(left, right, (dims, ((), ())), preferred_element_type=F32)  17.6 us
    pallas_call x1, Pallas kernels, kv_gather(): pl.pallas_call(kv_kernel, out_shape=jax.ShapeDtypeStruct((8,) + kv.shape,...  16.8 us
  transfers between devices with their start and end apart: 7, of which 4 were waited for; matrix products, arithmetic and copies ran while one was open for 15% of the time, Pallas kernels for 31%

profile of v1, /device:TPU:0, one launch (start us, length us, event | category | flops | bytes accessed | tf_op | source)
XLA Modules:
  0.0 792.7 jit_solution(6997963014944616786)
XLA Ops:
  4.9 2.3 copy.237
  9.2 4.5 fusion.12.wm
  14.7 129.9 %entry.1 = (bf16[8,272,144]{2,1,0:T(8,128)(2,1)}, bf16[8,256,144]{2,1,0:T(8,128)(2,1)}, bf16[2,1152,1280]{2,1,0:T(8,128)(2,1)}, bf16[3,1152,1792]{2,1,0:T(8,128)(2,1)}) custom-call(bf16[8,272,144]{2,1,0:T(8,128)(2,1)} %pad_maximum_fusion.6.tk, bf16[8,256,144]{2,1,0:T(8,128)(2,1)} %bitcast.191, bf16[288,1280]{1,0:T(8,128)(2,1)} %pad_maximum_fusion.9.wa, ...), custom_call_target="tpu_custom_call" | custom-call | tf_op jit(solution)/shard_map/entry/pallas_call | solution.py:210
  144.6 2.8 slice_convert_fusion.1
  152.5 2.5 fusion.20
  160.1 3.3 slice_bitcast_fusion.7
  165.0 2.7 copy.248
  174.6 16.8 %kv_gather.1 = bf16[8,256,512]{2,1,0:T(8,128)(2,1)} custom-call(bf16[256,512]{1,0:T(8,128)(2,1)} %pad_maximum_fusion.13.kv), custom_call_target="tpu_custom_call" | custom-call | tf_op jit(solution)/shard_map/kv_gather/pallas_call | solution.py:259
  191.6 2.3 compare_and_fusion.1
  193.9 3.1 fusion.10
  200.6 2.4 fusion.29
  207.3 8.8 %slice_bitcast_fusion = (bf16[1152,1792]{1,0:T(8,128)(2,1)}, bf16[1152,1792]{1,0:T(8,128)(2,1)}, bf16[1152,1792]{1,0:T(8,128)(2,1)}) fusion(bf16[3,1152,1792]{2,1,0:T(8,128)(2,1)} %get-tuple-element.28), kind=kLoop, calls=%fused_computation.25 | loop fusion | bytes 24772608 | tf_op jit(solution)/shard_map/squeeze | solution.py:879
  217.1 180.3 %feed_forward.1 = (bf16[256,1152]{1,0:T(8,128)(2,1)}, f32[1,1152]{1,0:T(1,128)}, f32[256,1152]{1,0:T(8,128)}, bf16[3,7,2,288,256]{4,3,2,1,0:T(8,128)(2,1)}) custom-call(bf16[256,1152]{1,0:T(8,128)(2,1)} %multiply_convert_fusion.2.pre, f32[256,1152]{1,0:T(8,128)} %copy-done.1, bf16[256,1152]{1,0:T(8,128)(2,1)} %copy.250.ct, ...), custom_call_target="tpu_custom_call" | custom-call | tf_op jit(solution)/shard_map/feed_forward/pallas_call | solution.py:435
  399.7 4.5 all-to-all-start
  404.3 2.3 compare_and_fusion
  413.5 5.0 fusion.4
  418.6 4.9 fusion.5
  431.5 20.9 %kv_sum.1 = f32[256,512]{1,0:T(8,128)} custom-call(bf16[8,256,512]{2,1,0:T(8,128)(2,1)} %pad_maximum_fusion.1.parts), custom_call_target="tpu_custom_call" | custom-call | tf_op jit(solution)/shard_map/kv_sum/pallas_call | solution.py:501
  455.1 3.8 fusion.28
  463.5 2.3 convolution_add_fusion
  476.9 2.9 convert_bitcast_fusion
  483.6 2.9 maximum_maximum_fusion.parts
  486.5 41.9 %attn_sum.1 = bf16[288,1280]{1,0:T(8,128)(2,1)} custom-call(bf16[2,4,288,1280]{3,2,1,0:T(8,128)(2,1)} %maximum_maximum_fusion.parts), custom_call_target="tpu_custom_call" | custom-call | tf_op jit(solution)/shard_map/attn_sum/pallas_call | solution.py:549
  530.5 182.8 %line_sum.1 = (bf16[21,2,288,256]{3,2,1,0:T(8,128)(2,1)}, bf16[1,2,288,640]{3,2,1,0:T(8,128)(2,1)}) custom-call(bf16[21,2,288,256]{3,2,1,0:T(8,128)(2,1)} %bitcast.182, bf16[1,2,288,640]{3,2,1,0:T(8,128)(2,1)} %maximum_bitcast_fusion.a), custom_call_target="tpu_custom_call" | custom-call | tf_op jit(solution)/shard_map/line_sum/pallas_call | solution.py:723
  713.3 9.2 %copy.269 = bf16[3,7,2,288,256]{4,1,2,3,0:T(8,128)(2,1)} copy(bf16[3,7,2,288,256]{4,3,2,1,0:T(8,128)(2,1)} %bitcast.183) | data formatting | bytes 12386304 | tf_op jit(solution)/shard_map/reshape | solution.py:951
  722.6 9.5 %fusion.9 = bf16[3,288,2,7,256]{4,3,2,1,0:T(8,128)(2,1)} fusion(bf16[3,7,2,288,256]{4,1,2,3,0:T(8,128)(2,1)} %copy.269, pred[]{:T(512)S(6)} %eq.91), kind=kLoop, calls=%fused_computation.18 | loop fusion | flops 3096576 | bytes 12386305 | tf_op jit(solution)/shard_map/transpose | solution.py:953
  732.1 12.4 %reshape.513 = bf16[3,288,3584]{2,1,0:T(8,128)(2,1)} reshape(bf16[3,288,2,7,256]{4,3,2,1,0:T(8,128)(2,1)} %fusion.9) | data formatting | bytes 12386304 | tf_op jit(solution)/shard_map/reshape | solution.py:953
  744.5 7.8 slice_convert_fusion
  752.3 9.4 %slice_bitcast_fusion.3 = (f32[3456,288]{0,1:T(8,128)}, f32[288,3456]{1,0:T(8,128)}, f32[288,3456]{1,0:T(8,128)}) fusion(f32[3,288,3456]{2,1,0:T(8,128)} %slice_convert_fusion), kind=kLoop, calls=%fused_computation.28 | loop fusion | bytes 23887872 | tf_op jit(solution)/shard_map/transpose | solution.py:980
  774.3 3.3 collective-permute-start.4
  777.6 3.5 all-to-all-start.1
  787.8 3.2 all-to-all-done.1
  (329 shorter events, 95.0 us)
Async XLA Ops:
  156.1 15.7 %copy-start.8 = (f32[256,4,256]{0,2,1:T(8,128)}, f32[256,4,256]{0,2,1:T(8,128)S(1)}, u32[]{:S(2)}) copy-start(f32[256,4,256]{0,2,1:T(8,128)S(1)} %copy.242) | copy-start | bytes 3145732
  165.0 4.7 copy-start.80
  165.0 5.9 copy-start.77
  172.5 19.1 %copy-start.68 = (s32[256]{0:T(256)S(1)}, s32[256]{0:T(256)}, u32[]{:S(2)}) copy-start(s32[256]{0:T(256)} %copy-done.67) | copy-start | bytes 3076
  193.9 4.6 copy-start.3
  205.0 11.1 %copy-start.1 = (f32[256,1152]{1,0:T(8,128)}, f32[256,1152]{1,0:T(8,128)S(1)}, u32[]{:S(2)}) copy-start(f32[256,1152]{1,0:T(8,128)S(1)} %get-tuple-element.50.res) | copy-start | bytes 3538948
  397.4 6.8 copy-start.69
  397.5 6.8 copy-start.72
  397.5 9.1 %copy-start.2 = (f32[256,1152]{1,0:T(8,128)S(1)}, f32[256,1152]{1,0:T(8,128)}, u32[]{:S(2)}) copy-start(f32[256,1152]{1,0:T(8,128)} %copy-done.1) | copy-start | bytes 3538948
  399.7 9.0 %copy-start.15 = (f32[256,1152]{1,0:T(8,128)S(1)}, f32[256,1152]{1,0:T(8,128)}, u32[]{:S(2)}) copy-start(f32[256,1152]{1,0:T(8,128)} %copy-done.14) | copy-start | bytes 3538948
  399.7 9.0 %copy-start.23 = (bf16[256,1152]{1,0:T(8,128)(2,1)S(1)}, bf16[256,1152]{1,0:T(8,128)(2,1)}, u32[]{:S(2)}) copy-start(bf16[256,1152]{1,0:T(8,128)(2,1)} %copy.250.ct) | copy-start | bytes 1769476
  399.7 377.9 %all-to-all-start = ((bf16[8,256,144]{1,2,0:T(8,128)(2,1)}), bf16[8,256,144]{1,2,0:T(8,128)(2,1)}, u32[]{:S(2)}, u32[]{:S(2)}) async-start(bf16[8,256,144]{1,2,0:T(8,128)(2,1)} %bitcast.196), calls=%async_computation | async-start | bytes 1179648 | tf_op jit(solution)/shard_map/all_to_all | solution.py:958
  413.5 5.0 copy-start.4
  413.5 5.0 copy-start.19
  418.5 5.0 slice-start
  418.6 5.9 slice-start.1
  431.5 22.0 %copy-start.71 = (f32[256]{0:T(256)S(1)}, f32[256]{0:T(256)}, u32[]{:S(2)}) copy-start(f32[256]{0:T(256)} %copy-done.70) | copy-start | bytes 3076
  431.5 22.0 %copy-start.78 = (f32[128]{0:T(128)S(1)}, f32[128]{0:T(128)}, u32[]{:S(2)}) copy-start(f32[128]{0:T(128)} %multiply_exponential_fusion) | copy-start | bytes 1540
  455.1 4.8 copy-start.34
  461.1 4.7 copy-start.29
  465.9 4.9 copy-start.75
  465.9 7.5 copy-start.76
  465.9 8.8 %copy-start.28 = (bf16[256,1152]{1,0:T(8,128)(2,1)S(1)}, bf16[256,1152]{1,0:T(8,128)(2,1)}, u32[]{:S(2)}) copy-start(bf16[256,1152]{1,0:T(8,128)(2,1)} %copy-done.27) | copy-start | bytes 1769476
  474.7 287.5 %collective-permute-start = (f32[5120]{0:T(1024)}, f32[5120]{0:T(1024)}, u32[]{:S(2)}, u32[]{:S(2)}) collective-permute-start(f32[5120]{0:T(1024)} %constant_dynamic-update-slice_fusion.9), channel_id=1, source_target_pairs={{0,2},{1,3},{2,0},{3,1},{4,6},{5,7},{6,4},{7,5},{8,10},{9,11},{10,... | collective-permute-start | bytes 61448 | tf_op jit(solution)/shard_map/ppermute | solution.py:745
  752.3 9.4 %copy-start.7 = (f32[256,1152]{1,0:T(8,128)S(1)}, f32[256,1152]{1,0:T(8,128)}, u32[]{:S(2)}) copy-start(f32[256,1152]{1,0:T(8,128)} %copy.248) | copy-start | bytes 3538948
  752.3 9.4 %copy-start.11 = (f32[256,1152]{1,0:T(8,128)S(1)}, f32[256,1152]{1,0:T(8,128)}, u32[]{:S(2)}) copy-start(f32[256,1152]{1,0:T(8,128)} %copy-done.10) | copy-start | bytes 3538948
  752.3 9.4 %copy-start.13 = (f32[256,1152]{1,0:T(8,128)S(1)}, f32[256,1152]{1,0:T(8,128)}, u32[]{:S(2)}) copy-start(f32[256,1152]{1,0:T(8,128)} %copy-done.12) | copy-start | bytes 3538948
  762.9 3.8 collective-permute-start.1
  766.7 3.8 collective-permute-start.2
  770.5 3.8 collective-permute-start.3
  774.3 8.5 %collective-permute-start.4 = (f32[5120]{0:T(1024)S(1)}, f32[5120]{0:T(1024)S(1)}, u32[]{:S(2)}, u32[]{:S(2)}) collective-permute-start(f32[5120]{0:T(1024)S(1)} %add.424), channel_id=1, source_target_pairs={{0,16},{8,24},{16,0},{24,8},{1,17},{9,25},{17,1},{25,9},{2,18},{10... | collective-permute-start | bytes 61448 | tf_op jit(solution)/shard_map/ppermute | solution.py:754
  777.6 13.4 %all-to-all-start.1 = ((bf16[8,256,144]{1,2,0:T(8,128)(2,1)}), bf16[8,256,144]{1,2,0:T(8,128)(2,1)S(1)}, u32[]{:S(2)}, u32[]{:S(2)}) async-start(bf16[8,256,144]{1,2,0:T(8,128)(2,1)} %bitcast.44), calls=%async_computation.1 | async-start | bytes 1179648 | tf_op jit(solution)/shard_map/all_to_all | solution.py:958
  (59 other events, 145.3 us)

commit v2 on v1

--- a/solution.py
+++ b/solution.py
@@ -271,7 +271,7 @@
     pre, res, ct, gpost, wg_h, wu_h, wd_h,
     lo, dgpost, dpre, grads,
     wg, wu, wd, pre_all, pre_t, gm_all, gm_t, aa, bb, hh, acc, own, parts, prc, prc2, dwb, crecv,
-    w_sem, ag_s, ag_r, rs_s, rs_r, gs_s, gs_r, bs_s, bs_r, c_s, c_r, y_s, y_r, l_s,
+    w_sem, ag_s, ag_r, rs_s, rs_r, gs_s, gs_r, bs_s, bs_r, c_s, c_r, l_s,
 ):
     place, row, col, high, core = whereabouts()
     px, py, pd, pc = peers()
@@ -379,11 +379,9 @@
             dwb.at[n % 2, m, 2 * y2 + 1 - core], crecv.at[m, n, y2], c_s.at[n % 2, m, y2], c_r.at[m, n, y2], pc
         )
 
-    def to_far(n, m):
-        return remote(crecv.at[m, n, 1 - high], grads.at[m, n, 1], y_s.at[m, n], y_r.at[m, n], py)
-
-    def to_out(n, m):
-        return pltpu.make_async_copy(crecv.at[m, n, high], grads.at[m, n, 0], l_s.at[m, n])
+    def to_out(n, m, y2):
+        slot = (high + y2) % 2
+        return pltpu.make_async_copy(crecv.at[m, n, y2], grads.at[m, n, slot], l_s.at[m, n, y2])
 
     def produce(n):
         for m, (left, right) in enumerate(((pre_t, bb), (pre_t, aa), (gm_t, hh))):
@@ -399,8 +397,8 @@
                 crecv[m, n, y2] = (
                     crecv[m, n, y2].astype(F32) + dwb[n % 2, m, 2 * y2 + core].astype(F32)
                 ).astype(BF)
-            to_far(n, m).start()
-            to_out(n, m).start()
+            for y2 in range(2):
+                to_out(n, m, y2).start()
 
     produce(0)
 
@@ -417,8 +415,8 @@
 
     def finish(n, carry):
         for m in range(3):
-            to_far(n, m).wait()
-            to_out(n, m).wait()
+            for y2 in range(2):
+                to_out(n, m, y2).wait()
         return carry
 
     lax.fori_loop(0, tiles, finish, 0)
@@ -462,104 +460,11 @@
             pltpu.VMEM((3, tiles, 2, depth, TILE), BF),
             dma((3,)),
             dma((3,)), dma((3,)), dma((3,)), dma((3,)), dma((3,)), dma((3,)), dma((3,)), dma((3,)),
-            dma((2, 3, 2)), dma((3, tiles, 2)), dma((3, tiles)), dma((3, tiles)), dma((3, tiles)),
+            dma((2, 3, 2)), dma((3, tiles, 2)), dma((3, tiles, 2)),
         ],
         compiler_params=params(3),
         name="feed_forward",
     )(pre, res, ct, gpost, w_gate, w_up, w_down)
-
-
-def kv_sum_kernel(parts, out, cr, summed, qr, c_s, c_r, q_s, q_r):
-    px, py, pd, pc = peers()
-    greet((px, py, pd, pc))
-    core = [
-        remote(parts.at[slot + 2], cr.at[i], c_s.at[i], c_r.at[i], pc) for i, slot in enumerate(KV_SLOTS)
-    ]
-    for copy in core:
-        copy.start()
-    sends = []
-    for i, device in ((3, pd), (1, px), (2, py), (0, None)):
-        core[i].wait_recv()
-        total = parts[KV_SLOTS[i]].astype(F32) + cr[i].astype(F32)
-        if device is None:
-            out[...] = total
-        else:
-            summed[i - 1] = total.astype(BF)
-            copy = remote(summed.at[i - 1], qr.at[i - 1], q_s.at[i - 1], q_r.at[i - 1], device)
-            copy.start()
-            sends.append(copy)
-    for copy in sends:
-        copy.wait()
-    out[...] += qr[0].astype(F32) + qr[1].astype(F32) + qr[2].astype(F32)
-    for copy in core:
-        copy.wait_send()
-
-
-def kv_sum(parts):
-    shape = parts.shape[1:]
-    dma = pltpu.SemaphoreType.DMA
-    return pl.pallas_call(
-        kv_sum_kernel,
-        out_shape=jax.ShapeDtypeStruct(shape, F32),
-        in_specs=[vmem_spec()],
-        out_specs=vmem_spec(),
-        scratch_shapes=[
-            pltpu.VMEM((4,) + shape, BF),
-            pltpu.VMEM((3,) + shape, BF),
-            pltpu.VMEM((3,) + shape, BF),
-            dma((4,)), dma((4,)), dma((3,)), dma((3,)),
-        ],
-        compiler_params=params(4),
-        name="kv_sum",
-    )(parts)
-
-
-def attn_sum_kernel(parts, out, cr, summed, qr, c_s, c_r, q_s, q_r):
-    place, row, col, high, core = whereabouts()
-    px, py, pd, pc = peers()
-    greet((px, py, pd, pc))
-    wanted = ((1 - col, 1 - high, pd), (1 - col, high, px), (col, 1 - high, py), (col, high, None))
-    copies = [
-        remote(parts.at[c2, 2 * y2 + 1 - core], cr.at[c2, y2], c_s.at[i], c_r.at[c2, y2], pc)
-        for i, (c2, y2, _) in enumerate(wanted)
-    ]
-    for copy in copies:
-        copy.start()
-    sends = []
-    for i, (c2, y2, device) in enumerate(wanted):
-        copies[i].wait_recv()
-        total = parts[c2, 2 * y2 + core].astype(F32) + cr[c2, y2].astype(F32)
-        if device is None:
-            own = total
-        else:
-            summed[i] = total.astype(BF)
-            copy = remote(summed.at[i], qr.at[i], q_s.at[i], q_r.at[i], device)
-            copy.start()
-            sends.append(copy)
-    for copy in sends:
-        copy.wait()
-    out[...] = (own + qr[0].astype(F32) + qr[1].astype(F32) + qr[2].astype(F32)).astype(BF)
-    for copy in copies:
-        copy.wait_send()
-
-
-def attn_sum(parts):
-    shape = parts.shape[2:]
-    dma = pltpu.SemaphoreType.DMA
-    return pl.pallas_call(
-        attn_sum_kernel,
-        out_shape=jax.ShapeDtypeStruct(shape, BF),
-        in_specs=[vmem_spec()],
-        out_specs=vmem_spec(),
-        scratch_shapes=[
-            pltpu.VMEM((2, 2) + shape, BF),
-            pltpu.VMEM((3,) + shape, BF),
-            pltpu.VMEM((3,) + shape, BF),
-            dma((4,)), dma((2, 2)), dma((3,)), dma((3,)),
-        ],
-        compiler_params=params(5),
-        name="attn_sum",
-    )(parts)
 
 
 class Line:
@@ -650,19 +555,30 @@
             for h in range(2):
                 self.outward(k, h, self.out).wait_send()
 
-    def greet(self):
-        barrier = pltpu.get_barrier_semaphore()
-
-        @pl.when(self.end)
-        def _():
-            pl.semaphore_signal(barrier, inc=1, device_id=self.inner, device_id_type=MESH)
-            pl.semaphore_wait(barrier, 1)
-
-        @pl.when(jnp.logical_not(self.end))
-        def _():
-            pl.semaphore_signal(barrier, inc=1, device_id=self.outer, device_id_type=MESH)
-            pl.semaphore_signal(barrier, inc=1, device_id=self.across, device_id_type=MESH)
-            pl.semaphore_wait(barrier, 2)
+
+class Alone:
+    def __init__(self, mine, inbox, middle, out, sems):
+        self.mine, self.out, self.sems = mine, out, sems[0]
+
+    def send(self, k):
+        pass
+
+    def add(self, k):
+        pass
+
+    def forward(self, k):
+        pass
+
+    def copy(self, k, h):
+        return pltpu.make_async_copy(self.mine.at[k, h], self.out.at[k, h], self.sems.at[k, h])
+
+    def total(self, k):
+        for h in range(2):
+            self.copy(k, h).start()
+
+    def drain(self, k):
+        for h in range(2):
+            self.copy(k, h).wait()
 
 
 def line_sems(count):
@@ -673,86 +589,396 @@
     ]
 
 
-def line_kernel(g, a, g_out, a_out, g_mine, g_in, g_mid, a_mine, a_in, a_mid, load, *sems):
-    big = Line(g_mine, g_in, g_mid, g_out, sems[:9])
-    small = Line(a_mine, a_in, a_mid, a_out, sems[9:])
-    count = g_mine.shape[0]
-    fetch = [pltpu.make_async_copy(g, g_mine, load.at[0]), pltpu.make_async_copy(a, a_mine, load.at[1])]
-    for copy in fetch:
+def mask_bias(lengths, span, bias, me, slots):
+    local = bias.shape[1]
+    inverse = 1.0 / jnp.full((1, 1), span[0], jnp.int32).astype(F32)
+
+    def place(tokens):
+        document = jnp.zeros_like(tokens)
+        first = jnp.zeros_like(tokens)
+        end = jnp.int32(0)
+        for i in range(lengths.shape[1]):
+            end = end + lengths[0, i]
+            past = tokens >= end
+            document = jnp.where(past, i + 1, document)
+            first = jnp.where(past, end, first)
+        return document, jnp.floor(((tokens - first).astype(F32) + 0.5) * inverse)
+
+    query_doc, query_block = place(me * local + lax.broadcasted_iota(jnp.int32, (1, local), 1))
+    for s, owner in enumerate(slots):
+        key_doc, key_block = place(owner * local + lax.broadcasted_iota(jnp.int32, (local, 1), 0))
+        seen = (key_doc == query_doc) & (key_block <= query_block)
+        bias[s * local : (s + 1) * local, :] = jnp.where(seen, 0.0, -1e30)
+
+
+def slot_owners():
+    place, row, col, high, core = whereabouts()
+    owners = []
+    for s in range(8):
+        r2 = (high + s // 4) % 2 * 2 + (core + s // 2) % 2
+        owners.append(2 * r2 + (col + s) % 2)
+    return owners
+
+
+def sent_to_all(index):
+    place, row, col, high, core = whereabouts()
+    others = []
+    for s in range(1, 8):
+        r2, c2 = (high + s // 4) % 2 * 2 + (core + s // 2) % 2, (col + s) % 2
+        others.append((2 * r2 + c2, (place, r2, c2)))
+    return others
+
+
+def back_kernel(
+    grads, lo, dpre, res, ao, ct, x, gains, gq, gk, heads, q_pre, k_pre, q_bf, kv, lse, cos, sin, wa, dgpost, lengths, span,
+    g_out, a_out, lo_out, gt_out, gain_out,
+    mine, inbox, middle, a_mine, a_in, a_mid,
+    bias, k_t, ga, gh, dk, dv, stage, kv_cr, kv_sum_, kv_qr, dh, g_res, parts, cr, summed, qr, lo_cut, gt_cut, gain_buf, gain_in,
+    f_s, y_s, y_r, kc_s, kc_r, kq_s, kq_r, pc_s, pc_r, pq_s, pq_r, lo_s, lo_r, gt_s, gt_r, gn_s, gn_r, loc_s, *line_refs,
+):
+    place, row, col, high, core = whereabouts()
+    me = 2 * row + col
+    px, py, pd, pc = peers()
+    quad = (px, py, pd)
+    others = sent_to_all(me)
+    on_line = lax.axis_size("dp") == 4
+    make = Line if on_line else Alone
+    line = make(mine, inbox, middle, g_out, line_refs[:9])
+    small = make(a_mine, a_in, a_mid, a_out, line_refs[9:])
+    hidden_pairs = grads.shape[0]
+    pairs = mine.shape[0]
+    loc, width = x.shape
+    depth = mine.shape[2]
+    cut = width // 8
+    head_count = q_pre.shape[1] // HD
+    half = HD // 2
+
+    gain_peers = [pc, px, py]
+    friends = [device for _, device in others]
+    if on_line:
+        gain_peers += [(place + 1 - 2 * (place % 2), row, col), ((place + 2) % 4, row, col)]
+        friends += [((place + i) % 4, row, col) for i in range(1, 4)]
+    greet(friends)
+
+    def fetch(k):
+        return pltpu.make_async_copy(grads.at[k, 0], mine.at[k, 0], f_s.at[k])
+
+    def pull(k):
+        return remote(grads.at[k, 1], mine.at[k, 1], y_s.at[k], y_r.at[k], py)
+
+    def begin(k, carry):
+        fetch(k).start()
+        pull(k).start()
+        return carry
+
+    lax.fori_loop(0, hidden_pairs, begin, 0)
+
+    def ready(k):
+        fetch(k).wait()
+        pull(k).wait_recv()
+        line.send(k)
+
+    def line_step(k):
+        for j in (2 * k + 1, 2 * k + 2):
+            if isinstance(k, int):
+                if j < hidden_pairs:
+                    ready(j)
+        line.add(k)
+        if not isinstance(k, int) or k >= 1:
+            line.total(k - 1)
+        if not isinstance(k, int) or k >= 2:
+            line.forward(k - 2)
+
+    for f in range(8):
+        lo_cut[f] = lo[:, f * cut : (f + 1) * cut]
+    lo_copies = [remote(lo_cut.at[i], lo_out.at[me], lo_s.at[j], lo_r.at[j], d) for j, (i, d) in enumerate(others)]
+    for copy in lo_copies:
         copy.start()
-    big.greet()
-    for copy in fetch:
+    lo_own = pltpu.make_async_copy(lo_cut.at[me], lo_out.at[me], loc_s.at[0])
+    lo_own.start()
+
+    def norm_grad(values, scales, upstream):
+        inverse = lax.rsqrt(jnp.mean(values * values, axis=1, keepdims=True) + EPS)
+        scaled = upstream * (1.0 + scales)
+        inner = jnp.mean(scaled * values, axis=1, keepdims=True)
+        grad = scaled * inverse - values * (inverse * inverse * inverse * inner)
+        return grad, jnp.sum(upstream * values * inverse, axis=0, keepdims=True)
+
+    gain_buf[...] = jnp.zeros_like(gain_buf)
+    grad, gain_buf[0, 2:3, :] = norm_grad(res[...], gains[2:3, :], dpre[...])
+    g_res[...] = grad + ct[...].astype(F32)
+    grad, gain_buf[0, 1:2, :] = norm_grad(ao[...], gains[1:2, :], g_res[...])
+    ga[...] = grad.astype(BF)
+    gain_buf[0, 3:4, :] = dgpost[...]
+    feats = heads.shape[1] // 2
+    qkv = wa.shape[2] - feats
+    for j in range(2):
+        gh[:, j * feats : (j + 1) * feats] = nn(ga[...], wa[j, :, qkv:]).astype(BF)
+    ready(0)
+    mask_bias(lengths, span, bias, me, slot_owners())
+    k_t[...] = kv[:, :HD].T
+    line_step(0)
+
+    step_keys = 512
+    for h in range(head_count):
+        cols = slice(h * HD, (h + 1) * HD)
+        query, grad_head = q_bf[:, cols], gh[:, cols]
+        delta = jnp.sum(
+            (grad_head.astype(F32) * heads[:, cols].astype(F32)).T, axis=0, keepdims=True
+        )
+
+        def keys(c, total, h=h, query=query, grad_head=grad_head, delta=delta):
+            rows = pl.ds(pl.multiple_of(c * step_keys, step_keys), step_keys)
+            scores = nt(kv[rows, :HD], query) + bias[rows, :]
+            probs = jnp.exp(scores - lse[h : h + 1, :])
+            grad_probs = nt(kv[rows, HD:], grad_head)
+            grad_scores = (probs * (grad_probs - delta)).astype(BF)
+            add_v = nn(probs.astype(BF), grad_head)
+            add_k = nn(grad_scores, query)
+            if h:
+                dv[rows, :] += add_v
+                dk[rows, :] += add_k
+            else:
+                dv[rows, :] = add_v
+                dk[rows, :] = add_k
+            return total + nn(k_t[:, rows], grad_scores)
+
+        total = lax.fori_loop(0, kv.shape[0] // step_keys, keys, jnp.zeros((HD, loc), F32))
+        grad_query = total.T * (1.0 / math.sqrt(HD))
+        first, second = grad_query[:, :half], grad_query[:, half:]
+        turned = jnp.concatenate(
+            [first * cos[...] + second * sin[...], second * cos[...] - first * sin[...]], axis=1
+        )
+        grad, gain = norm_grad(q_pre[:, cols], gq[...], turned)
+        gain_buf[0, 4:5, :HD] += gain
+        dh[h // 2, :, (h % 2) * HD : (h % 2 + 1) * HD] = grad.astype(BF)
+        line_step(h + 1)
+
+    for i, slot in enumerate(KV_SLOTS):
+        rows = slice((slot + 2) * loc, (slot + 3) * loc)
+        stage[i, :, :HD] = dk[rows, :].astype(BF)
+        stage[i, :, HD:] = dv[rows, :].astype(BF)
+    kv_core = [remote(stage.at[i], kv_cr.at[i], kc_s.at[i], kc_r.at[i], pc) for i in range(4)]
+    for copy in kv_core:
+        copy.start()
+    line_step(5)
+    kv_sends = []
+    for i, device in ((3, pd), (1, px), (2, py)):
+        kv_core[i].wait_recv()
+        rows = slice(KV_SLOTS[i] * loc, (KV_SLOTS[i] + 1) * loc)
+        kv_sum_[i - 1, :, :HD] = (dk[rows, :] + kv_cr[i, :, :HD].astype(F32)).astype(BF)
+        kv_sum_[i - 1, :, HD:] = (dv[rows, :] + kv_cr[i, :, HD:].astype(F32)).astype(BF)
+        copy = remote(kv_sum_.at[i - 1], kv_qr.at[i - 1], kq_s.at[i - 1], kq_r.at[i - 1], device)
+        copy.start()
+        kv_sends.append(copy)
+    kv_core[0].wait_recv()
+    line_step(6)
+    line_step(7)
+    for copy in kv_sends:
         copy.wait()
-
-    def send(k, carry):
-        big.send(k)
+    got = kv_qr[0].astype(F32) + kv_qr[1].astype(F32) + kv_qr[2].astype(F32) + kv_cr[0].astype(F32)
+    grad_key = dk[:loc, :] + got[:, :HD]
+    grad_value = dv[:loc, :] + got[:, HD:]
+    first, second = grad_key[:, :half], grad_key[:, half:]
+    turned = jnp.concatenate(
+        [first * cos[...] + second * sin[...], second * cos[...] - first * sin[...]], axis=1
+    )
+    grad, gain_buf[0, 5:6, :HD] = norm_grad(k_pre[...], gk[...], turned)
+    feat_q = dh.shape[2] - HD
+    for j in range(2):
+        dh[j, :, feat_q : feat_q + half] = grad[:, j * half : (j + 1) * half].astype(BF)
+        dh[j, :, feat_q + half :] = grad_value[:, j * half : (j + 1) * half].astype(BF)
+
+    inputs = x[...].astype(F32)
+    inverse = lax.rsqrt(jnp.mean(inputs * inputs, axis=1, keepdims=True) + EPS)
+    normed_t = (inputs * inverse * (1.0 + gains[0:1, :])).astype(BF).T
+    ga_t = ga[...].T
+    for j in range(2):
+        for n in range(qkv // TILE):
+            parts[j, :, :, n * TILE : (n + 1) * TILE] = (
+                nn(normed_t, dh[j, :, n * TILE : (n + 1) * TILE]).astype(BF).reshape(4, depth, TILE)
+            )
+        for n in range(feats // TILE):
+            parts[j, :, :, qkv + n * TILE : qkv + (n + 1) * TILE] = (
+                nn(ga_t, heads[:, j * feats + n * TILE : j * feats + (n + 1) * TILE]).astype(BF).reshape(4, depth, TILE)
+            )
+    wanted = ((1 - col, 1 - high, pd), (1 - col, high, px), (col, 1 - high, py), (col, high, None))
+    part_core = [
+        remote(parts.at[c2, 2 * y2 + 1 - core], cr.at[c2, y2], pc_s.at[i], pc_r.at[c2, y2], pc)
+        for i, (c2, y2, _) in enumerate(wanted)
+    ]
+    for copy in part_core:
+        copy.start()
+    grad_normed = nt(dh[0], wa[0, :, :qkv]) + nt(dh[1], wa[1, :, :qkv])
+    grad, gain_buf[0, 0:1, :] = norm_grad(inputs, gains[0:1, :], grad_normed)
+    grad = (grad + g_res[...]).astype(BF)
+    for f in range(8):
+        gt_cut[f] = grad[:, f * cut : (f + 1) * cut]
+    gt_copies = [remote(gt_cut.at[i], gt_out.at[me], gt_s.at[j], gt_r.at[j], d) for j, (i, d) in enumerate(others)]
+    for copy in gt_copies:
+        copy.start()
+    gt_own = pltpu.make_async_copy(gt_cut.at[me], gt_out.at[me], loc_s.at[1])
+    gt_own.start()
+    line_step(8)
+    part_sends = []
+    for i, (c2, y2, device) in enumerate(wanted):
+        part_core[i].wait_recv()
+        if device is None:
+            break
+        summed[i] = (parts[c2, 2 * y2 + core].astype(F32) + cr[c2, y2].astype(F32)).astype(BF)
+        copy = remote(summed.at[i], qr.at[i], pq_s.at[i], pq_r.at[i], device)
+        copy.start()
+        part_sends.append(copy)
+    for i in range(5):
+        if i < len(gain_peers):
+            copy = remote(gain_buf.at[i], gain_in.at[i], gn_s.at[i], gn_r.at[i], gain_peers[i])
+            copy.start()
+        line_step(9 + i)
+        if i < len(gain_peers):
+            copy.wait()
+            gain_buf[i + 1] = gain_buf[i] + gain_in[i]
+    gain_out[...] = gain_buf[len(gain_peers)]
+    for copy in part_sends:
+        copy.wait()
+    total = (
+        parts[col, 2 * high + core].astype(F32)
+        + cr[col, high].astype(F32)
+        + qr[0].astype(F32)
+        + qr[1].astype(F32)
+        + qr[2].astype(F32)
+    ).astype(BF)
+    whole = total.shape[1] // TILE // 2
+    for i in range(2 * whole):
+        mine[hidden_pairs + i // 2, i % 2] = total[:, i * TILE : (i + 1) * TILE]
+    for i in range(2):
+        a_mine[0, i] = total[i * depth // 2 : (i + 1) * depth // 2, 2 * whole * TILE :]
+    for k in range(hidden_pairs, pairs):
+        line.send(k)
+    small.send(0)
+
+    def step(k, carry):
+        line_step(k)
         return carry
 
-    lax.fori_loop(0, count, send, 0)
-    small.send(0)
-    big.add(0)
-    big.add(1)
-    big.total(0)
-
-    def step(k, carry):
-        big.add(k)
-        big.total(k - 1)
-        big.forward(k - 2)
+    lax.fori_loop(14, pairs, step, 0)
+    small.add(0)
+    line.total(pairs - 1)
+    line.forward(pairs - 2)
+    small.total(0)
+    line.forward(pairs - 1)
+    small.forward(0)
+
+    def drain(k, carry):
+        line.drain(k)
         return carry
 
-    lax.fori_loop(2, count, step, 0)
-    small.add(0)
-    big.total(count - 1)
-    big.forward(count - 2)
-    small.total(0)
-    big.forward(count - 1)
-    small.forward(0)
-
-    def drain(k, carry):
-        big.drain(k)
+    lax.fori_loop(0, pairs, drain, 0)
+    small.drain(0)
+
+    def pulled(k, carry):
+        pull(k).wait_send()
         return carry
 
-    lax.fori_loop(0, count, drain, 0)
-    small.drain(0)
-
-
-def line_sum(g, a):
-    count = g.shape[0]
-    shape, small = g.shape[2:], a.shape[2:]
+    lax.fori_loop(0, hidden_pairs, pulled, 0)
+    for copy in lo_copies + gt_copies:
+        copy.wait()
+    lo_own.wait()
+    gt_own.wait()
+    for copy in kv_core + part_core:
+        copy.wait_send()
+
+
+def attention_back(*args):
+    grads, lo, heads, q_pre, kv, wa = args[0], args[1], args[10], args[11], args[14], args[18]
+    hidden_pairs, _, depth, _ = grads.shape
+    loc, width = lo.shape
+    feats = wa.shape[2]
+    pairs = hidden_pairs + feats // TILE // 2
+    keys = kv.shape[0]
+    cut = width // 8
     dma = pltpu.SemaphoreType.DMA
+    piece = (depth, TILE)
+    rest = (depth // 2, feats - 2 * (feats // TILE // 2) * TILE)
+    smem = pl.BlockSpec(memory_space=pltpu.SMEM)
     return pl.pallas_call(
-        line_kernel,
-        out_shape=(jax.ShapeDtypeStruct(g.shape, BF), jax.ShapeDtypeStruct(a.shape, BF)),
-        in_specs=[any_spec()] * 2,
-        out_specs=[any_spec()] * 2,
+        back_kernel,
+        out_shape=(
+            jax.ShapeDtypeStruct((pairs, 2) + piece, BF),
+            jax.ShapeDtypeStruct((1, 2) + rest, BF),
+            jax.ShapeDtypeStruct((8, loc, cut), BF),
+            jax.ShapeDtypeStruct((8, loc, cut), BF),
+            jax.ShapeDtypeStruct((8, width), F32),
+        ),
+        in_specs=[any_spec()] + [vmem_spec()] * (len(args) - 3) + [smem] * 2,
+        out_specs=[any_spec()] * 4 + [vmem_spec()],
         scratch_shapes=[
-            pltpu.VMEM(g.shape, BF), pltpu.VMEM(g.shape, BF), pltpu.VMEM((count,) + shape, BF),
-            pltpu.VMEM(a.shape, BF), pltpu.VMEM(a.shape, BF), pltpu.VMEM((1,) + small, BF),
-            dma((2,)),
-        ] + line_sems(count) + line_sems(1),
+            pltpu.VMEM((pairs, 2) + piece, BF),
+            pltpu.VMEM((pairs, 2) + piece, BF),
+            pltpu.VMEM((pairs,) + piece, BF),
+            pltpu.VMEM((1, 2) + rest, BF),
+            pltpu.VMEM((1, 2) + rest, BF),
+            pltpu.VMEM((1,) + rest, BF),
+            pltpu.VMEM((keys, loc), F32),
+            pltpu.VMEM((HD, keys), BF),
+            pltpu.VMEM((loc, width), BF),
+            pltpu.VMEM(heads.shape, BF),
+            pltpu.VMEM((keys, HD), F32),
+            pltpu.VMEM((keys, HD), F32),
+            pltpu.VMEM((4, loc, 2 * HD), BF),
+            pltpu.VMEM((4, loc, 2 * HD), BF),
+            pltpu.VMEM((3, loc, 2 * HD), BF),
+            pltpu.VMEM((3, loc, 2 * HD), BF),
+            pltpu.VMEM((2, loc, feats - heads.shape[1] // 2), BF),
+            pltpu.VMEM((loc, width), F32),
+            pltpu.VMEM((2, 4, depth, feats), BF),
+            pltpu.VMEM((2, 2, depth, feats), BF),
+            pltpu.VMEM((3, depth, feats), BF),
+            pltpu.VMEM((3, depth, feats), BF),
+            pltpu.VMEM((8, loc, cut), BF),
+            pltpu.VMEM((8, loc, cut), BF),
+            pltpu.VMEM((6, 8, width), F32),
+            pltpu.VMEM((5, 8, width), F32),
+            dma((hidden_pairs,)), dma((hidden_pairs,)), dma((hidden_pairs,)),
+            dma((4,)), dma((4,)), dma((3,)), dma((3,)),
+            dma((4,)), dma((2, 2)), dma((3,)), dma((3,)),
+            dma((7,)), dma((7,)), dma((7,)), dma((7,)), dma((5,)), dma((5,)), dma((2,)),
+        ] + line_sems(pairs) + line_sems(1),
         compiler_params=params(6),
-        name="line_sum",
-    )(g, a)
-
-
-def swap(values, d_row, d_col):
-    n_row, n_col = lax.axis_size("row"), lax.axis_size("col")
-    pairs = [
-        (i * n_col + j, (i ^ d_row) * n_col + (j ^ d_col))
-        for i in range(n_row)
-        for j in range(n_col)
-    ]
-    return lax.ppermute(values, ("row", "col"), pairs)
-
-
-def all_sum(values):
-    for d_row, d_col in ((1, 0), (0, 1), (2, 0)):
-        values = values + swap(values, d_row, d_col)
-    if lax.axis_size("dp") != 4:
-        return lax.psum(values, "dp")
-    for step in (1, 2):
-        values = values + lax.ppermute(values, "dp", [(i, i ^ step) for i in range(4)])
-    return values
+        name="attention_back",
+    )(*args)
+
+
+def finish_kernel(high, pieces, gate, up, down):
+    gate[...] = pieces[0, 0, 0].astype(F32)
+    up[...] = pieces[1, 0, 0].astype(F32)
+    down[...] = pieces[2, 0, 0].astype(F32).T
+
+
+def finish(pieces, high, hidden):
+    _, tiles, _, depth, _ = pieces.shape
+    return pl.pallas_call(
+        finish_kernel,
+        grid_spec=pltpu.PrefetchScalarGridSpec(
+            num_scalar_prefetch=1,
+            grid=(-(-hidden // TILE),),
+            in_specs=[
+                pl.BlockSpec(
+                    (3, 1, 1, depth, TILE), lambda i, high: (0, i % tiles, (i // tiles + high[0]) % 2, 0, 0)
+                )
+            ],
+            out_specs=[
+                pl.BlockSpec((depth, TILE), lambda i, high: (0, i)),
+                pl.BlockSpec((depth, TILE), lambda i, high: (0, i)),
+                pl.BlockSpec((TILE, depth), lambda i, high: (i, 0)),
+            ],
+        ),
+        out_shape=(
+            jax.ShapeDtypeStruct((depth, hidden), F32),
+            jax.ShapeDtypeStruct((depth, hidden), F32),
+            jax.ShapeDtypeStruct((hidden, depth), F32),
+        ),
+        name="finish",
+    )(high, pieces)
 
 
 def cut_low(values):
@@ -764,12 +990,6 @@
     middle = cut_low(values - high)
     low = cut_low(values - high - middle)
     return jnp.stack([high, middle, low]).astype(BF)
-
-
-def dp_sums(grads, attn):
-    if lax.axis_size("dp") != 4:
-        return lax.psum(grads.astype(F32), "dp"), lax.psum(attn.astype(F32), "dp")
-    return line_sum(grads, attn)
 
 
 def body(
@@ -879,111 +1099,63 @@
         pre_normed.astype(BF), residual, upstream_bf, g_post[None], w_hidden[0], w_hidden[1], w_hidden[2]
     )
 
-    grad_resid, grad_g_pre = norm_back(residual, g_pre, inverse_pre, grad_pre)
-    grad_resid = grad_resid + upstream
-    grad_attn, grad_g_attn = norm_back(attn_out, g_attn, inverse_attn, grad_resid)
-    grad_attn_bf = grad_attn.astype(BF)
-    grad_w_out = tn(grad_attn_bf, head_bf)
-    grad_head_bf = nn(grad_attn_bf, w_out).astype(BF).reshape(local, head_count, HD)
-
-    scores = attention_scores()
-    probs = jnp.exp(scores - log_total)
-    probs_bf = probs.astype(BF)
-    grad_probs = jnp.einsum("thd,sd->hts", grad_head_bf, values_bf, preferred_element_type=F32)
-    grad_values = jnp.einsum("hts,thd->sd", probs_bf, grad_head_bf, preferred_element_type=F32)
-    row_inner = jnp.sum(probs * grad_probs, axis=-1, keepdims=True)
-    grad_scores = (probs * (grad_probs - row_inner)).astype(BF)
-    grad_query = (
-        jnp.einsum("hts,sd->thd", grad_scores, keys_bf, preferred_element_type=F32) * query_scale
-    )
-    grad_keys = jnp.einsum("hts,thd->sd", grad_scores, query_bf, preferred_element_type=F32)
-    grad_kv = kv_sum(
-        jnp.concatenate([grad_keys, grad_values], axis=1).astype(BF).reshape(members, local, 2 * HD)
-    )
-    grad_key, grad_value = grad_kv[:, :HD], grad_kv[:, HD:]
-
-    unused, pull = jax.vjp(
-        lambda rows_in, scales_in: head_norm(rows_in, scales_in, cos_heads, sin_heads),
-        query_pre,
-        gain_query,
-    )
-    grad_query_pre, grad_g_query = pull(grad_query)
-    unused, pull = jax.vjp(
-        lambda rows_in, scales_in: head_norm(rows_in, scales_in, cos_table, sin_table),
+    tiles = hidden_grads.shape[1]
+    summed, attn_rest, layer_cut, token_cut, gain_sums = attention_back(
+        hidden_grads.reshape(3 * tiles, 2, depth, TILE),
+        layer_rows,
+        grad_pre,
+        residual,
+        attn_out,
+        upstream_bf,
+        inputs.astype(BF),
+        gain_rows,
+        gain_query[None],
+        gain_key[None],
+        head_bf,
+        query_pre.reshape(local, head_count * HD),
         key_pre,
-        gain_key,
-    )
-    grad_key_pre, grad_g_key = pull(grad_key)
-    grad_query_bf = grad_query_pre.astype(BF).reshape(local, head_count * HD)
-    grad_key_bf = grad_key_pre.astype(BF)
-    grad_value_bf = grad_value.astype(BF)
-    grad_halves = [
-        jnp.concatenate(
-            [
-                grad_query_bf[:, j * q_half : (j + 1) * q_half],
-                grad_key_bf[:, j * kv_half : (j + 1) * kv_half],
-                grad_value_bf[:, j * kv_half : (j + 1) * kv_half],
-            ],
-            axis=1,
+        query_bf.reshape(local, head_count * HD),
+        kv_all,
+        log_total[:, :, 0],
+        cos_table,
+        sin_table,
+        w_attn,
+        grad_g_post,
+        doc_lengths,
+        block_size,
+    )
+    if lax.axis_size("dp") != 4:
+        summed, attn_rest, gain_sums = (
+            lax.psum(v.astype(F32), "dp") for v in (summed, attn_rest, gain_sums)
         )
-        for j in range(n_col)
-    ]
-    grad_normed = sum(nt(grad_halves[j], w_qkv[j]) for j in range(n_col))
-    grad_in, grad_g_input = norm_back(inputs, g_input, inverse_in, grad_normed)
-
-    out_half = grad_w_out.shape[1] // n_col
-    attn_grads = jnp.stack(
-        [
-            jnp.concatenate(
-                [tn(normed_bf, grad_halves[j]), grad_w_out[:, j * out_half : (j + 1) * out_half]], axis=1
-            ).astype(BF)
-            for j in range(n_col)
-        ]
-    ).reshape(n_col, n_row, depth, -1)
-    attn_mine = attn_sum(attn_grads)
-    feats = attn_mine.shape[1]
-    attn_pair = jnp.stack([attn_mine[:, : feats // 2], attn_mine[:, feats // 2 :]])[None]
-    tiles = hidden_grads.shape[1]
-    hidden_sum, attn_pair = dp_sums(
-        hidden_grads.reshape((3 * tiles, 2, depth, TILE)), attn_pair
-    )
-    attn_mine = jnp.concatenate([attn_pair[0, 0], attn_pair[0, 1]], axis=1).astype(F32)
-    hidden_sum = hidden_sum.reshape(3, tiles, 2, depth, TILE)
-    hidden_sum = jnp.where(high == 0, hidden_sum, hidden_sum[:, :, ::-1])
-    hidden_sum = hidden_sum.transpose(0, 3, 2, 1, 4).reshape(3, depth, 2 * slab)
-    hidden_sum = hidden_sum[:, :, :hidden_half].astype(F32)
-
-    def from_tokens(values):
-        cubes = values.astype(BF).reshape(local, members, cut).transpose(1, 0, 2)
-        return lax.all_to_all(cubes, ("row", "col"), split_axis=0, concat_axis=0, tiled=True).reshape(
-            tok_count, cut
-        )
-
-    grad_tokens = from_tokens(grad_in + grad_resid).astype(F32)
-    layer_out = from_tokens(layer_rows)
-
-    def my_gain(values):
-        return lax.dynamic_slice_in_dim(values, me * cut, cut, 0)
-
-    sums = all_sum(
-        jnp.concatenate([grad_g_input, grad_g_attn, grad_g_pre, grad_g_post[0], grad_g_query, grad_g_key])
-    )
+    grad_gate, grad_up, grad_down = finish(
+        summed[: 3 * tiles].reshape(3, tiles, 2, depth, TILE), high[None], hidden_half
+    )
+    attn_mine = jnp.concatenate(
+        [summed[3 * tiles + i // 2, i % 2] for i in range(2 * (summed.shape[0] - 3 * tiles))]
+        + [attn_rest[0].reshape(depth, -1)],
+        axis=1,
+    ).astype(F32)
+
+    def my_gain(i):
+        return lax.dynamic_slice_in_dim(gain_sums[i], me * cut, cut, 0)
+
     return (
-        layer_out,
-        grad_tokens,
+        layer_cut.reshape(tok_count, cut),
+        token_cut.reshape(tok_count, cut).astype(F32),
         attn_mine[:, :q_half],
         attn_mine[:, q_half : q_half + kv_half],
         attn_mine[:, q_half + kv_half : qkv_half],
         attn_mine[:, qkv_half:].T,
-        hidden_sum[0],
-        hidden_sum[1],
-        hidden_sum[2].T,
-        my_gain(sums[:width]),
-        my_gain(sums[width : 2 * width]),
-        my_gain(sums[2 * width : 3 * width]),
-        my_gain(sums[3 * width : 4 * width]),
-        sums[4 * width : 4 * width + HD],
-        sums[4 * width + HD :],
+        grad_gate,
+        grad_up,
+        grad_down,
+        my_gain(0),
+        my_gain(1),
+        my_gain(2),
+        my_gain(3),
+        gain_sums[4, :HD],
+        gain_sums[5, :HD],
     )
 
 

time: 801 us -> 622 us (0.78)
  Pallas kernels: 573 us -> 530 us
  other arithmetic: 66.9 us -> 24.7 us
  local copies, waits for them, and re-layouts: 91.6 us -> 50.6 us
  matrix products: 34.4 us -> 9.07 us
  starting transfers between devices: 14.4 us -> 0 us
  waiting for transfers between devices: 9.39 us -> 0 us
    pallas_call x1, Pallas kernels: 180 us -> 127 us  [mlp(): pl.pallas_call(mlp_kernel, out_shape=(jax.ShapeDtypeStruct((loc, width),...]
    reshape x4 -> x1, local copies, waits for them, and re-layouts: 23.9 us -> 1.17 us  [body(): head_bf = head_out.astype(BF).reshape(local, head_count * HD)]
    convert_element_type x9 -> x2, other arithmetic: 19 us -> 0.32 us  [the longest x1 0.22 us: body(): token_cut.reshape(tok_count, cut).astype(F32)]
    dot_general x9 -> x3, matrix products: 17.6 us -> 5.34 us  [dot(): lax.dot_general(left, right, (dims, ((), ())), preferred_element_type=F32)]
    dot_general x4 -> x0, matrix products: 11.4 us -> none  [the longest x1 4.95 us: body(): jnp.einsum('thd,sd->hts', grad_head_bf, values_bf, preferred_element_type...]
    pallas_call x3 -> x2, Pallas kernels: 246 us -> 256 us  [the longest x1 245 us: attention_back(): pl.pallas_call(back_kernel, out_shape=(jax.ShapeDtypeStruct((pairs, 2) +...]
    transpose x2 -> x0, other arithmetic: 10.4 us -> none  [the longest x1 9.54 us: body(): hidden_sum = hidden_sum.transpose(0, 3, 2, 1, 4).reshape(3, depth, 2 * slab)]
    slice x6 -> x7, local copies, waits for them, and re-layouts: 0.79 us -> 11.2 us  [the longest x1 6.04 us: body(): summed[:3 * tiles].reshape(3, tiles, 2, depth, TILE)]
  transfers between devices with their start and end apart: 7 -> 0, of which waited for: 4 -> 0; matrix products, arithmetic and copies ran while one was open for 15% -> 0% of each run, Pallas kernels for 31% -> 0%
where the time goes in v2:
time: 622 us; the launch traced here: 617 us
  Pallas kernels  530 us (85%)
  local copies, waits for them, and re-layouts  50.6 us (8%)
  other arithmetic  24.7 us (4%)
  matrix products  9.07 us (1%)
    pallas_call x1, Pallas kernels, attention_back(): pl.pallas_call(back_kernel, out_shape=(jax.ShapeDtypeStruct((pairs, 2) +...  245 us
    pallas_call x1, Pallas kernels, entry(): pl.pallas_call(entry_kernel, out_shape=(jax.ShapeDtypeStruct(tk.shape, BF...  130 us
    pallas_call x1, Pallas kernels, mlp(): pl.pallas_call(mlp_kernel, out_shape=(jax.ShapeDtypeStruct((loc, width),...  127 us
    unnamed x47, local copies, waits for them, and re-layouts  17.9 us
    pallas_call x1, Pallas kernels, kv_gather(): pl.pallas_call(kv_kernel, out_shape=jax.ShapeDtypeStruct((8,) + kv.shape,...  16.8 us

profile of v2, /device:TPU:0, one launch (start us, length us, event | category | flops | bytes accessed | tf_op | source)
XLA Modules:
  0.0 616.9 jit_solution(9920533781466271650)
XLA Ops:
  7.4 2.3 compare_and_fusion
  9.6 2.0 pad_maximum_fusion.2.wa
  12.2 1.2 pad_maximum_fusion.tk
  13.4 2.2 copy.101
  15.6 5.3 fusion.6.wm
  20.9 129.9 %entry.1 = (bf16[8,272,144]{2,1,0:T(8,128)(2,1)}, bf16[8,256,144]{2,1,0:T(8,128)(2,1)}, bf16[2,1152,1280]{2,1,0:T(8,128)(2,1)}, bf16[3,1152,1792]{2,1,0:T(8,128)(2,1)}) custom-call(bf16[8,272,144]{2,1,0:T(8,128)(2,1)} %pad_maximum_fusion.tk, bf16[8,256,144]{2,1,0:T(8,128)(2,1)} %bitcast.115, bf16[288,1280]{1,0:T(8,128)(2,1)} %pad_maximum_fusion.2.wa, ...), custom_call_target="tpu_custom_call" | custom-call | tf_op jit(solution)/shard_map/entry/pallas_call | solution.py:210
  150.8 1.6 copy.111
  152.3 1.1 copy.112.ct
  155.6 1.0 copy.102
  156.6 1.1 copy.103.x
  157.7 2.2 fusion.15
  160.0 2.2 fusion.17
  166.1 1.0 copy.124
  167.2 16.8 %kv_gather.1 = bf16[8,256,512]{2,1,0:T(8,128)(2,1)} custom-call(bf16[256,512]{1,0:T(8,128)(2,1)} %pad_maximum_fusion.4.kv), custom_call_target="tpu_custom_call" | custom-call | tf_op jit(solution)/shard_map/kv_gather/pallas_call | solution.py:259
  184.1 1.9 slice_bitcast_fusion.4
  186.7 1.4 fusion.3
  188.1 1.5 fusion.4
  189.6 2.4 fusion.21
  192.6 1.0 multiply_reduce_fusion.1
  193.6 1.2 copy.122.heads
  195.2 1.0 copy-done
  196.2 1.0 multiply_convert_fusion.pre
  197.2 8.8 %slice_bitcast_fusion = (bf16[1152,1792]{1,0:T(8,128)(2,1)}, bf16[1152,1792]{1,0:T(8,128)(2,1)}, bf16[1152,1792]{1,0:T(8,128)(2,1)}) fusion(bf16[3,1152,1792]{2,1,0:T(8,128)(2,1)} %get-tuple-element.34), kind=kLoop, calls=%fused_computation.12 | loop fusion | bytes 24772608 | tf_op jit(solution)/shard_map/squeeze | solution.py:1099
  206.0 127.0 %feed_forward.1 = (bf16[256,1152]{1,0:T(8,128)(2,1)}, f32[1,1152]{1,0:T(1,128)}, f32[256,1152]{1,0:T(8,128)}, bf16[3,7,2,288,256]{4,3,2,1,0:T(8,128)(2,1)}) custom-call(bf16[256,1152]{1,0:T(8,128)(2,1)} %multiply_convert_fusion.pre, f32[256,1152]{1,0:T(8,128)} %copy-done, bf16[256,1152]{1,0:T(8,128)(2,1)} %copy.112.ct, f32[1,1152]{1,0:T(1,128)} %get-tuple-element.146.gpost, ...), custom_call_target="tpu_custom_call" | custom-call | tf_op jit(solution)/shard_map/feed_forward/pallas_call | solution.py:433
  333.0 244.7 %attention_back.1 = (bf16[23,2,288,256]{3,2,1,0:T(8,128)(2,1)}, bf16[1,2,144,256]{3,2,1,0:T(8,128)(2,1)}, bf16[8,256,144]{2,1,0:T(8,128)(2,1)}, bf16[8,256,144]{2,1,0:T(8,128)(2,1)}, f32[8,1152]{1,0:T(8,128)}) custom-call(bf16[21,2,288,256]{3,2,1,0:T(8,128)(2,1)} %bitcast.112, bf16[256,1152]{1,0:T(8,128)(2,1)} %get-tuple-element.36.lo, ...), custom_call_target="tpu_custom_call" | custom-call | tf_op jit(solution)/shard_map/attention_back/pallas_call | solution.py:903
  577.7 2.1 copy.116
  579.8 1.3 fusion.45
  581.1 0.9 fusion.46
  588.3 6.0 slice.163
  597.2 1.6 copy.117
  598.8 11.8 %finish.1 = (f32[288,3456]{1,0:T(8,128)}, f32[288,3456]{1,0:T(8,128)}, f32[3456,288]{1,0:T(8,128)}) custom-call(s32[1]{0:T(128)} %bitcast.41.high, bf16[3,7,2,288,256]{4,3,2,1,0:T(8,128)(2,1)} %bitcast.103), custom_call_target="tpu_custom_call" | custom-call | tf_op jit(solution)/shard_map/finish/pallas_call | solution.py:959
  610.7 6.0 copy.118
  (125 shorter events, 23.1 us)
Async XLA Ops:
  0.6 11.0 %copy-start.15 = (bf16[2048,144]{0,1:T(8,128)(2,1)S(1)}, bf16[2048,144]{0,1:T(8,128)(2,1)}, u32[]{:S(2)}) copy-start(bf16[2048,144]{0,1:T(8,128)(2,1)} %param.17) | copy-start | bytes 1769476
  12.2 3.4 copy-start.11
  150.8 2.6 copy-start.2
  154.0 1.6 copy-start.16
  162.2 1.1 copy-start.18
  162.4 3.3 copy-start.1
  163.9 2.0 copy-start.12
  163.9 2.0 copy-start.13
  166.0 1.1 copy-start.7
  166.0 1.1 copy-start.9
  184.0 2.3 copy-start.3
  184.0 2.4 copy-start.6
  184.0 2.5 copy-start.8
  184.1 2.7 copy-start.10
  192.6 2.2 copy-start.4
  193.6 3.6 copy-start.5
  195.1 1.0 copy-start
  588.3 6.0 copy-start.17
  595.1 1.9 copy-start.14

commit v3 on v2

v3 whole, which is shorter than its diff:
```python
import math

import jax
import jax.numpy as jnp
from jax import lax
from jax.experimental import pallas as pl
from jax.experimental.pallas import tpu as pltpu
from jax.sharding import PartitionSpec as P

HD = 256
EPS = 1e-06
ROPE_BASE = 1000000.0
GELU_C = 0.7978845608028654
BF = jnp.bfloat16
F32 = jnp.float32
PLANE = ("row", "col")


def dot(left, right, dims):
    return lax.dot_general(left, right, (dims, ((), ())), preferred_element_type=F32)


def nn(left, right):
    return dot(left, right, ((1,), (0,)))


def nt(left, right):
    return dot(left, right, ((1,), (1,)))


def tn(left, right):
    return dot(left, right, ((0,), (0,)))


MESH = pl.DeviceIdType.MESH
TILE = 256
KV_SLOTS = (0, 1, 4, 5)
LEAD = 4
VMEM_LIMIT = 64 * 1024 * 1024 - 512 * 1024


def whereabouts():
    place, row, col = lax.axis_index("dp"), lax.axis_index("row"), lax.axis_index("col")
    return place, row, col, row // 2, row % 2


def peers():
    place, row, col, high, core = whereabouts()
    far = row + 2 - 4 * high
    return (
        (place, row, 1 - col),
        (place, far, col),
        (place, far, 1 - col),
        (place, row + 1 - 2 * core, col),
    )


def remote(src, dst, send, recv, device):
    return pltpu.make_async_remote_copy(
        src_ref=src, dst_ref=dst, send_sem=send, recv_sem=recv, device_id=device, device_id_type=MESH
    )


def greet(devices):
    barrier = pltpu.get_barrier_semaphore()
    for device in devices:
        pl.semaphore_signal(barrier, inc=1, device_id=device, device_id_type=MESH)
    pl.semaphore_wait(barrier, len(devices))


def any_spec():
    return pl.BlockSpec(memory_space=pl.ANY)


def vmem_spec():
    return pl.BlockSpec(memory_space=pltpu.VMEM)


def params(number):
    return pltpu.CompilerParams(
        collective_id=number, has_side_effects=True, vmem_limit_bytes=VMEM_LIMIT
    )


def token_places(lengths, span, tokens):
    inverse = 1.0 / jnp.full((1, 1), span[0], jnp.int32).astype(F32)
    document = jnp.zeros_like(tokens)
    first = jnp.zeros_like(tokens)
    end = jnp.int32(0)
    for i in range(lengths.shape[1]):
        end = end + lengths[0, i]
        past = tokens >= end
        document = jnp.where(past, i + 1, document)
        first = jnp.where(past, end, first)
    position = (tokens - first).astype(F32)
    return document, jnp.floor((position + 0.5) * inverse), position


def mask_bias(lengths, span, bias, me, slots):
    local = bias.shape[1]
    query_doc, query_block, _ = token_places(
        lengths, span, me * local + lax.broadcasted_iota(jnp.int32, (1, local), 1)
    )
    for s, owner in enumerate(slots):
        key_doc, key_block, _ = token_places(
            lengths, span, owner * local + lax.broadcasted_iota(jnp.int32, (local, 1), 0)
        )
        seen = (key_doc == query_doc) & (key_block <= query_block)
        bias[s * local : (s + 1) * local, :] = jnp.where(seen, 0.0, -1e30).astype(BF)


def slot_owners():
    place, row, col, high, core = whereabouts()
    owners = []
    for s in range(8):
        r2 = (high + s // 4) % 2 * 2 + (core + s // 2) % 2
        owners.append(2 * r2 + (col + s) % 2)
    return owners


def sent_to_all(index):
    place, row, col, high, core = whereabouts()
    others = []
    for s in range(1, 8):
        r2, c2 = (high + s // 4) % 2 * 2 + (core + s // 2) % 2, (col + s) % 2
        others.append((2 * r2 + c2, (place, r2, c2)))
    return others


def head_forward(values, scales, cos, sin):
    half = values.shape[1] // 2
    inverse = lax.rsqrt(jnp.mean(values * values, axis=1, keepdims=True) + EPS)
    scaled = values * inverse * (1.0 + scales)
    first, second = scaled[:, :half], scaled[:, half:]
    return jnp.concatenate([first * cos - second * sin, second * cos + first * sin], axis=1)


def front_kernel(
    tok, ct, gain_block, wq, wk, wv, wo, wg, wu, wd, gq, gk, lengths, span,
    wm_out, wa_out, kv_out, bias_out, x_out, ct_out, gains, q_pre, k_pre, lse, cos, sin, heads, ao, res, pre,
    wm, wa, tok_all, ct_all, gain_all, q_out, kv, v_t, bias, probs,
    wm_l, wa_l, tk_s, tk_r, ct_s, ct_r, gn_s, gn_r, wa_s, wa_r, wb_s, wb_r, wy_s, wy_r, wu_s, wd_s, wz_r, wc_s, wc_r, wo_s, wo_r, kv_s, kv_r, loc_s,
):
    place, row, col, high, core = whereabouts()
    me = 2 * row + col
    px, py, pd, pc = peers()
    others = sent_to_all(me)
    depth, hidden = wg.shape
    slab = wm_out.shape[2]
    cut = tok.shape[0]
    loc = x_out.shape[0]
    head_count = heads.shape[1] // HD
    half = HD // 2
    members = len(others) + 1
    share = lax.axis_size("dp") == 4
    far_row = row + 2 - 4 * high
    friends = [device for _, device in others]
    if share:
        friends += [((place + i) % 4, row, col) for i in range(1, 4)]

    loads = [
        pltpu.make_async_copy(src, wm.at[m, :, pl.ds(0, hidden)], wm_l.at[m]) for m, src in enumerate((wg, wu, wd))
    ]
    rows = pl.ds(row * depth, depth)
    far_rows = pl.ds(far_row * depth, depth)
    spots, at = [], 0
    for src in (wq, wk, wv, wo):
        spots.append(pl.ds(at, src.shape[1]))
        at += src.shape[1]
    qkv = at - wo.shape[1]
    own = [
        pltpu.make_async_copy(src, wa.at[col, rows, spot], wa_l.at[i])
        for i, (src, spot) in enumerate(zip((wq, wk, wv, wo), spots))
    ]
    tok_own = pltpu.make_async_copy(
        tok.at[:, pl.ds(pl.multiple_of(me * loc, 128), loc)], tok_all.at[pl.ds(me * cut, cut)], loc_s.at[0]
    )
    ct_own = pltpu.make_async_copy(
        ct.at[:, pl.ds(pl.multiple_of(me * loc, 128), loc)], ct_all.at[pl.ds(me * cut, cut)], loc_s.at[1]
    )
    gain_own = pltpu.make_async_copy(gain_block, gain_all.at[me], loc_s.at[2])
    for copy in [tok_own, gain_own] + own + [ct_own] + loads:
        copy.start()
    greet(friends)

    def scatter(src, dst, send, recv):
        copies = [
            remote(
                src.at[:, pl.ds(pl.multiple_of(index * loc, 128), loc)],
                dst.at[pl.ds(me * cut, cut)],
                send.at[j],
                recv.at[j],
                device,
            )
            for j, (index, device) in enumerate(others)
        ]
        for copy in copies:
            copy.start()
        return copies

    tok_copies = scatter(tok, tok_all, tk_s, tk_r)
    gain_copies = [
        remote(gain_block, gain_all.at[me], gn_s.at[j], gn_r.at[j], device) for j, (_, device) in enumerate(others)
    ]
    for copy in gain_copies:
        copy.start()
    attn_copies = {}

    def hand_out(which):
        for i in ((0, 1, 2), (3,))[which]:
            for j, device in enumerate((px, py, pd, pc)):
                attn_copies[i, j] = remote(
                    (wq, wk, wv, wo)[i], wa.at[col, rows, spots[i]], wa_s.at[i, j], wa_r.at[i, j], device
                )
                attn_copies[i, j].start()

    hand_out(0)

    for copy in loads:
        copy.wait()
    for m in range(3):
        wm[m, :, hidden:] = jnp.zeros((depth, 2 * slab - hidden), BF)
    mine = pl.ds(pl.multiple_of(high * slab, 128), slab)
    away = pl.ds(pl.multiple_of((1 - high) * slab, 128), slab)
    unit = depth // 6
    groups, rounds = 18, 4

    def group(start, g):
        return g // 6, pl.ds(pl.multiple_of(start + g % 6 * unit, 16), unit)

    def over(g):
        m, at = group(0, g)
        return remote(wm.at[m, at, away], wm_out.at[group(row * depth, g)], wy_s.at[g], wy_r.at[g], py)

    def along(g, step):
        spot = wm_out.at[group(far_row * depth, g)]
        return remote(spot, spot, (wu_s if step > 0 else wd_s).at[g], wz_r.at[g], ((place + step) % 4, row, col))

    def between(g):
        spot = wm_out.at[group(far_row * depth, g)]
        return remote(spot, spot, wc_s.at[g], wc_r.at[g], pc)

    own_hidden = [pltpu.make_async_copy(wm.at[m, :, mine], wm_out.at[m, rows], wm_l.at[m]) for m in range(3)]
    beside = [remote(wm.at[m, :, mine], wm_out.at[m, rows], wo_s.at[m], wo_r.at[m], pc) for m in range(3)]
    extra = 16 + place % 2
    for m in range(3):
        own_hidden[m].start()
        beside[m].start()
    fetched = [rounds * r + place for r in range(rounds)] + [extra] if share else list(range(groups))
    for g in fetched:
        over(g).start()

    def travel(distance, act_up, act_down):
        for r in range(rounds):
            if distance == 0:
                g = rounds * r + place
                pl.when(place < 3)(lambda g=g: act_up(g))
                pl.when(place > 0)(lambda g=g: act_down(g))
            else:
                below, above = rounds * r + place - distance, rounds * r + place + distance
                pl.when(jnp.logical_and(place >= distance, place < 3))(lambda g=below: act_up(g))
                pl.when(jnp.logical_and(place + distance <= 3, place > 0))(lambda g=above: act_down(g))

    def arrive(distance):
        if not share:
            if distance == 0:
                for g in fetched:
                    over(g).wait_recv()
                    between(g).start()
            return
        if distance == 0:
            for g in fetched:
                over(g).wait_recv()
                between(g).start()
            step = 1 - 2 * (place % 2)
            pl.when(step > 0)(lambda: along(extra, 1).start())
            pl.when(step < 0)(lambda: along(extra, -1).start())
        else:
            for r in range(rounds):
                for g, there in (
                    (rounds * r + place - distance, place >= distance),
                    (rounds * r + place + distance, place + distance <= 3),
                ):

                    @pl.when(there)
                    def _(g=g):
                        along(g, 1).wait_recv()
                        between(g).start()

        travel(distance, lambda g: along(g, 1).start(), lambda g: along(g, -1).start())

    def arrived():
        if share:
            other = 33 - extra
            along(other, 1).wait_recv()
            between(other).start()
            pl.when(place % 2 == 0)(lambda: along(extra, 1).wait_send())
            pl.when(place % 2 == 1)(lambda: along(extra, -1).wait_send())
            for distance in range(4):
                travel(distance, lambda g: along(g, 1).wait_send(), lambda g: along(g, -1).wait_send())
        for g in fetched:
            over(g).wait_send()
        for g in range(groups):
            between(g).wait()
        for m in range(3):
            beside[m].wait()
            own_hidden[m].wait()

    doc, _, position = token_places(lengths, span, me * loc + lax.broadcasted_iota(jnp.int32, (loc, 1), 0))
    steps = lax.broadcasted_iota(jnp.int32, (1, half), 1).astype(F32)
    phases = position * jnp.exp(steps * (-2.0 * math.log(ROPE_BASE) / HD))
    cos[...] = jnp.cos(phases)
    sin[...] = jnp.sin(phases)
    mask_bias(lengths, span, bias, me, slot_owners())
    bias_copy = pltpu.make_async_copy(bias, bias_out, loc_s.at[3])
    bias_copy.start()

    tok_own.wait()
    gain_own.wait()
    for copy in tok_copies + gain_copies:
        copy.wait_recv()
    for f in range(members):
        gains[:, f * cut : (f + 1) * cut] = gain_all[f]
    x_out[...] = tok_all[...].T
    inputs = x_out[...].astype(F32)
    inverse = lax.rsqrt(jnp.mean(inputs * inputs, axis=1, keepdims=True) + EPS)
    normed = (inputs * inverse * (1.0 + gains[0:1, :])).astype(BF)

    corners = ((row, 1 - col), (far_row, col), (far_row, 1 - col))
    part_spots = (pl.ds(0, qkv), pl.ds(qkv, wo.shape[1]))
    passed = {}

    def pass_on(which):
        for j, (r2, c2) in enumerate(corners):
            for i in ((0, 1, 2), (3,))[which]:
                attn_copies[i, j].wait_recv()
            slot = wa.at[c2, pl.ds(r2 * depth, depth), part_spots[which]]
            passed[which, j] = remote(slot, slot, wb_s.at[which, j], wb_r.at[which, j], pc)
            passed[which, j].start()

    def settled(which):
        for i in ((0, 1, 2), (3,))[which]:
            own[i].wait()
            attn_copies[i, 3].wait_recv()
        for j in range(3):
            passed[which, j].wait_recv()

    pass_on(0)
    settled(0)
    q_half, kv_half = wq.shape[1], wk.shape[1]
    for j in range(2):
        found = nn(normed, wa[j, :, :qkv])
        q_pre[:, j * q_half : (j + 1) * q_half] = found[:, :q_half]
        k_pre[:, j * kv_half : (j + 1) * kv_half] = found[:, q_half : q_half + kv_half]
        kv[:loc, HD + j * kv_half : HD + (j + 1) * kv_half] = found[:, q_half + kv_half :].astype(BF)
    kv[:loc, :HD] = head_forward(k_pre[...], gk[...], cos[...], sin[...]).astype(BF)
    kv_first = [
        remote(kv.at[pl.ds(0, loc)], kv.at[pl.ds(slot * loc, loc)], kv_s.at[i], kv_r.at[i], device)
        for i, (slot, device) in enumerate(((1, px), (4, py), (5, pd), (2, pc)))
    ]
    for copy in kv_first:
        copy.start()
    hand_out(1)
    ct_copies = scatter(ct, ct_all, ct_s, ct_r)
    for h in range(head_count):
        cols = slice(h * HD, (h + 1) * HD)
        q_out[:, cols] = (head_forward(q_pre[:, cols], gq[...], cos[...], sin[...]) * (1.0 / math.sqrt(HD))).astype(BF)
    lse[...] = jnp.zeros_like(lse)
    arrive(0)

    def slot_scores(slot):
        keys = slice(slot * loc, (slot + 1) * loc)
        v_t[:, keys] = kv[keys, HD:].T
        for h in range(head_count):
            grown = jnp.exp(nt(kv[keys, :HD], q_out[:, h * HD : (h + 1) * HD]) + bias[keys, :].astype(F32))
            probs[h, keys, :] = grown
            lse[h : h + 1, :] += jnp.sum(grown, axis=0, keepdims=True)

    slot_scores(0)
    kv_relay = []
    for i, slot in enumerate((1, 4, 5)):
        kv_first[i].wait_recv()
        keys = pl.ds(slot * loc, loc)
        copy = remote(kv.at[keys], kv.at[pl.ds((slot + 2) * loc, loc)], kv_s.at[4 + i], kv_r.at[4 + i], pc)
        copy.start()
        kv_relay.append(copy)
        slot_scores(slot)
        if i == 0:
            kv_first[3].wait_recv()
            slot_scores(2)
    arrive(1)
    for i, slot in enumerate((3, 6, 7)):
        kv_relay[i].wait_recv()
        slot_scores(slot)
    kv_copy = pltpu.make_async_copy(kv, kv_out, loc_s.at[4])
    kv_copy.start()
    arrive(2)
    pass_on(1)
    for h in range(head_count):
        inverse = 1.0 / lse[h : h + 1, :]
        total = nn(v_t[...], (probs[h] * inverse).astype(BF))
        heads[:, h * HD : (h + 1) * HD] = total.T.astype(BF)
    lse[...] = jnp.log(lse[...])
    settled(1)
    wa_copy = pltpu.make_async_copy(wa, wa_out, loc_s.at[5])
    wa_copy.start()
    feats = wo.shape[1]
    ao[...] = nt(heads[:, :feats], wa[0, :, qkv:]) + nt(heads[:, feats:], wa[1, :, qkv:])

    def norm_rows(values, scales):
        inverse = lax.rsqrt(jnp.mean(values * values, axis=1, keepdims=True) + EPS)
        return values * inverse * (1.0 + scales)

    res[...] = inputs + norm_rows(ao[...], gains[1:2, :])
    pre[...] = norm_rows(res[...], gains[2:3, :]).astype(BF)
    ct_own.wait()
    for copy in ct_copies:
        copy.wait_recv()
    ct_out[...] = ct_all[...].T
    arrive(3)
    arrived()
    for copy in tok_copies + gain_copies + ct_copies + kv_first:
        copy.wait_send()
    for copy in kv_relay + list(passed.values()) + list(attn_copies.values()):
        copy.wait_send()
    bias_copy.wait()
    kv_copy.wait()
    wa_copy.wait()


def attention_front(*args):
    tok, _, gain_block, wq, wk, wv, wo, wg = args[:8]
    cut, tok_count = tok.shape
    members = 8
    width, loc = cut * members, tok_count // members
    depth, hidden = wg.shape
    slab = -(-hidden // (2 * TILE)) * TILE
    feats = wq.shape[1] + wk.shape[1] + wv.shape[1] + wo.shape[1]
    q_width = 2 * wq.shape[1]
    dma = pltpu.SemaphoreType.DMA
    struct = jax.ShapeDtypeStruct
    smem = pl.BlockSpec(memory_space=pltpu.SMEM)
    return pl.pallas_call(
        front_kernel,
        out_shape=(
            struct((3, width, slab), BF),
            struct((2, width, feats), BF),
            struct((tok_count, 2 * HD), BF),
            struct((tok_count, loc), BF),
            struct((loc, width), BF),
            struct((loc, width), BF),
            struct((8, width), F32),
            struct((loc, q_width), F32),
            struct((loc, HD), F32),
            struct((q_width // HD, loc), F32),
            struct((loc, HD // 2), F32),
            struct((loc, HD // 2), F32),
            struct((loc, q_width), BF),
            struct((loc, width), F32),
            struct((loc, width), F32),
            struct((loc, width), BF),
        ),
        in_specs=[any_spec()] * 10 + [vmem_spec()] * 2 + [smem] * 2,
        out_specs=[any_spec()] * 4 + [vmem_spec()] * 12,
        scratch_shapes=[
            pltpu.VMEM((3, depth, 2 * slab), BF),
            pltpu.VMEM((2, width, feats), BF),
            pltpu.VMEM((width, loc), BF),
            pltpu.VMEM((width, loc), BF),
            pltpu.VMEM((members,) + gain_block.shape, F32),
            pltpu.VMEM((loc, q_width), BF),
            pltpu.VMEM((tok_count, 2 * HD), BF),
            pltpu.VMEM((HD, tok_count), BF),
            pltpu.VMEM((tok_count, loc), BF),
            pltpu.VMEM((q_width // HD, tok_count, loc), F32),
            dma((3,)), dma((4,)), dma((7,)), dma((7,)), dma((7,)), dma((7,)), dma((7,)), dma((7,)),
            dma((4, 4)), dma((4, 4)), dma((2, 3)), dma((2, 3)), dma((18,)), dma((18,)), dma((18,)), dma((18,)),
            dma((18,)), dma((18,)), dma((18,)), dma((3,)), dma((3,)), dma((7,)), dma((7,)), dma((6,)),
        ],
        compiler_params=params(1),
        name="attention_front",
    )(*args)


def mlp_kernel(
    pre, res, ct, gains, w_h,
    lo, dgpost, dpre, dparts, pre_t_out, gm_t_out, hh_out, bb_out, aa_out,
    wg, wu, wd, pre_all, pre_t, gm_all, gm_t, aa, bb, hh, acc, own, parts, prc,
    w_sem, ag_s, ag_r, rs_s, rs_r, gs_s, gs_r, st_s,
):
    place, row, col, high, core = whereabouts()
    px, py, pd, pc = peers()
    quad = (px, py, pd)
    loc, width = pre.shape
    slab = wg.shape[1]
    tiles = slab // TILE
    stores = []

    def store(src, dst):
        copy = pltpu.make_async_copy(src, dst, st_s.at[len(stores)])
        copy.start()
        stores.append(copy)

    loads = [
        pltpu.make_async_copy(src, dst, w_sem.at[i])
        for i, (src, dst) in enumerate(((w_h.at[0], wg), (w_h.at[1], wu), (w_h.at[2], wd)))
    ]
    for copy in loads:
        copy.start()
    greet((px, py, pd, pc))

    def spread(src, buffer, send, recv):
        copies = [remote(src, buffer.at[i + 1], send.at[i], recv.at[i], p) for i, p in enumerate(quad)]
        for copy in copies:
            copy.start()
        return copies

    def lanes(n):
        return pl.ds(pl.multiple_of(n * TILE, TILE), TILE)

    gathers = spread(pre, pre_all, ag_s, ag_r)
    pre_all[0] = pre[...]
    for copy in loads:
        copy.wait()

    scatters = []
    for j in range(4):
        if j:
            gathers[j - 1].wait_recv()
        acc[...] = jnp.zeros_like(acc)
        rows = pl.ds(j * loc, loc)

        def forward(n, carry, j=j, rows=rows):
            x = pre_all[j]
            gate = nn(x, wg[:, lanes(n)])
            up = nn(x, wu[:, lanes(n)])
            square = gate * gate
            bend = jnp.tanh(GELU_C * gate * (1.0 + 0.044715 * square))
            half = 0.5 * (1.0 + bend)
            gelu = gate * half
            slope = half + 0.5 * gate * (1.0 - bend * bend) * (GELU_C * (1.0 + 0.134145 * square))
            hidden = (gelu * up).astype(BF)
            aa[rows, lanes(n)] = gelu.astype(BF)
            bb[rows, lanes(n)] = (up * slope).astype(BF)
            hh[rows, lanes(n)] = hidden
            acc[...] += nt(hidden, wd[:, lanes(n)])
            return carry

        lax.fori_loop(0, tiles, forward, 0)
        store(hh.at[rows], hh_out.at[rows])
        if j:
            parts[j - 1] = acc[...].astype(BF)
            copy = remote(parts.at[j - 1], prc.at[j - 1], rs_s.at[j - 1], rs_r.at[j - 1], quad[j - 1])
            copy.start()
            scatters.append(copy)
        else:
            own[...] = acc[...]
    for j in range(4):
        pre_t[:, j * loc : (j + 1) * loc] = pre_all[j].T
    store(pre_t, pre_t_out)
    for copy in scatters:
        copy.wait()
    out = own[...] + prc[0].astype(F32) + prc[1].astype(F32) + prc[2].astype(F32)
    scale = 1.0 + gains[3:4, :]
    inverse = lax.rsqrt(jnp.mean(out * out, axis=1, keepdims=True) + EPS)
    lo[...] = (res[...] + out * inverse * scale).astype(BF)
    upstream = ct[...].astype(F32)
    scaled = upstream * scale
    inner = jnp.mean(scaled * out, axis=1, keepdims=True)
    gm_all[0] = (scaled * inverse - out * (inverse * inverse * inverse * inner)).astype(BF)
    dgpost[...] = jnp.sum(upstream * out * inverse, axis=0, keepdims=True)

    gathers2 = spread(gm_all.at[0], gm_all, gs_s, gs_r)
    for j in range(4):
        if j:
            gathers2[j - 1].wait_recv()
        acc[...] = jnp.zeros_like(acc)
        rows = pl.ds(j * loc, loc)

        def backward(n, carry, j=j, rows=rows):
            grad_hidden = nn(gm_all[j], wd[:, lanes(n)])
            grad_gate = (grad_hidden * bb[rows, lanes(n)].astype(F32)).astype(BF)
            grad_up = (grad_hidden * aa[rows, lanes(n)].astype(F32)).astype(BF)
            bb[rows, lanes(n)] = grad_gate
            aa[rows, lanes(n)] = grad_up
            acc[...] += nt(grad_gate, wg[:, lanes(n)]) + nt(grad_up, wu[:, lanes(n)])
            return carry

        lax.fori_loop(0, tiles, backward, 0)
        gm_t[:, j * loc : (j + 1) * loc] = gm_all[j].T
        store(bb.at[rows], bb_out.at[rows])
        store(aa.at[rows], aa_out.at[rows])
        if j:
            dparts[j - 1] = acc[...].astype(BF)
        else:
            dpre[...] = acc[...]
    store(gm_t, gm_t_out)
    for copy in stores:
        copy.wait()
    for copy in gathers + gathers2:
        copy.wait_send()


def mlp(pre, res, ct, gains, weights):
    loc, width = pre.shape
    slab = weights.shape[2]
    dma = pltpu.SemaphoreType.DMA
    struct = jax.ShapeDtypeStruct
    return pl.pallas_call(
        mlp_kernel,
        out_shape=(
            struct((loc, width), BF),
            struct((1, width), F32),
            struct((loc, width), F32),
            struct((3, loc, width), BF),
            struct((width, 4 * loc), BF),
            struct((width, 4 * loc), BF),
            struct((4 * loc, slab), BF),
            struct((4 * loc, slab), BF),
            struct((4 * loc, slab), BF),
        ),
        in_specs=[vmem_spec()] * 4 + [any_spec()],
        out_specs=[vmem_spec()] * 4 + [any_spec()] * 5,
        scratch_shapes=[
            pltpu.VMEM((width, slab), BF),
            pltpu.VMEM((width, slab), BF),
            pltpu.VMEM((width, slab), BF),
            pltpu.VMEM((4, loc, width), BF),
            pltpu.VMEM((width, 4 * loc), BF),
            pltpu.VMEM((4, loc, width), BF),
            pltpu.VMEM((width, 4 * loc), BF),
            pltpu.VMEM((4 * loc, slab), BF),
            pltpu.VMEM((4 * loc, slab), BF),
            pltpu.VMEM((4 * loc, slab), BF),
            pltpu.VMEM((loc, width), F32),
            pltpu.VMEM((loc, width), F32),
            pltpu.VMEM((3, loc, width), BF),
            pltpu.VMEM((3, loc, width), BF),
            dma((3,)),
            dma((3,)), dma((3,)), dma((3,)), dma((3,)), dma((3,)), dma((3,)), dma((14,)),
        ],
        compiler_params=params(3),
        name="feed_forward",
    )(pre, res, ct, gains, weights)


class Line:
    def __init__(self, mine, inbox, middle, turned, out, sems, turns):
        self.mine, self.inbox, self.middle, self.turned, self.out = mine, inbox, middle, turned, out
        self.in_s, self.in_r, self.mid_s, self.mid_r, self.x_s, self.x_r, self.o_s, self.o_r, self.l_s, self.y_s, self.y_r = sems
        place, row, col, high, core = whereabouts()
        self.turns = turns
        self.end = (place % 3) == 0
        self.inner = (jnp.where(place == 0, 1, 2), row, col)
        self.outer = ((place - 1) * 3 % 6, row, col)
        self.across = (3 - place, row, col)
        self.beside = (place, row + 2 - 4 * high, col)
        self.place = place

    def root(self, k):
        return (k + self.place + 1) % 2

    def inward(self, k, h):
        return remote(self.mine.at[k, h], self.inbox.at[k, h], self.in_s.at[k, h], self.in_r.at[k, h], self.inner)

    def partial(self, k):
        return remote(
            self.mine.at[k, 1 - self.root(k)], self.middle.at[k], self.mid_s.at[k], self.mid_r.at[k], self.across
        )

    def turn(self, k):
        return remote(self.mine.at[k, 1], self.turned.at[k], self.y_s.at[k], self.y_r.at[k], self.beside)

    def exchange(self, k, h, source):
        return remote(source, self.out.at[k, h], self.x_s.at[k], self.x_r.at[k], self.across)

    def outward(self, k, h, source):
        return remote(source, self.out.at[k, h], self.o_s.at[k, h], self.o_r.at[k, h], self.outer)

    def keep(self, k, h, source):
        return pltpu.make_async_copy(source, self.out.at[k, h], self.l_s.at[k])

    def inside(self, act):
        pl.when(jnp.logical_not(self.end))(act)

    def turns_here(self, k):
        return jnp.logical_and(k < self.turns, self.root(k) == 1)

    def send(self, k):
        @pl.when(self.end)
        def _():
            for h in range(2):
                self.inward(k, h).start()

    def sent(self, k):
        @pl.when(self.end)
        def _():
            for h in range(2):
                self.inward(k, h).wait_send()

    def add(self, k):
        def act():
            other = 1 - self.root(k)
            self.inward(k, other).wait_recv()
            self.mine[k, other] = (
                self.mine[k, other].astype(F32) + self.inbox[k, other].astype(F32)
            ).astype(BF)
            self.partial(k).start()

        self.inside(act)

    def share(self, k, h, source):
        self.outward(k, h, source).start()
        self.exchange(k, h, source).start()
        self.keep(k, h, source).start()

    def total(self, k):
        def act():
            root = self.root(k)
            self.inward(k, root).wait_recv()
            self.partial(k).wait_recv()
            self.mine[k, root] = (
                self.mine[k, root].astype(F32) + self.inbox[k, root].astype(F32) + self.middle[k].astype(F32)
            ).astype(BF)

            if isinstance(k, int) and k >= self.turns:
                self.share(k, root, self.mine.at[k, root])
                return

            @pl.when(self.turns_here(k))
            def _():
                self.turn(k).start()

            @pl.when(jnp.logical_not(self.turns_here(k)))
            def _():
                self.share(k, root, self.mine.at[k, root])

        self.inside(act)

    def spread(self, k):
        @pl.when(jnp.logical_and(jnp.logical_not(self.end), self.turns_here(k)))
        def _():
            self.turn(k).wait_recv()
            self.share(k, 1, self.turned.at[k])

    def forward(self, k):
        def act():
            other = 1 - self.root(k)
            source = self.out.at[k, other]
            self.exchange(k, other, self.mine.at[k, other]).wait_recv()
            self.outward(k, other, source).start()

        self.inside(act)

    def drain(self, k):
        @pl.when(self.end)
        def _():
            for h in range(2):
                self.outward(k, h, self.mine.at[k, h]).wait_recv()

        def act():
            root = self.root(k)
            self.partial(k).wait_send()
            self.exchange(k, root, self.mine.at[k, root]).wait_send()
            self.keep(k, root, self.mine.at[k, root]).wait()
            for h in range(2):
                self.outward(k, h, self.mine.at[k, h]).wait_send()

            if not isinstance(k, int):
                pl.when(self.turns_here(k))(lambda: self.turn(k).wait_send())

        self.inside(act)


class Alone:
    def __init__(self, mine, inbox, middle, turned, out, sems, turns):
        self.mine, self.out, self.turns = mine, out, turns
        self.l_s, self.y_s, self.y_r = sems[0], sems[9], sems[10]
        place, row, col, high, core = whereabouts()
        self.beside = (place, row + 2 - 4 * high, col)

    def send(self, k):
        pass

    def sent(self, k):
        pass

    def add(self, k):
        pass

    def spread(self, k):
        pass

    def forward(self, k):
        pass

    def copy(self, k, h):
        return pltpu.make_async_copy(self.mine.at[k, h], self.out.at[k, h], self.l_s.at[k, h])

    def turn(self, k):
        return remote(self.mine.at[k, 1], self.out.at[k, 1], self.y_s.at[k], self.y_r.at[k], self.beside)

    def total(self, k):
        self.copy(k, 0).start()
        if isinstance(k, int):
            (self.turn(k) if k < self.turns else self.copy(k, 1)).start()
        else:
            pl.when(k < self.turns)(lambda: self.turn(k).start())
            pl.when(k >= self.turns)(lambda: self.copy(k, 1).start())

    def drain(self, k):
        self.copy(k, 0).wait()
        if isinstance(k, int):
            (self.turn(k) if k < self.turns else self.copy(k, 1)).wait()
        else:
            pl.when(k < self.turns)(lambda: self.turn(k).wait())
            pl.when(k >= self.turns)(lambda: self.copy(k, 1).wait())


def line_sems(count):
    dma = pltpu.SemaphoreType.DMA
    return [
        dma((count, 2)), dma((count, 2)), dma((count,)), dma((count,)), dma((count,)), dma((count,)),
        dma((count, 2)), dma((count, 2)), dma((count,)), dma((count,)), dma((count,)),
    ]


EARLY, AHEAD = 5, 3


def back_kernel(
    dparts, pre_t_h, gm_t_h, hh_h, bb_h, aa_h, own_h, lo_h, ao_h, ct_h, x_h, heads_h, q_pre_h, k_pre_h, kv_h,
    bias_h, wa_h, gains, gq, gk, lse, cos, sin, dgpost,
    g_out, a_out, lo_out, gt_out, gain_out,
    mine, inbox, middle, turned, a_mine, a_in, a_mid, parts, cr, summed, qr, rsr, lefts, ring, halves,
    own, ga, ao, ct, x, heads, q_pre, k_pre, kv, bias,
    k_t, gh, dk, dv, kv_cr, kv_qr, dh, cut_t, gain_buf, gain_in,
    in_s, t_s, big_s, wa_l, rs_s, rs_r, c_s, c_r, kc_s, kc_r, kq_s, kq_r, pc_s, pc_r, pq_s, pq_r,
    lo_s, lo_r, gt_s, gt_r, gn_s, gn_r, loc_s, *line_refs,
):
    place, row, col, high, core = whereabouts()
    me = 2 * row + col
    px, py, pd, pc = peers()
    quad = (px, py, pd)
    others = sent_to_all(me)
    on_line = lax.axis_size("dp") == 4
    make = Line if on_line else Alone
    hidden_pairs = turned.shape[0]
    line = make(mine, inbox, middle, turned, g_out, line_refs[:11], hidden_pairs)
    small = make(a_mine, a_in, a_mid, turned, a_out, line_refs[11:], 0)
    tiles = hidden_pairs // 3
    pairs = mine.shape[0]
    loc, width = x.shape
    depth = mine.shape[2]
    cut = width // 8
    all_tok = pre_t_h.shape[1]
    head_count = q_pre.shape[1] // HD
    half = HD // 2
    out_half = heads.shape[1] // 2
    feats = parts.shape[2]
    qkv = feats - out_half

    big = [
        pltpu.make_async_copy(src, lefts.at[i], big_s.at[i]) for i, src in enumerate((pre_t_h, gm_t_h))
    ]
    sources = (bb_h, aa_h, hh_h)

    def lanes(index):
        return pl.ds(pl.multiple_of(index * TILE, TILE), TILE)

    def load(n, m):
        return pltpu.make_async_copy(sources[m].at[:, lanes(n)], ring.at[m], t_s.at[m])

    for m in range(3):
        load(0, m).start()
        if m < 2:
            big[m].start()
    whole_wa = pltpu.make_async_copy(wa_h, parts, wa_l)
    smalls = [
        pltpu.make_async_copy(src, dst, in_s.at[i])
        for i, (src, dst) in enumerate(
            (
                (lo_h, ga), (own_h, own), (ao_h, ao), (ct_h, ct), (heads_h, heads),
                (kv_h, kv), (bias_h, bias), (q_pre_h, q_pre), (k_pre_h, k_pre), (x_h, x),
            )
        )
    ]
    for copy in smalls + [whole_wa]:
        copy.start()
    friends = [device for _, device in others]
    if on_line:
        friends += [((place + i) % 4, row, col) for i in range(1, 4)]
    greet(friends)
    scatters = [remote(dparts.at[i], rsr.at[i], rs_s.at[i], rs_r.at[i], device) for i, device in enumerate(quad)]
    for copy in scatters:
        copy.start()

    def to_core(k, m):
        return (
            remote(halves.at[m, 2 * high + 1 - core], mine.at[k, 0], c_s.at[m, 0], c_r.at[k, 0], pc),
            remote(halves.at[m, 3 - 2 * high - core], mine.at[k, 1], c_s.at[m, 1], c_r.at[k, 1], pc),
        )

    def produce(n):
        for m in range(3):
            load(n, m).wait()

        def one(m, carry):
            product = nn(lefts[m // 2], ring[m]).astype(BF)
            for b in range(4):
                halves[m, b] = product[b * depth : (b + 1) * depth]
            for copy in to_core(3 * n + m, m):
                copy.start()
            return carry

        lax.fori_loop(0, 3, one, 0)
        if n + 1 < tiles:
            for m in range(3):
                load(n + 1, m).start()

    def settle(n):
        def one(m, carry):
            k = 3 * n + m
            for copy in to_core(k, m):
                copy.wait()
            mine[k, 0] = (mine[k, 0].astype(F32) + halves[m, 2 * high + core].astype(F32)).astype(BF)
            mine[k, 1] = (mine[k, 1].astype(F32) + halves[m, 2 - 2 * high + core].astype(F32)).astype(BF)
            return carry

        lax.fori_loop(0, 3, one, 0)

    def line_step(k):
        line.sent(k)
        if isinstance(k, int):
            if k + AHEAD <= hidden_pairs:
                line.send(k + AHEAD)
        else:
            pl.when(k + AHEAD < pairs)(lambda: line.send(k + AHEAD))
        line.add(k)
        if not isinstance(k, int) or k >= 1:
            line.total(k - 1)
        if not isinstance(k, int) or k >= 2:
            line.spread(k - 2)
        if not isinstance(k, int) or k >= 3:
            line.forward(k - 3)

    for copy in big:
        copy.wait()
    produce(0)
    for n in range(1, EARLY):
        settle(n - 1)
        for i in range(3 * n - 3, min(3 * n, AHEAD)):
            line.send(i)
        produce(n)
        if n >= EARLY - 2:
            line_step(n + 2 - EARLY)

    here = pl.ds(pl.multiple_of(me * loc, 128), loc)

    def give(src, dst, send, recv, local):
        copies = [
            remote(src.at[pl.ds(i * cut, cut)], dst.at[:, here], send.at[j], recv.at[j], d)
            for j, (i, d) in enumerate(others)
        ]
        for copy in copies:
            copy.start()
        stays = pltpu.make_async_copy(src.at[pl.ds(me * cut, cut)], dst.at[:, here], local)
        stays.start()
        return copies, stays

    def norm_grad(values, scales, upstream):
        inverse = lax.rsqrt(jnp.mean(values * values, axis=1, keepdims=True) + EPS)
        scaled = upstream * (1.0 + scales)
        inner = jnp.mean(scaled * values, axis=1, keepdims=True)
        grad = scaled * inverse - values * (inverse * inverse * inverse * inner)
        return grad, jnp.sum(upstream * values * inverse, axis=0, keepdims=True)

    smalls[0].wait()
    cut_t[...] = ga[...].T
    lo_copies, lo_own = give(cut_t, lo_out, lo_s, lo_r, loc_s.at[0])
    gain_buf[...] = jnp.zeros_like(gain_buf)
    for copy in smalls[1:] + [whole_wa]:
        copy.wait()
    k_t[...] = kv[:, :HD].T
    settle(EARLY - 1)
    produce(EARLY)
    line_step(2)
    for copy in scatters:
        copy.wait()
    grad_pre = own[...] + rsr[0].astype(F32) + rsr[1].astype(F32) + rsr[2].astype(F32)
    inverse = lax.rsqrt(jnp.mean(ao[...] * ao[...], axis=1, keepdims=True) + EPS)
    residual = x[...].astype(F32) + ao[...] * inverse * (1.0 + gains[1:2, :])
    grad, gain_buf[0, 2:3, :] = norm_grad(residual, gains[2:3, :], grad_pre)
    own[...] = grad + ct[...].astype(F32)
    grad, gain_buf[0, 1:2, :] = norm_grad(ao[...], gains[1:2, :], own[...])
    ga[...] = grad.astype(BF)
    gain_buf[0, 3:4, :] = dgpost[...]
    for j in range(2):
        gh[:, j * out_half : (j + 1) * out_half] = nn(ga[...], parts[j, :, qkv:]).astype(BF)
    line_step(3)

    wanted = ((1 - col, 1 - high, pd), (1 - col, high, px), (col, 1 - high, py), (col, high, None))

    def block(ref, index, columns):
        return ref.at[pl.ds(pl.multiple_of(index * depth, 16), depth), columns]

    class PlaneSum:
        def __init__(self, which, start, size):
            self.columns = pl.ds(start, size)
            self.core = [
                remote(
                    block(parts.at[c2], 2 * y2 + 1 - core, self.columns),
                    block(cr, 2 * c2 + y2, self.columns),
                    pc_s.at[which, i],
                    pc_r.at[which, 2 * c2 + y2],
                    pc,
                )
                for i, (c2, y2, _) in enumerate(wanted)
            ]
            self.sends = [
                remote(block(summed, i, self.columns), qr.at[i, :, self.columns], pq_s.at[which, i], pq_r.at[which, i], d)
                for i, (_, _, d) in enumerate(wanted[:3])
            ]

        def begin(self):
            for copy in self.core:
                copy.start()

        def added(self, i):
            c2, y2, _ = wanted[i]
            self.core[i].wait_recv()
            return block(parts.at[c2], 2 * y2 + core, self.columns)[...].astype(F32) + block(
                cr, 2 * c2 + y2, self.columns
            )[...].astype(F32)

        def spread(self):
            for i in range(3):
                block(summed, i, self.columns)[...] = self.added(i).astype(BF)
                self.sends[i].start()

        def result(self):
            total = self.added(3)
            for i in range(3):
                self.sends[i].wait()
                total = total + qr[i, :, self.columns].astype(F32)
            for copy in self.core:
                copy.wait_send()
            return total.astype(BF)

    ga_t = ga[...].T
    for j in range(2):
        for n in range(out_half // TILE):
            parts[j, :, qkv + n * TILE : qkv + (n + 1) * TILE] = nn(
                ga_t, heads[:, j * out_half + n * TILE : j * out_half + (n + 1) * TILE]
            ).astype(BF)
    out_sum = PlaneSum(0, qkv, out_half)
    out_sum.begin()
    line_step(4)

    step_keys = 512
    for h in range(head_count):
        cols = slice(h * HD, (h + 1) * HD)
        query = head_forward(q_pre[:, cols], gq[...], cos[...], sin[...]) * (1.0 / math.sqrt(HD))
        query, grad_head = query.astype(BF), gh[:, cols]
        delta = jnp.sum((grad_head.astype(F32) * heads[:, cols].astype(F32)).T, axis=0, keepdims=True)

        def keys(c, total, h=h, query=query, grad_head=grad_head, delta=delta):
            rows = pl.ds(pl.multiple_of(c * step_keys, step_keys), step_keys)
            scores = nt(kv[rows, :HD], query) + bias[rows, :].astype(F32)
            probs = jnp.exp(scores - lse[h : h + 1, :])
            grad_probs = nt(kv[rows, HD:], grad_head)
            grad_scores = (probs * (grad_probs - delta)).astype(BF)
            add_v = nn(probs.astype(BF), grad_head)
            add_k = nn(grad_scores, query)
            if h:
                dv[rows, :] += add_v
                dk[rows, :] += add_k
            else:
                dv[rows, :] = add_v
                dk[rows, :] = add_k
            return total + nn(k_t[:, rows], grad_scores)

        total = lax.fori_loop(0, kv.shape[0] // step_keys, keys, jnp.zeros((HD, loc), F32))
        grad_query = total.T * (1.0 / math.sqrt(HD))
        first, second = grad_query[:, :half], grad_query[:, half:]
        turned = jnp.concatenate(
            [first * cos[...] + second * sin[...], second * cos[...] - first * sin[...]], axis=1
        )
        grad, gain = norm_grad(q_pre[:, cols], gq[...], turned)
        gain_buf[0, 4:5, :HD] += gain
        dh[h // 2, :, (h % 2) * HD : (h % 2 + 1) * HD] = grad.astype(BF)
        if h == 0:
            out_sum.spread()
        if h % 2:
            line_step(3 + 2 * (h // 2 + 1))
            line_step(4 + 2 * (h // 2 + 1))

    stage = [rsr.at[i // 2, :, pl.ds(i % 2 * 2 * HD, 2 * HD)] for i in range(4)]
    for i, slot in enumerate(KV_SLOTS):
        rows = slice((slot + 2) * loc, (slot + 3) * loc)
        stage[i][:, :HD] = dk[rows, :].astype(BF)
        stage[i][:, HD:] = dv[rows, :].astype(BF)
    kv_core = [remote(stage[i], kv_cr.at[i], kc_s.at[i], kc_r.at[i], pc) for i in range(4)]
    for copy in kv_core:
        copy.start()
    kv_sums = (ct.at[:, pl.ds(0, 2 * HD)], ct.at[:, pl.ds(2 * HD, 2 * HD)], rsr.at[2, :, pl.ds(0, 2 * HD)])
    kv_sends = []
    for i, device in ((3, pd), (1, px), (2, py)):
        kv_core[i].wait_recv()
        rows = slice(KV_SLOTS[i] * loc, (KV_SLOTS[i] + 1) * loc)
        kv_sums[i - 1][:, :HD] = (dk[rows, :] + kv_cr[i, :, :HD].astype(F32)).astype(BF)
        kv_sums[i - 1][:, HD:] = (dv[rows, :] + kv_cr[i, :, HD:].astype(F32)).astype(BF)
        copy = remote(kv_sums[i - 1], kv_qr.at[i - 1], kq_s.at[i - 1], kq_r.at[i - 1], device)
        copy.start()
        kv_sends.append(copy)
    kv_core[0].wait_recv()
    settle(EARLY)
    produce(EARLY + 1)
    line_step(9)
    line_step(10)
    total = out_sum.result()
    for i in range(2):
        mine[hidden_pairs, i] = total[:, i * TILE : (i + 1) * TILE]
    for copy in kv_sends:
        copy.wait()
    got = kv_qr[0].astype(F32) + kv_qr[1].astype(F32) + kv_qr[2].astype(F32) + kv_cr[0].astype(F32)
    grad_key = dk[:loc, :] + got[:, :HD]
    grad_value = dv[:loc, :] + got[:, HD:]
    first, second = grad_key[:, :half], grad_key[:, half:]
    turned = jnp.concatenate(
        [first * cos[...] + second * sin[...], second * cos[...] - first * sin[...]], axis=1
    )
    grad, gain_buf[0, 5:6, :HD] = norm_grad(k_pre[...], gk[...], turned)
    feat_q = dh.shape[2] - HD
    for j in range(2):
        dh[j, :, feat_q : feat_q + half] = grad[:, j * half : (j + 1) * half].astype(BF)
        dh[j, :, feat_q + half :] = grad_value[:, j * half : (j + 1) * half].astype(BF)

    inputs = x[...].astype(F32)
    inverse = lax.rsqrt(jnp.mean(inputs * inputs, axis=1, keepdims=True) + EPS)
    normed_t = (inputs * inverse * (1.0 + gains[0:1, :])).astype(BF).T
    grad_normed = nt(dh[0], parts[0, :, :qkv]) + nt(dh[1], parts[1, :, :qkv])
    for j in range(2):
        for n in range(qkv // TILE):
            parts[j, :, n * TILE : (n + 1) * TILE] = nn(normed_t, dh[j, :, n * TILE : (n + 1) * TILE]).astype(BF)
    in_sum = PlaneSum(1, 0, qkv)
    in_sum.begin()
    grad, gain_buf[0, 0:1, :] = norm_grad(inputs, gains[0:1, :], grad_normed)
    in_sum.spread()
    for copy in lo_copies:
        copy.wait_send()
    lo_own.wait()
    cut_t[...] = (grad + own[...]).astype(BF).T
    gt_copies, gt_own = give(cut_t, gt_out, gt_s, gt_r, loc_s.at[1])
    settle(EARLY + 1)
    line_step(11)
    gain_copies = [
        remote(gain_buf.at[0], gain_in.at[j], gn_s.at[j], gn_r.at[j], d) for j, (_, d) in enumerate(others)
    ]
    for copy in gain_copies:
        copy.start()
    for i in range(12, 16):
        line_step(i)
    total = in_sum.result()
    for i in range(2):
        mine[hidden_pairs + 1, i] = total[:, i * TILE : (i + 1) * TILE]
        a_mine[0, i] = total[i * depth // 2 : (i + 1) * depth // 2, 2 * TILE :]
    for copy in gain_copies:
        copy.wait()
    gain_buf[1] = gain_buf[0] + sum(gain_in[j] for j in range(7))
    gain_copies = [
        remote(gain_buf.at[1], gain_in.at[7 + i], gn_s.at[7 + i], gn_r.at[7 + i], ((place + i + 1) % 4, row, col))
        for i in range(3 if on_line else 0)
    ]
    for copy in gain_copies:
        copy.start()

    def step(k, carry):
        line_step(k)
        pl.when(k == pairs - 1 - AHEAD)(lambda: small.send(0))
        return carry

    lax.fori_loop(16, pairs, step, 0)
    small.sent(0)
    small.add(0)
    line.total(pairs - 1)
    line.forward(pairs - 3)
    small.total(0)
    line.forward(pairs - 2)
    line.forward(pairs - 1)
    small.forward(0)

    def drain(k, carry):
        line.drain(k)
        return carry

    lax.fori_loop(0, pairs, drain, 0)
    small.drain(0)
    for copy in gain_copies:
        copy.wait()
    gain_out[...] = gain_buf[1]
    for i in range(len(gain_copies)):
        gain_out[...] += gain_in[7 + i]
    for copy in lo_copies:
        copy.wait_recv()
    for copy in gt_copies:
        copy.wait()
    gt_own.wait()
    for copy in kv_core:
        copy.wait_send()


def attention_back(*args):
    dparts, pre_t, hh, lo, heads, q_pre, kv, bias, wa = (args[i] for i in (0, 1, 3, 7, 11, 12, 14, 15, 16))
    loc, width = lo.shape
    depth, feats = width // 4, wa.shape[2]
    hidden_pairs = 3 * hh.shape[1] // TILE
    pairs = hidden_pairs + 2
    keys = kv.shape[0]
    cut = width // 8
    dma = pltpu.SemaphoreType.DMA
    piece = (depth, TILE)
    rest = (depth // 2, TILE)
    struct = jax.ShapeDtypeStruct
    vmem = pltpu.VMEM
    return pl.pallas_call(
        back_kernel,
        out_shape=(
            struct((pairs, 2) + piece, BF),
            struct((1, 2) + rest, BF),
            struct((cut, keys), BF),
            struct((cut, keys), BF),
            struct((8, width), F32),
        ),
        in_specs=[any_spec()] * 17 + [vmem_spec()] * 7,
        out_specs=[any_spec()] * 4 + [vmem_spec()],
        scratch_shapes=[
            vmem((pairs, 2) + piece, BF),
            vmem((pairs, 2) + piece, BF),
            vmem((pairs,) + piece, BF),
            vmem((hidden_pairs,) + piece, BF),
            vmem((1, 2) + rest, BF),
            vmem((1, 2) + rest, BF),
            vmem((1,) + rest, BF),
            vmem((2, width, feats), BF),
            vmem((width, feats), BF),
            vmem((3 * depth, feats), BF),
            vmem((3, depth, feats), BF),
            vmem(dparts.shape, BF),
            vmem((2,) + pre_t.shape, BF),
            vmem((3, pre_t.shape[1], TILE), BF),
            vmem((3, 4) + piece, BF),
        ]
        + [vmem(args[i].shape, args[i].dtype) for i in (6, 7, 8, 9, 10, 11, 12, 13, 14, 15)]
        + [
            vmem((HD, keys), BF),
            vmem(heads.shape, BF),
            vmem((keys, HD), F32),
            vmem((keys, HD), F32),
            vmem((4, loc, 2 * HD), BF),
            vmem((3, loc, 2 * HD), BF),
            vmem((2, loc, feats - heads.shape[1] // 2), BF),
            vmem((width, loc), BF),
            vmem((2, 8, width), F32),
            vmem((10, 8, width), F32),
            dma((12,)), dma((3,)), dma((2,)), dma(()), dma((3,)), dma((3,)), dma((3, 2)), dma((hidden_pairs, 2)),
            dma((4,)), dma((4,)), dma((3,)), dma((3,)),
            dma((2, 4)), dma((2, 4)), dma((2, 3)), dma((2, 3)),
            dma((7,)), dma((7,)), dma((7,)), dma((7,)), dma((10,)), dma((10,)), dma((2,)),
        ]
        + line_sems(pairs)
        + line_sems(1),
        compiler_params=params(6),
        name="attention_back",
    )(*args)


def finish_kernel(high, gate_in, up_in, down_in, gate, up, down):
    gate[...] = gate_in[0, 0].astype(F32)
    up[...] = up_in[0, 0].astype(F32)
    down[...] = down_in[0, 0].astype(F32)


def finish(pieces, high, hidden, tiles):
    depth = pieces.shape[2]

    def source(m):
        return pl.BlockSpec(
            (1, 1, depth, TILE), lambda i, high: (3 * (i % tiles) + m, (i // tiles + high[0]) % 2, 0, 0)
        )

    return pl.pallas_call(
        finish_kernel,
        grid_spec=pltpu.PrefetchScalarGridSpec(
            num_scalar_prefetch=1,
            grid=(-(-hidden // TILE),),
            in_specs=[source(m) for m in range(3)],
            out_specs=[pl.BlockSpec((depth, TILE), lambda i, high: (0, i))] * 3,
        ),
        out_shape=[jax.ShapeDtypeStruct((depth, hidden), F32)] * 3,
        name="finish",
    )(high, pieces, pieces, pieces)


def body(
    tokens,
    cotangent,
    weight_query,
    weight_key,
    weight_value,
    weight_out,
    weight_gate,
    weight_up,
    weight_down,
    gain_input,
    gain_attn,
    gain_pre,
    gain_post,
    gain_query,
    gain_key,
    doc_lengths,
    block_size,
):
    cut = tokens.shape[1]
    row, col = lax.axis_index("row"), lax.axis_index("col")
    me = row * lax.axis_size("col") + col
    depth, hidden_half = weight_gate.shape
    q_half, kv_half = weight_query.shape[1], weight_key.shape[1]
    qkv_half = q_half + 2 * kv_half
    gain_block = jnp.pad(jnp.stack([gain_input, gain_attn, gain_pre, gain_post]), ((0, 4), (0, 0)))
    (
        w_hidden, w_attn, kv_all, bias, inputs, upstream, gains, query_pre, key_pre, log_total,
        cos_table, sin_table, head_bf, attn_out, residual, pre_normed,
    ) = attention_front(
        tokens.T, cotangent.T, gain_block, weight_query, weight_key, weight_value, weight_out.T,
        weight_gate, weight_up, weight_down.T, gain_query[None], gain_key[None], doc_lengths, block_size,
    )
    layer_rows, grad_g_post, grad_own, grad_parts, pre_t, grad_mlp_t, hidden, grad_gate, grad_up = mlp(
        pre_normed, residual, upstream, gains, w_hidden
    )
    tiles = hidden.shape[1] // TILE
    summed, attn_rest, layer_cut, token_cut, gain_sums = attention_back(
        grad_parts, pre_t, grad_mlp_t, hidden, grad_gate, grad_up, grad_own, layer_rows, attn_out, upstream,
        inputs, head_bf, query_pre, key_pre, kv_all, bias, w_attn, gains, gain_query[None], gain_key[None],
        log_total, cos_table, sin_table, grad_g_post,
    )
    if lax.axis_size("dp") != 4:
        summed, attn_rest, gain_sums = (lax.psum(v.astype(F32), "dp") for v in (summed, attn_rest, gain_sums))
    grad_gate, grad_up, grad_down = finish(summed, (row // 2)[None], hidden_half, tiles)
    attn_mine = jnp.concatenate(
        [summed[-1, 0], summed[-1, 1], attn_rest[0].reshape(depth, -1), summed[-2, 0], summed[-2, 1]], axis=1
    ).astype(F32)
    my_gains = lax.dynamic_slice_in_dim(gain_sums[:4], me * cut, cut, 1)
    return (
        layer_cut.T,
        token_cut.T.astype(F32),
        attn_mine[:, :q_half],
        attn_mine[:, q_half : q_half + kv_half],
        attn_mine[:, q_half + kv_half : qkv_half],
        attn_mine[:, qkv_half:].T,
        grad_gate,
        grad_up,
        grad_down.T,
        my_gains[0],
        my_gains[1],
        my_gains[2],
        my_gains[3],
        gain_sums[4, :HD],
        gain_sums[5, :HD],
    )


def solution(mesh):
    in_specs = (
        P("dp", ("row", "col")),
        P("dp", ("row", "col")),
        P("row", "col"),
        P("row", "col"),
        P("row", "col"),
        P("col", "row"),
        P("row", "col"),
        P("row", "col"),
        P("col", "row"),
        P(("row", "col")),
        P(("row", "col")),
        P(("row", "col")),
        P(("row", "col")),
        P(),
        P(),
        P("dp", None),
        P(),
    )
    out_specs = (
        P("dp", ("row", "col")),
        P("dp", ("row", "col")),
        P("row", "col"),
        P("row", "col"),
        P("row", "col"),
        P("col", "row"),
        P("row", "col"),
        P("row", "col"),
        P("col", "row"),
        P(("row", "col")),
        P(("row", "col")),
        P(("row", "col")),
        P(("row", "col")),
        P(),
        P(),
    )
    return jax.shard_map(body, mesh=mesh, in_specs=in_specs, out_specs=out_specs, check_vma=False)
```

time: 622 us -> 481 us (0.77)
  Pallas kernels: 530 us -> 459 us
  local copies, waits for them, and re-layouts: 50.6 us -> 8.26 us
  other arithmetic: 24.7 us -> 2.57 us
  matrix products: 9.07 us -> 0 us
    pallas_call x4 -> x3, Pallas kernels: 518 us -> 448 us  [the longest x1 226 us: attention_back(): pl.pallas_call(back_kernel, out_shape=(struct((pairs, 2) + piece, BF), st...]
    unnamed x47 -> x13, local copies, waits for them, and re-layouts: 17.9 us -> 3.61 us
    squeeze x2 -> x0, local copies, waits for them, and re-layouts: 10.8 us -> none  [the longest x1 8.85 us: body(): w_hidden[2]]
    dot_general x5 -> x0, matrix products: 9.07 us -> none  [the longest x3 5.34 us: dot(): lax.dot_general(left, right, (dims, ((), ())), preferred_element_type=F32)]
    slice x11 -> x2, local copies, waits for them, and re-layouts: 9.24 us -> 0.65 us  [the longest x1 0.65 us: body(): my_gains[3]]
    another operation x6 -> x1, other arithmetic: 8.88 us -> 1.34 us  [body(): jnp.stack([gain_input, gain_attn, gain_pre, gain_post])]
where the time goes in v3:
time: 481 us; the launch traced here: 472 us
  Pallas kernels  459 us (95%)
  local copies, waits for them, and re-layouts  8.26 us (2%)
    pallas_call x1, Pallas kernels, attention_back(): pl.pallas_call(back_kernel, out_shape=(struct((pairs, 2) + piece, BF), st...  226 us
    pallas_call x1, Pallas kernels, attention_front(): pl.pallas_call(front_kernel, out_shape=(struct((3, width, slab), BF), str...  115 us
    pallas_call x1, Pallas kernels, mlp(): pl.pallas_call(mlp_kernel, out_shape=(struct((loc, width), BF), struct((1...  107 us
    pallas_call x1, Pallas kernels, finish(): pl.pallas_call(finish_kernel, grid_spec=pltpu.PrefetchScalarGridSpec(num_...  11.6 us

profile of v3, /device:TPU:0, one launch (start us, length us, event | category | flops | bytes accessed | tf_op | source)
XLA Modules:
  0.0 472.0 jit_solution(6706952179430293417)
XLA Ops:
  0.6 1.3 select_maximum_fusion.gain_block
  2.6 115.1 %attention_front.1 = (bf16[3,1152,1792]{2,1,0:T(8,128)(2,1)}, bf16[2,1152,1280]{2,1,0:T(8,128)(2,1)}, bf16[2048,512]{1,0:T(8,128)(2,1)}, bf16[2048,256]{1,0:T(8,...) custom-call(bf16[144,2048]{1,0:T(8,128)(2,1)} %bitcast.33, ...), custom_call_target="tpu_custom_call" | custom-call | tf_op jit(solution)/shard_map/attention_front/pallas_call | solution.py:443
  117.7 106.9 %feed_forward.1 = (bf16[256,1152]{1,0:T(8,128)(2,1)}, f32[1,1152]{1,0:T(1,128)}, f32[256,1152]{1,0:T(8,128)}, bf16[3,256,1152]{2,1,0:T(8,128)(2,1)}, bf16[1152,1...) custom-call(bf16[256,1152]{1,0:T(8,128)(2,1)} %get-tuple-element.48., ...), custom_call_target="tpu_custom_call" | custom-call | tf_op jit(solution)/shard_map/feed_forward/pallas_call | solution.py:609
  224.6 225.8 %attention_back.1 = (bf16[23,2,288,256]{3,2,1,0:T(8,128)(2,1)}, bf16[1,2,144,256]{3,2,1,0:T(8,128)(2,1)}, bf16[144,2048]{1,0:T(8,128)(2,1)}, bf16[144,2048]{1,0:T(8,128)(2,1)}, f32[8,1152]{1,0:T(8,128)}) custom-call(bf16[3,256,1152]{2,1,0:T(8,128)(2,1)} %get-tuple-element.53.dparts, bf16[1152,1024]{1,0:T(8,128)(2,1)} %get-tuple-element.54.pre_t_h, ...), custom_call_target="tpu_custom_call" | custom-call | tf_op jit(solution)/shard_map/attention_back/pallas_call | solution.py:1226
  450.4 0.0 copy-start.2
  450.4 11.6 %finish.1 = (f32[288,3456]{1,0:T(8,128)}, f32[288,3456]{1,0:T(8,128)}, f32[288,3456]{1,0:T(8,128)}) custom-call(s32[1]{0:T(128)} %bitcast.18.high, bf16[23,2,288,256]{3,2,1,0:T(8,128)(2,1)} %get-tuple-element.75.gate_in.up_in.down_in, bf16[23,2,288,256]{3,2,1,0:T(8,128)(2,1)} %get-tuple-element.75.gate_in.up_in.down_in, ...), custom_call_target="tpu_custom_call" | custom-call | tf_op jit(solution)/shard_map/finish/pallas_call | solution.py:1292
  462.0 0.9 bitcast_dynamic-update-slice_fusion.3
  463.0 0.9 bitcast_dynamic-update-slice_fusion.2
  463.9 0.0 copy-done.2
  463.9 0.9 bitcast_dynamic-update-slice_fusion.1
  464.8 0.9 bitcast_dynamic-update-slice_fusion
  465.8 0.0 copy-start
  465.8 0.1 convert_element_type.13
  465.9 0.0 copy-start.3
  465.9 0.0 copy-start.1
  465.9 0.9 slice_bitcast_fusion
  466.8 0.9 slice.60
  467.7 0.7 fusion
  468.4 0.0 copy-done
  468.4 1.1 convert_bitcast_fusion
  469.5 0.0 copy-done.3
  469.6 0.7 fusion.2
  470.2 0.6 fusion.1
  470.8 0.0 copy-done.1
  470.8 0.8 copy.38
  (2 shorter events, 0.0 us)
Async XLA Ops:
  450.4 13.5 %copy-start.2 = (bf16[1,2,144,256]{3,2,1,0:T(8,128)(2,1)S(1)}, bf16[1,2,144,256]{3,2,1,0:T(8,128)(2,1)}, u32[]{:S(2)}) copy-start(bf16[1,2,144,256]{3,2,1,0:T(8,128)(2,1)} %get-tuple-element.76) | copy-start | bytes 442372
  465.8 2.6 copy-start
  465.9 3.7 copy-start.3
  465.9 4.9 %copy-start.1 = (bf16[144,2048]{1,0:T(8,128)(2,1)S(1)}, bf16[144,2048]{1,0:T(8,128)(2,1)}, u32[]{:S(2)}) copy-start(bf16[144,2048]{1,0:T(8,128)(2,1)} %get-tuple-element.73) | copy-start | bytes 1769476

commit v4 on v3

--- a/solution.py
+++ b/solution.py
@@ -1,3 +1,4 @@
+import functools
 import math
 
 import jax
@@ -250,44 +251,60 @@
     for g in fetched:
         over(g).start()
 
-    def travel(distance, act_up, act_down):
-        for r in range(rounds):
-            if distance == 0:
-                g = rounds * r + place
-                pl.when(place < 3)(lambda g=g: act_up(g))
-                pl.when(place > 0)(lambda g=g: act_down(g))
-            else:
-                below, above = rounds * r + place - distance, rounds * r + place + distance
-                pl.when(jnp.logical_and(place >= distance, place < 3))(lambda g=below: act_up(g))
-                pl.when(jnp.logical_and(place + distance <= 3, place > 0))(lambda g=above: act_down(g))
-
-    def arrive(distance):
-        if not share:
-            if distance == 0:
-                for g in fetched:
-                    over(g).wait_recv()
+    def travel(distance, r, act_up, act_down):
+        if distance == 0:
+            g = rounds * r + place
+            pl.when(place < 3)(lambda: act_up(g))
+            pl.when(place > 0)(lambda: act_down(g))
+        else:
+            below, above = rounds * r + place - distance, rounds * r + place + distance
+            pl.when(jnp.logical_and(place >= distance, place < 3))(lambda: act_up(below))
+            pl.when(jnp.logical_and(place + distance <= 3, place > 0))(lambda: act_down(above))
+
+    def arrive(distance, r):
+        if distance == 0:
+            g = rounds * r + place
+            over(g).wait_recv()
+            between(g).start()
+        else:
+            for g, there in (
+                (rounds * r + place - distance, place >= distance),
+                (rounds * r + place + distance, place + distance <= 3),
+            ):
+
+                @pl.when(there)
+                def _(g=g):
+                    along(g, 1).wait_recv()
                     between(g).start()
-            return
-        if distance == 0:
-            for g in fetched:
-                over(g).wait_recv()
-                between(g).start()
-            step = 1 - 2 * (place % 2)
-            pl.when(step > 0)(lambda: along(extra, 1).start())
-            pl.when(step < 0)(lambda: along(extra, -1).start())
-        else:
-            for r in range(rounds):
-                for g, there in (
-                    (rounds * r + place - distance, place >= distance),
-                    (rounds * r + place + distance, place + distance <= 3),
-                ):
-
-                    @pl.when(there)
-                    def _(g=g):
-                        along(g, 1).wait_recv()
-                        between(g).start()
-
-        travel(distance, lambda g: along(g, 1).start(), lambda g: along(g, -1).start())
+
+        travel(distance, r, lambda g: along(g, 1).start(), lambda g: along(g, -1).start())
+
+    def arrive_extra():
+        over(extra).wait_recv()
+        between(extra).start()
+        pl.when(place % 2 == 0)(lambda: along(extra, 1).start())
+        pl.when(place % 2 == 1)(lambda: along(extra, -1).start())
+
+    def arrive_whole():
+        for g in fetched:
+            over(g).wait_recv()
+            between(g).start()
+
+    if share:
+        events = [
+            functools.partial(arrive, distance, r)
+            for distance, r in (
+                (0, 0), (0, 1), (0, 2), (1, 0), (0, 3), (1, 1), (2, 0), (1, 2), (2, 1), (3, 0), (1, 3), (2, 2), (3, 1),
+                (2, 3), (3, 2), (3, 3),
+            )
+        ]
+        events.insert(7, arrive_extra)
+    else:
+        events = [arrive_whole]
+
+    def poll(count):
+        for _ in range(min(count, len(events))):
+            events.pop(0)()
 
     def arrived():
         if share:
@@ -297,7 +314,8 @@
             pl.when(place % 2 == 0)(lambda: along(extra, 1).wait_send())
             pl.when(place % 2 == 1)(lambda: along(extra, -1).wait_send())
             for distance in range(4):
-                travel(distance, lambda g: along(g, 1).wait_send(), lambda g: along(g, -1).wait_send())
+                for r in range(rounds):
+                    travel(distance, r, lambda g: along(g, 1).wait_send(), lambda g: along(g, -1).wait_send())
         for g in fetched:
             over(g).wait_send()
         for g in range(groups):
@@ -346,7 +364,9 @@
             passed[which, j].wait_recv()
 
     pass_on(0)
+    poll(1)
     settled(0)
+    poll(1)
     q_half, kv_half = wq.shape[1], wk.shape[1]
     for j in range(2):
         found = nn(normed, wa[j, :, :qkv])
@@ -366,7 +386,7 @@
         cols = slice(h * HD, (h + 1) * HD)
         q_out[:, cols] = (head_forward(q_pre[:, cols], gq[...], cos[...], sin[...]) * (1.0 / math.sqrt(HD))).astype(BF)
     lse[...] = jnp.zeros_like(lse)
-    arrive(0)
+    poll(1)
 
     def slot_scores(slot):
         keys = slice(slot * loc, (slot + 1) * loc)
@@ -377,6 +397,7 @@
             lse[h : h + 1, :] += jnp.sum(grown, axis=0, keepdims=True)
 
     slot_scores(0)
+    poll(2)
     kv_relay = []
     for i, slot in enumerate((1, 4, 5)):
         kv_first[i].wait_recv()
@@ -385,22 +406,25 @@
         copy.start()
         kv_relay.append(copy)
         slot_scores(slot)
+        poll(1)
         if i == 0:
             kv_first[3].wait_recv()
             slot_scores(2)
-    arrive(1)
+            poll(1)
     for i, slot in enumerate((3, 6, 7)):
         kv_relay[i].wait_recv()
         slot_scores(slot)
+        poll(1)
     kv_copy = pltpu.make_async_copy(kv, kv_out, loc_s.at[4])
     kv_copy.start()
-    arrive(2)
-    pass_on(1)
     for h in range(head_count):
         inverse = 1.0 / lse[h : h + 1, :]
         total = nn(v_t[...], (probs[h] * inverse).astype(BF))
         heads[:, h * HD : (h + 1) * HD] = total.T.astype(BF)
+        poll(1)
     lse[...] = jnp.log(lse[...])
+    pass_on(1)
+    poll(1)
     settled(1)
     wa_copy = pltpu.make_async_copy(wa, wa_out, loc_s.at[5])
     wa_copy.start()
@@ -417,7 +441,7 @@
     for copy in ct_copies:
         copy.wait_recv()
     ct_out[...] = ct_all[...].T
-    arrive(3)
+    poll(len(events))
     arrived()
     for copy in tok_copies + gain_copies + ct_copies + kv_first:
         copy.wait_send()
@@ -494,12 +518,10 @@
     loc, width = pre.shape
     slab = wg.shape[1]
     tiles = slab // TILE
-    stores = []
-
-    def store(src, dst):
-        copy = pltpu.make_async_copy(src, dst, st_s.at[len(stores)])
-        copy.start()
-        stores.append(copy)
+
+    def store(kind, j, src, dst):
+        rows = chunk_rows(j)
+        return pltpu.make_async_copy(src.at[rows], dst.at[rows], st_s.at[kind, j])
 
     loads = [
         pltpu.make_async_copy(src, dst, w_sem.at[i])
@@ -515,51 +537,62 @@
             copy.start()
         return copies
 
-    def lanes(n):
-        return pl.ds(pl.multiple_of(n * TILE, TILE), TILE)
-
     gathers = spread(pre, pre_all, ag_s, ag_r)
     pre_all[0] = pre[...]
     for copy in loads:
         copy.wait()
 
-    scatters = []
-    for j in range(4):
-        if j:
-            gathers[j - 1].wait_recv()
+    def chunk_rows(j):
+        return pl.ds(pl.multiple_of(j * loc, 256), loc)
+
+    def chunk_device(j):
+        return (place, (row + j // 2 * 2) % 4, (col + j) % 2)
+
+    def give_part(j):
+        return remote(parts.at[j - 1], prc.at[j - 1], rs_s.at[j - 1], rs_r.at[j - 1], chunk_device(j))
+
+    def got_chunk(j, buffer, send, recv):
+        pl.when(j > 0)(lambda: remote(pre, buffer.at[j], send.at[j - 1], recv.at[j - 1], chunk_device(j)).wait_recv())
+
+    def forward(j, carry):
+        got_chunk(j, pre_all, ag_s, ag_r)
         acc[...] = jnp.zeros_like(acc)
-        rows = pl.ds(j * loc, loc)
-
-        def forward(n, carry, j=j, rows=rows):
+        rows = chunk_rows(j)
+        for n in range(tiles):
+            at = slice(n * TILE, (n + 1) * TILE)
             x = pre_all[j]
-            gate = nn(x, wg[:, lanes(n)])
-            up = nn(x, wu[:, lanes(n)])
+            gate = nn(x, wg[:, at])
+            up = nn(x, wu[:, at])
             square = gate * gate
             bend = jnp.tanh(GELU_C * gate * (1.0 + 0.044715 * square))
             half = 0.5 * (1.0 + bend)
             gelu = gate * half
             slope = half + 0.5 * gate * (1.0 - bend * bend) * (GELU_C * (1.0 + 0.134145 * square))
             hidden = (gelu * up).astype(BF)
-            aa[rows, lanes(n)] = gelu.astype(BF)
-            bb[rows, lanes(n)] = (up * slope).astype(BF)
-            hh[rows, lanes(n)] = hidden
-            acc[...] += nt(hidden, wd[:, lanes(n)])
-            return carry
-
-        lax.fori_loop(0, tiles, forward, 0)
-        store(hh.at[rows], hh_out.at[rows])
-        if j:
+            aa[rows, at] = gelu.astype(BF)
+            bb[rows, at] = (up * slope).astype(BF)
+            hh[rows, at] = hidden
+            acc[...] += nt(hidden, wd[:, at])
+        store(0, j, hh, hh_out).start()
+
+        @pl.when(j == 0)
+        def _():
+            own[...] = acc[...]
+
+        @pl.when(j > 0)
+        def _():
             parts[j - 1] = acc[...].astype(BF)
-            copy = remote(parts.at[j - 1], prc.at[j - 1], rs_s.at[j - 1], rs_r.at[j - 1], quad[j - 1])
-            copy.start()
-            scatters.append(copy)
-        else:
-            own[...] = acc[...]
+            give_part(j).start()
+
+        return carry
+
+    lax.fori_loop(0, 4, forward, 0)
     for j in range(4):
         pre_t[:, j * loc : (j + 1) * loc] = pre_all[j].T
-    store(pre_t, pre_t_out)
-    for copy in scatters:
-        copy.wait()
+    pre_copy = pltpu.make_async_copy(pre_t, pre_t_out, st_s.at[3, 0])
+    pre_copy.start()
+    for j in range(1, 4):
+        give_part(j).wait()
     out = own[...] + prc[0].astype(F32) + prc[1].astype(F32) + prc[2].astype(F32)
     scale = 1.0 + gains[3:4, :]
     inverse = lax.rsqrt(jnp.mean(out * out, axis=1, keepdims=True) + EPS)
@@ -571,32 +604,41 @@
     dgpost[...] = jnp.sum(upstream * out * inverse, axis=0, keepdims=True)
 
     gathers2 = spread(gm_all.at[0], gm_all, gs_s, gs_r)
+    def backward(j, carry):
+        got_chunk(j, gm_all, gs_s, gs_r)
+        acc[...] = jnp.zeros_like(acc)
+        rows = chunk_rows(j)
+        for n in range(tiles):
+            at = slice(n * TILE, (n + 1) * TILE)
+            grad_hidden = nn(gm_all[j], wd[:, at])
+            grad_gate = (grad_hidden * bb[rows, at].astype(F32)).astype(BF)
+            grad_up = (grad_hidden * aa[rows, at].astype(F32)).astype(BF)
+            bb[rows, at] = grad_gate
+            aa[rows, at] = grad_up
+            acc[...] += nt(grad_gate, wg[:, at]) + nt(grad_up, wu[:, at])
+        gm_t[:, rows] = gm_all[j].T
+        store(1, j, bb, bb_out).start()
+        store(2, j, aa, aa_out).start()
+
+        @pl.when(j == 0)
+        def _():
+            dpre[...] = acc[...]
+
+        @pl.when(j > 0)
+        def _():
+            dparts[j - 1] = acc[...].astype(BF)
+
+        return carry
+
+    lax.fori_loop(0, 4, backward, 0)
+    gm_copy = pltpu.make_async_copy(gm_t, gm_t_out, st_s.at[3, 1])
+    gm_copy.start()
     for j in range(4):
-        if j:
-            gathers2[j - 1].wait_recv()
-        acc[...] = jnp.zeros_like(acc)
-        rows = pl.ds(j * loc, loc)
-
-        def backward(n, carry, j=j, rows=rows):
-            grad_hidden = nn(gm_all[j], wd[:, lanes(n)])
-            grad_gate = (grad_hidden * bb[rows, lanes(n)].astype(F32)).astype(BF)
-            grad_up = (grad_hidden * aa[rows, lanes(n)].astype(F32)).astype(BF)
-            bb[rows, lanes(n)] = grad_gate
-            aa[rows, lanes(n)] = grad_up
-            acc[...] += nt(grad_gate, wg[:, lanes(n)]) + nt(grad_up, wu[:, lanes(n)])
-            return carry
-
-        lax.fori_loop(0, tiles, backward, 0)
-        gm_t[:, j * loc : (j + 1) * loc] = gm_all[j].T
-        store(bb.at[rows], bb_out.at[rows])
-        store(aa.at[rows], aa_out.at[rows])
-        if j:
-            dparts[j - 1] = acc[...].astype(BF)
-        else:
-            dpre[...] = acc[...]
-    store(gm_t, gm_t_out)
-    for copy in stores:
-        copy.wait()
+        store(0, j, hh, hh_out).wait()
+        store(1, j, bb, bb_out).wait()
+        store(2, j, aa, aa_out).wait()
+    pre_copy.wait()
+    gm_copy.wait()
     for copy in gathers + gathers2:
         copy.wait_send()
 
@@ -637,7 +679,7 @@
             pltpu.VMEM((3, loc, width), BF),
             pltpu.VMEM((3, loc, width), BF),
             dma((3,)),
-            dma((3,)), dma((3,)), dma((3,)), dma((3,)), dma((3,)), dma((3,)), dma((14,)),
+            dma((3,)), dma((3,)), dma((3,)), dma((3,)), dma((3,)), dma((3,)), dma((4, 4)),
         ],
         compiler_params=params(3),
         name="feed_forward",
@@ -669,16 +711,19 @@
         )
 
     def turn(self, k):
-        return remote(self.mine.at[k, 1], self.turned.at[k], self.y_s.at[k], self.y_r.at[k], self.beside)
+        return remote(self.mine.at[k, 1], self.turned.at[k // 2], self.y_s.at[k], self.y_r.at[k], self.beside)
+
+    def spot(self, k, h):
+        return self.out(k, h) if isinstance(k, int) else self.mine.at[k, h]
 
     def exchange(self, k, h, source):
-        return remote(source, self.out.at[k, h], self.x_s.at[k], self.x_r.at[k], self.across)
+        return remote(source, self.spot(k, h), self.x_s.at[k], self.x_r.at[k], self.across)
 
     def outward(self, k, h, source):
-        return remote(source, self.out.at[k, h], self.o_s.at[k, h], self.o_r.at[k, h], self.outer)
+        return remote(source, self.spot(k, h), self.o_s.at[k, h], self.o_r.at[k, h], self.outer)
 
     def keep(self, k, h, source):
-        return pltpu.make_async_copy(source, self.out.at[k, h], self.l_s.at[k])
+        return pltpu.make_async_copy(source, self.spot(k, h), self.l_s.at[k])
 
     def inside(self, act):
         pl.when(jnp.logical_not(self.end))(act)
@@ -741,16 +786,20 @@
         @pl.when(jnp.logical_and(jnp.logical_not(self.end), self.turns_here(k)))
         def _():
             self.turn(k).wait_recv()
-            self.share(k, 1, self.turned.at[k])
-
-    def forward(self, k):
+            self.share(k, 1, self.turned.at[k // 2])
+
+    def forward(self, k, late):
         def act():
             other = 1 - self.root(k)
-            source = self.out.at[k, other]
+            source = self.out(k, other)
             self.exchange(k, other, self.mine.at[k, other]).wait_recv()
             self.outward(k, other, source).start()
 
-        self.inside(act)
+        if k >= self.turns:
+            if not late:
+                self.inside(act)
+        else:
+            pl.when(jnp.logical_and(jnp.logical_not(self.end), self.root(k) == (0 if late else 1)))(act)
 
     def drain(self, k):
         @pl.when(self.end)
@@ -791,14 +840,16 @@
     def spread(self, k):
         pass
 
-    def forward(self, k):
+    def forward(self, k, late):
         pass
 
     def copy(self, k, h):
-        return pltpu.make_async_copy(self.mine.at[k, h], self.out.at[k, h], self.l_s.at[k, h])
+        spot = self.out(k, h) if isinstance(k, int) else self.mine.at[k, h]
+        return pltpu.make_async_copy(self.mine.at[k, h], spot, self.l_s.at[k, h])
 
     def turn(self, k):
-        return remote(self.mine.at[k, 1], self.out.at[k, 1], self.y_s.at[k], self.y_r.at[k], self.beside)
+        spot = self.out(k, 0) if isinstance(k, int) else self.mine.at[k, 1]
+        return remote(self.mine.at[k, 1], spot, self.y_s.at[k], self.y_r.at[k], self.beside)
 
     def total(self, k):
         self.copy(k, 0).start()
@@ -825,13 +876,13 @@
     ]
 
 
-EARLY, AHEAD = 5, 3
+EARLY, AHEAD, SPREAD, LATE = 5, 3, 4, 6
 
 
 def back_kernel(
     dparts, pre_t_h, gm_t_h, hh_h, bb_h, aa_h, own_h, lo_h, ao_h, ct_h, x_h, heads_h, q_pre_h, k_pre_h, kv_h,
     bias_h, wa_h, gains, gq, gk, lse, cos, sin, dgpost,
-    g_out, a_out, lo_out, gt_out, gain_out,
+    gate_out, up_out, down_out, a_out, lo_out, gt_out, gain_out,
     mine, inbox, middle, turned, a_mine, a_in, a_mid, parts, cr, summed, qr, rsr, lefts, ring, halves,
     own, ga, ao, ct, x, heads, q_pre, k_pre, kv, bias,
     k_t, gh, dk, dv, kv_cr, kv_qr, dh, cut_t, gain_buf, gain_in,
@@ -845,9 +896,20 @@
     others = sent_to_all(me)
     on_line = lax.axis_size("dp") == 4
     make = Line if on_line else Alone
-    hidden_pairs = turned.shape[0]
-    line = make(mine, inbox, middle, turned, g_out, line_refs[:11], hidden_pairs)
-    small = make(a_mine, a_in, a_mid, turned, a_out, line_refs[11:], 0)
+    hidden_pairs = mine.shape[0] - 2
+    slab = gate_out.shape[1] // 2
+
+    def place_of(k, h):
+        if k >= hidden_pairs:
+            return a_out.at[:, pl.ds((0 if k > hidden_pairs else qkv) + h * TILE, TILE)]
+        start = (high + h) % 2 * slab + k // 3 * TILE
+        return (gate_out, up_out, down_out)[k % 3].at[:, pl.ds(pl.multiple_of(start, TILE), TILE)]
+
+    def place_of_small(k, h):
+        return a_out.at[pl.ds(h * (depth // 2), depth // 2), pl.ds(qkv - TILE, TILE)]
+
+    line = make(mine, inbox, middle, turned, place_of, line_refs[:11], hidden_pairs)
+    small = make(a_mine, a_in, a_mid, turned, place_of_small, line_refs[11:], 0)
     tiles = hidden_pairs // 3
     pairs = mine.shape[0]
     loc, width = x.shape
@@ -929,20 +991,26 @@
 
         lax.fori_loop(0, 3, one, 0)
 
-    def line_step(k):
-        line.sent(k)
-        if isinstance(k, int):
-            if k + AHEAD <= hidden_pairs:
-                line.send(k + AHEAD)
-        else:
-            pl.when(k + AHEAD < pairs)(lambda: line.send(k + AHEAD))
-        line.add(k)
-        if not isinstance(k, int) or k >= 1:
-            line.total(k - 1)
-        if not isinstance(k, int) or k >= 2:
-            line.spread(k - 2)
-        if not isinstance(k, int) or k >= 3:
-            line.forward(k - 3)
+    order = list(range(14)) + [hidden_pairs] + list(range(14, 18)) + [hidden_pairs + 1] + list(range(18, hidden_pairs))
+
+    def line_rest(p):
+        if 0 <= p - 1 < pairs:
+            line.total(order[p - 1])
+        if 0 <= p - SPREAD < pairs and order[p - SPREAD] < hidden_pairs:
+            line.spread(order[p - SPREAD])
+        if 0 <= p - 3 < pairs:
+            line.forward(order[p - 3], False)
+        if 0 <= p - LATE < pairs:
+            line.forward(order[p - LATE], True)
+
+    def line_step(p):
+        line.sent(order[p])
+        if p + AHEAD < pairs:
+            line.send(order[p + AHEAD])
+        elif p + AHEAD == pairs:
+            small.send(0)
+        line.add(order[p])
+        line_rest(p)
 
     for copy in big:
         copy.wait()
@@ -1103,6 +1171,11 @@
     kv_core = [remote(stage[i], kv_cr.at[i], kc_s.at[i], kc_r.at[i], pc) for i in range(4)]
     for copy in kv_core:
         copy.start()
+    inputs = x[...].astype(F32)
+    inverse = lax.rsqrt(jnp.mean(inputs * inputs, axis=1, keepdims=True) + EPS)
+    normed_t = (inputs * inverse * (1.0 + gains[0:1, :])).astype(BF).T
+    feat_q = dh.shape[2] - HD
+    ao[...] = nt(dh[0, :, :feat_q], parts[0, :, :feat_q]) + nt(dh[1, :, :feat_q], parts[1, :, :feat_q])
     kv_sums = (ct.at[:, pl.ds(0, 2 * HD)], ct.at[:, pl.ds(2 * HD, 2 * HD)], rsr.at[2, :, pl.ds(0, 2 * HD)])
     kv_sends = []
     for i, device in ((3, pd), (1, px), (2, py)):
@@ -1114,8 +1187,14 @@
         copy.start()
         kv_sends.append(copy)
     kv_core[0].wait_recv()
+    for j in range(2):
+        for n in range(feat_q // TILE):
+            parts[j, :, n * TILE : (n + 1) * TILE] = nn(normed_t, dh[j, :, n * TILE : (n + 1) * TILE]).astype(BF)
+    query_sum = PlaneSum(1, 0, feat_q)
+    query_sum.begin()
     settle(EARLY)
     produce(EARLY + 1)
+    query_sum.spread()
     line_step(9)
     line_step(10)
     total = out_sum.result()
@@ -1127,44 +1206,42 @@
     grad_key = dk[:loc, :] + got[:, :HD]
     grad_value = dv[:loc, :] + got[:, HD:]
     first, second = grad_key[:, :half], grad_key[:, half:]
-    turned = jnp.concatenate(
+    turned_key = jnp.concatenate(
         [first * cos[...] + second * sin[...], second * cos[...] - first * sin[...]], axis=1
     )
-    grad, gain_buf[0, 5:6, :HD] = norm_grad(k_pre[...], gk[...], turned)
-    feat_q = dh.shape[2] - HD
+    grad, gain_buf[0, 5:6, :HD] = norm_grad(k_pre[...], gk[...], turned_key)
     for j in range(2):
         dh[j, :, feat_q : feat_q + half] = grad[:, j * half : (j + 1) * half].astype(BF)
         dh[j, :, feat_q + half :] = grad_value[:, j * half : (j + 1) * half].astype(BF)
-
-    inputs = x[...].astype(F32)
-    inverse = lax.rsqrt(jnp.mean(inputs * inputs, axis=1, keepdims=True) + EPS)
-    normed_t = (inputs * inverse * (1.0 + gains[0:1, :])).astype(BF).T
-    grad_normed = nt(dh[0], parts[0, :, :qkv]) + nt(dh[1], parts[1, :, :qkv])
+    ao[...] += nt(dh[0, :, feat_q:], parts[0, :, feat_q:qkv]) + nt(dh[1, :, feat_q:], parts[1, :, feat_q:qkv])
     for j in range(2):
-        for n in range(qkv // TILE):
-            parts[j, :, n * TILE : (n + 1) * TILE] = nn(normed_t, dh[j, :, n * TILE : (n + 1) * TILE]).astype(BF)
-    in_sum = PlaneSum(1, 0, qkv)
-    in_sum.begin()
-    grad, gain_buf[0, 0:1, :] = norm_grad(inputs, gains[0:1, :], grad_normed)
-    in_sum.spread()
+        parts[j, :, feat_q:qkv] = nn(normed_t, dh[j, :, feat_q:]).astype(BF)
+    key_sum = PlaneSum(2, feat_q, HD)
+    key_sum.begin()
+    grad, gain_buf[0, 0:1, :] = norm_grad(x[...].astype(F32), gains[0:1, :], ao[...])
+    key_sum.spread()
     for copy in lo_copies:
         copy.wait_send()
     lo_own.wait()
     cut_t[...] = (grad + own[...]).astype(BF).T
     gt_copies, gt_own = give(cut_t, gt_out, gt_s, gt_r, loc_s.at[1])
-    settle(EARLY + 1)
-    line_step(11)
     gain_copies = [
         remote(gain_buf.at[0], gain_in.at[j], gn_s.at[j], gn_r.at[j], d) for j, (_, d) in enumerate(others)
     ]
     for copy in gain_copies:
         copy.start()
-    for i in range(12, 16):
-        line_step(i)
-    total = in_sum.result()
+    settle(EARLY + 1)
+    line_step(11)
+    line_step(12)
+    line_step(13)
+    total = query_sum.result()
     for i in range(2):
         mine[hidden_pairs + 1, i] = total[:, i * TILE : (i + 1) * TILE]
-        a_mine[0, i] = total[i * depth // 2 : (i + 1) * depth // 2, 2 * TILE :]
+    line_step(14)
+    line_step(15)
+    total = key_sum.result()
+    for i in range(2):
+        a_mine[0, i] = total[i * depth // 2 : (i + 1) * depth // 2]
     for copy in gain_copies:
         copy.wait()
     gain_buf[1] = gain_buf[0] + sum(gain_in[j] for j in range(7))
@@ -1175,20 +1252,17 @@
     for copy in gain_copies:
         copy.start()
 
-    def step(k, carry):
-        line_step(k)
-        pl.when(k == pairs - 1 - AHEAD)(lambda: small.send(0))
-        return carry
-
-    lax.fori_loop(16, pairs, step, 0)
+    for p in range(16, pairs):
+        line_step(p)
     small.sent(0)
     small.add(0)
-    line.total(pairs - 1)
-    line.forward(pairs - 3)
+    line_rest(pairs)
     small.total(0)
-    line.forward(pairs - 2)
-    line.forward(pairs - 1)
-    small.forward(0)
+    for p in range(pairs + 1, pairs + 4):
+        line_rest(p)
+    small.forward(0, False)
+    for p in range(pairs + 4, pairs + LATE):
+        line_rest(p)
 
     def drain(k, carry):
         line.drain(k)
@@ -1226,19 +1300,21 @@
     return pl.pallas_call(
         back_kernel,
         out_shape=(
-            struct((pairs, 2) + piece, BF),
-            struct((1, 2) + rest, BF),
+            struct((depth, 2 * hh.shape[1]), BF),
+            struct((depth, 2 * hh.shape[1]), BF),
+            struct((depth, 2 * hh.shape[1]), BF),
+            struct((depth, feats), BF),
             struct((cut, keys), BF),
             struct((cut, keys), BF),
             struct((8, width), F32),
         ),
         in_specs=[any_spec()] * 17 + [vmem_spec()] * 7,
-        out_specs=[any_spec()] * 4 + [vmem_spec()],
+        out_specs=[any_spec()] * 6 + [vmem_spec()],
         scratch_shapes=[
             vmem((pairs, 2) + piece, BF),
             vmem((pairs, 2) + piece, BF),
             vmem((pairs,) + piece, BF),
-            vmem((hidden_pairs,) + piece, BF),
+            vmem(((hidden_pairs + 1) // 2,) + piece, BF),
             vmem((1, 2) + rest, BF),
             vmem((1, 2) + rest, BF),
             vmem((1,) + rest, BF),
@@ -1265,7 +1341,7 @@
             vmem((10, 8, width), F32),
             dma((12,)), dma((3,)), dma((2,)), dma(()), dma((3,)), dma((3,)), dma((3, 2)), dma((hidden_pairs, 2)),
             dma((4,)), dma((4,)), dma((3,)), dma((3,)),
-            dma((2, 4)), dma((2, 4)), dma((2, 3)), dma((2, 3)),
+            dma((3, 4)), dma((3, 4)), dma((3, 3)), dma((3, 3)),
             dma((7,)), dma((7,)), dma((7,)), dma((7,)), dma((10,)), dma((10,)), dma((2,)),
         ]
         + line_sems(pairs)
@@ -1273,33 +1349,6 @@
         compiler_params=params(6),
         name="attention_back",
     )(*args)
-
-
-def finish_kernel(high, gate_in, up_in, down_in, gate, up, down):
-    gate[...] = gate_in[0, 0].astype(F32)
-    up[...] = up_in[0, 0].astype(F32)
-    down[...] = down_in[0, 0].astype(F32)
-
-
-def finish(pieces, high, hidden, tiles):
-    depth = pieces.shape[2]
-
-    def source(m):
-        return pl.BlockSpec(
-            (1, 1, depth, TILE), lambda i, high: (3 * (i % tiles) + m, (i // tiles + high[0]) % 2, 0, 0)
-        )
-
-    return pl.pallas_call(
-        finish_kernel,
-        grid_spec=pltpu.PrefetchScalarGridSpec(
-            num_scalar_prefetch=1,
-            grid=(-(-hidden // TILE),),
-            in_specs=[source(m) for m in range(3)],
-            out_specs=[pl.BlockSpec((depth, TILE), lambda i, high: (0, i))] * 3,
-        ),
-        out_shape=[jax.ShapeDtypeStruct((depth, hidden), F32)] * 3,
-        name="finish",
-    )(high, pieces, pieces, pieces)
 
 
 def body(
@@ -1338,29 +1387,27 @@
     layer_rows, grad_g_post, grad_own, grad_parts, pre_t, grad_mlp_t, hidden, grad_gate, grad_up = mlp(
         pre_normed, residual, upstream, gains, w_hidden
     )
-    tiles = hidden.shape[1] // TILE
-    summed, attn_rest, layer_cut, token_cut, gain_sums = attention_back(
+    sum_gate, sum_up, sum_down, attn_sum, layer_cut, token_cut, gain_sums = attention_back(
         grad_parts, pre_t, grad_mlp_t, hidden, grad_gate, grad_up, grad_own, layer_rows, attn_out, upstream,
         inputs, head_bf, query_pre, key_pre, kv_all, bias, w_attn, gains, gain_query[None], gain_key[None],
         log_total, cos_table, sin_table, grad_g_post,
     )
     if lax.axis_size("dp") != 4:
-        summed, attn_rest, gain_sums = (lax.psum(v.astype(F32), "dp") for v in (summed, attn_rest, gain_sums))
-    grad_gate, grad_up, grad_down = finish(summed, (row // 2)[None], hidden_half, tiles)
-    attn_mine = jnp.concatenate(
-        [summed[-1, 0], summed[-1, 1], attn_rest[0].reshape(depth, -1), summed[-2, 0], summed[-2, 1]], axis=1
-    ).astype(F32)
+        sum_gate, sum_up, sum_down, attn_sum, gain_sums = (
+            lax.psum(v.astype(F32), "dp") for v in (sum_gate, sum_up, sum_down, attn_sum, gain_sums)
+        )
+    attn_sum = attn_sum.astype(F32)
     my_gains = lax.dynamic_slice_in_dim(gain_sums[:4], me * cut, cut, 1)
     return (
         layer_cut.T,
         token_cut.T.astype(F32),
-        attn_mine[:, :q_half],
-        attn_mine[:, q_half : q_half + kv_half],
-        attn_mine[:, q_half + kv_half : qkv_half],
-        attn_mine[:, qkv_half:].T,
-        grad_gate,
-        grad_up,
-        grad_down.T,
+        attn_sum[:, :q_half],
+        attn_sum[:, q_half : q_half + kv_half],
+        attn_sum[:, q_half + kv_half : qkv_half],
+        attn_sum[:, qkv_half:].T,
+        sum_gate[:, :hidden_half].astype(F32),
+        sum_up[:, :hidden_half].astype(F32),
+        sum_down[:, :hidden_half].astype(F32).T,
         my_gains[0],
         my_gains[1],
         my_gains[2],

time: 481 us -> 431 us (0.90)
  Pallas kernels: 459 us -> 406 us
  other arithmetic: 2.57 us -> 10.9 us
    pallas_call x2 -> x1, Pallas kernels: 237 us -> 210 us  [attention_back(): pl.pallas_call(back_kernel, out_shape=(struct((depth, 2 * hh.shape[1]), B...]
    pallas_call x1, Pallas kernels: 115 us -> 101 us  [attention_front(): pl.pallas_call(front_kernel, out_shape=(struct((3, width, slab), BF), str...]
    pallas_call x1, Pallas kernels: 107 us -> 94.2 us  [mlp(): pl.pallas_call(mlp_kernel, out_shape=(struct((loc, width), BF), struct((1...]
    transpose x0 -> x1, other arithmetic: none -> 6.11 us  [body(): sum_down[:, :hidden_half].astype(F32)]
where the time goes in v4:
time: 431 us; the launch traced here: 423 us
  Pallas kernels  406 us (94%)
  other arithmetic  10.9 us (3%)
  local copies, waits for them, and re-layouts  4.62 us (1%)
    pallas_call x1, Pallas kernels, attention_back(): pl.pallas_call(back_kernel, out_shape=(struct((depth, 2 * hh.shape[1]), B...  210 us
    pallas_call x1, Pallas kernels, attention_front(): pl.pallas_call(front_kernel, out_shape=(struct((3, width, slab), BF), str...  101 us
    pallas_call x1, Pallas kernels, mlp(): pl.pallas_call(mlp_kernel, out_shape=(struct((loc, width), BF), struct((1...  94.2 us

profile of v4, /device:TPU:0, one launch (start us, length us, event | category | flops | bytes accessed | tf_op | source)
XLA Modules:
  0.0 422.9 jit_solution(2803451490065962644)
XLA Ops:
  0.6 1.3 select_maximum_fusion.gain_block
  2.6 100.9 %attention_front.1 = (bf16[3,1152,1792]{2,1,0:T(8,128)(2,1)}, bf16[2,1152,1280]{2,1,0:T(8,128)(2,1)}, bf16[2048,512]{1,0:T(8,128)(2,1)}, bf16[2048,256]{1,0:T(8,...) custom-call(bf16[144,2048]{1,0:T(8,128)(2,1)} %bitcast.24, ...), custom_call_target="tpu_custom_call" | custom-call | tf_op jit(solution)/shard_map/attention_front/pallas_call | solution.py:467
  103.6 94.2 %feed_forward.1 = (bf16[256,1152]{1,0:T(8,128)(2,1)}, f32[1,1152]{1,0:T(1,128)}, f32[256,1152]{1,0:T(8,128)}, bf16[3,256,1152]{2,1,0:T(8,128)(2,1)}, bf16[1152,1...) custom-call(bf16[256,1152]{1,0:T(8,128)(2,1)} %get-tuple-element.47., ...), custom_call_target="tpu_custom_call" | custom-call | tf_op jit(solution)/shard_map/feed_forward/pallas_call | solution.py:651
  197.7 210.5 %attention_back.1 = (bf16[288,3584]{1,0:T(8,128)(2,1)}, bf16[288,3584]{1,0:T(8,128)(2,1)}, bf16[288,3584]{1,0:T(8,128)(2,1)}, bf16[288,1280]{1,0:T(8,128)(2,1)},...) custom-call(bf16[3,256,1152]{2,1,0:T(8,128)(2,1)} %get-tuple-element.52.dparts, ...), custom_call_target="tpu_custom_call" | custom-call | tf_op jit(solution)/shard_map/attention_back/pallas_call | solution.py:1300
  408.2 0.0 copy-start.1
  408.2 6.1 %convert_bitcast_fusion = (f32[3456,288]{0,1:T(8,128)}, f32[288,3456]{1,0:T(8,128)}) fusion(bf16[288,3584]{1,0:T(8,128)(2,1)} %get-tuple-element.77, bf16[288,3584]{1,0:T(8,128)(2,1)} %get-tuple-element.76), kind=kLoop, calls=%fused_computation | loop fusion | flops 1990656 | bytes 11943936 | tf_op jit(solution)/shard_map/transpose | solution.py:1410
  414.3 0.0 copy-done.1
  414.3 0.0 copy-start
  414.4 2.2 slice_convert_fusion.1
  416.5 0.0 copy-start.2
  416.6 0.0 copy-done
  416.6 0.1 convert_element_type.20
  416.7 0.9 slice_bitcast_fusion
  417.5 0.0 copy-start.4
  417.6 0.0 copy-start.3
  417.6 0.1 copy-done.2
  417.6 1.1 convert_bitcast_fusion.1
  418.8 0.9 slice.56
  419.6 0.7 fusion
  420.4 0.0 copy-done.4
  420.4 0.7 fusion.2
  421.0 0.6 fusion.1
  421.6 0.0 copy-done.3
  421.6 0.8 copy.34
  (1 shorter events, 0.0 us)
Async XLA Ops:
  408.2 6.1 %copy-start.1 = (bf16[288,3584]{1,0:T(8,128)(2,1)S(1)}, bf16[288,3584]{1,0:T(8,128)(2,1)}, u32[]{:S(2)}) copy-start(bf16[288,3584]{1,0:T(8,128)(2,1)} %get-tuple-element.75) | copy-start | bytes 6193156
  414.3 2.2 copy-start
  416.5 1.1 copy-start.2
  417.5 2.8 copy-start.4
  417.6 4.0 copy-start.3

commit v5 on v4

--- a/solution.py
+++ b/solution.py
@@ -215,8 +215,6 @@
                 )
                 attn_copies[i, j].start()
 
-    hand_out(0)
-
     for copy in loads:
         copy.wait()
     for m in range(3):
@@ -248,7 +246,10 @@
         own_hidden[m].start()
         beside[m].start()
     fetched = [rounds * r + place for r in range(rounds)] + [extra] if share else list(range(groups))
-    for g in fetched:
+    for g in fetched[:rounds]:
+        over(g).start()
+    hand_out(0)
+    for g in fetched[rounds:]:
         over(g).start()
 
     def travel(distance, r, act_up, act_down):
@@ -363,6 +364,7 @@
         for j in range(3):
             passed[which, j].wait_recv()
 
+    poll(4)
     pass_on(0)
     poll(1)
     settled(0)
@@ -1351,6 +1353,35 @@
     )(*args)
 
 
+def finish_kernel(gate_in, up_in, down_in, attn_in, tok_in, gate, up, down, wq, wk, wv, wo, tok):
+    for src, dst in ((gate_in, gate), (up_in, up), (down_in, down)):
+        dst[...] = src[:, : dst.shape[1]].astype(F32)
+    at = 0
+    for dst in (wq, wk, wv, wo):
+        dst[...] = attn_in[:, at : at + dst.shape[1]].astype(F32)
+        at += dst.shape[1]
+    tok[...] = tok_in[...].astype(F32)
+
+
+def finish(gate, up, down, attn, tok, hidden, widths):
+    depth, cut = gate.shape[0], tok.shape[0]
+    steps = cut // 16
+    outs = [(depth, hidden)] * 3 + [(depth, width) for width in widths] + [tok.shape]
+
+    def rows(shape):
+        return pl.BlockSpec((shape[0] // steps, shape[1]), lambda i: (i, 0))
+
+    return pl.pallas_call(
+        finish_kernel,
+        grid=(steps,),
+        in_specs=[rows(array.shape) for array in (gate, up, down, attn, tok)],
+        out_specs=[rows(shape) for shape in outs],
+        out_shape=[jax.ShapeDtypeStruct(shape, F32) for shape in outs],
+        compiler_params=pltpu.CompilerParams(vmem_limit_bytes=VMEM_LIMIT),
+        name="finish",
+    )(gate, up, down, attn, tok)
+
+
 def body(
     tokens,
     cotangent,
@@ -1375,7 +1406,6 @@
     me = row * lax.axis_size("col") + col
     depth, hidden_half = weight_gate.shape
     q_half, kv_half = weight_query.shape[1], weight_key.shape[1]
-    qkv_half = q_half + 2 * kv_half
     gain_block = jnp.pad(jnp.stack([gain_input, gain_attn, gain_pre, gain_post]), ((0, 4), (0, 0)))
     (
         w_hidden, w_attn, kv_all, bias, inputs, upstream, gains, query_pre, key_pre, log_total,
@@ -1396,18 +1426,20 @@
         sum_gate, sum_up, sum_down, attn_sum, gain_sums = (
             lax.psum(v.astype(F32), "dp") for v in (sum_gate, sum_up, sum_down, attn_sum, gain_sums)
         )
-    attn_sum = attn_sum.astype(F32)
+    grad_gate, grad_up, grad_down, grad_query, grad_key, grad_value, grad_out, grad_tokens = finish(
+        sum_gate, sum_up, sum_down, attn_sum, token_cut, hidden_half, (q_half, kv_half, kv_half, q_half)
+    )
     my_gains = lax.dynamic_slice_in_dim(gain_sums[:4], me * cut, cut, 1)
     return (
         layer_cut.T,
-        token_cut.T.astype(F32),
-        attn_sum[:, :q_half],
-        attn_sum[:, q_half : q_half + kv_half],
-        attn_sum[:, q_half + kv_half : qkv_half],
-        attn_sum[:, qkv_half:].T,
-        sum_gate[:, :hidden_half].astype(F32),
-        sum_up[:, :hidden_half].astype(F32),
-        sum_down[:, :hidden_half].astype(F32).T,
+        grad_tokens.T,
+        grad_query,
+        grad_key,
+        grad_value,
+        grad_out.T,
+        grad_gate,
+        grad_up,
+        grad_down.T,
         my_gains[0],
         my_gains[1],
         my_gains[2],

time: 431 us -> 423 us (0.981)
  the two profiles are of different devices: /device:TPU:0 before, /device:TPU:30 now
where the time goes in v5:
time: 423 us; the launch traced here: 415 us
  Pallas kernels  409 us (97%)
    pallas_call x1, Pallas kernels, attention_back(): pl.pallas_call(back_kernel, out_shape=(struct((depth, 2 * hh.shape[1]), B...  214 us
    pallas_call x1, Pallas kernels, mlp(): pl.pallas_call(mlp_kernel, out_shape=(struct((loc, width), BF), struct((1...  94.4 us
    pallas_call x1, Pallas kernels, attention_front(): pl.pallas_call(front_kernel, out_shape=(struct((3, width, slab), BF), str...  90.7 us
    pallas_call x1, Pallas kernels, finish(): pl.pallas_call(finish_kernel, grid=(steps,), in_specs=[rows(array.shape)...  10.1 us

profile of v5, /device:TPU:30, one launch (start us, length us, event | category | flops | bytes accessed | tf_op | source)
XLA Modules:
  0.0 415.0 jit_solution(4969834851558438863)
XLA Ops:
  0.6 1.3 select_maximum_fusion.gain_block
  2.6 90.7 %attention_front.1 = (bf16[3,1152,1792]{2,1,0:T(8,128)(2,1)}, bf16[2,1152,1280]{2,1,0:T(8,128)(2,1)}, bf16[2048,512]{1,0:T(8,128)(2,1)}, bf16[2048,256]{1,0:T(8,...) custom-call(bf16[144,2048]{1,0:T(8,128)(2,1)} %bitcast.21, ...), custom_call_target="tpu_custom_call" | custom-call | tf_op jit(solution)/shard_map/attention_front/pallas_call | solution.py:469
  93.3 94.4 %feed_forward.1 = (bf16[256,1152]{1,0:T(8,128)(2,1)}, f32[1,1152]{1,0:T(1,128)}, f32[256,1152]{1,0:T(8,128)}, bf16[3,256,1152]{2,1,0:T(8,128)(2,1)}, bf16[1152,1...) custom-call(bf16[256,1152]{1,0:T(8,128)(2,1)} %get-tuple-element.55., ...), custom_call_target="tpu_custom_call" | custom-call | tf_op jit(solution)/shard_map/feed_forward/pallas_call | solution.py:653
  187.7 213.6 %attention_back.1 = (bf16[288,3584]{1,0:T(8,128)(2,1)}, bf16[288,3584]{1,0:T(8,128)(2,1)}, bf16[288,3584]{1,0:T(8,128)(2,1)}, bf16[288,1280]{1,0:T(8,128)(2,1)},...) custom-call(bf16[3,256,1152]{2,1,0:T(8,128)(2,1)} %get-tuple-element.60.dparts, ...), custom_call_target="tpu_custom_call" | custom-call | tf_op jit(solution)/shard_map/attention_back/pallas_call | solution.py:1302
  401.3 0.0 copy-start
  401.3 10.1 %finish.1 = (f32[288,3456]{1,0:T(8,128)}, f32[288,3456]{1,0:T(8,128)}, f32[288,3456]{1,0:T(8,128)}, f32[288,512]{1,0:T(8,128)}, f32[288,128]{1,0:T(8,128)}, /*in...) custom-call(bf16[288,3584]{1,0:T(8,128)(2,1)} %get-tuple-element.81.gate_in, ...), custom_call_target="tpu_custom_call" | custom-call | tf_op jit(solution)/shard_map/finish/pallas_call | solution.py:1374
  411.4 0.0 copy-done
  411.4 0.7 fusion.1
  412.1 0.6 fusion
  412.6 1.9 copy.34
  (1 shorter events, 0.0 us)
Async XLA Ops:
  401.3 10.1 %copy-start = (f32[8,1152]{1,0:T(8,128)S(1)}, f32[8,1152]{1,0:T(8,128)}, u32[]{:S(2)}) copy-start(f32[8,1152]{1,0:T(8,128)} %get-tuple-element.94) | copy-start | bytes 110596

commit v6 on v5

--- a/solution.py
+++ b/solution.py
@@ -364,17 +364,16 @@
         for j in range(3):
             passed[which, j].wait_recv()
 
-    poll(4)
+    poll(5)
     pass_on(0)
     poll(1)
     settled(0)
     poll(1)
     q_half, kv_half = wq.shape[1], wk.shape[1]
     for j in range(2):
-        found = nn(normed, wa[j, :, :qkv])
-        q_pre[:, j * q_half : (j + 1) * q_half] = found[:, :q_half]
-        k_pre[:, j * kv_half : (j + 1) * kv_half] = found[:, q_half : q_half + kv_half]
-        kv[:loc, HD + j * kv_half : HD + (j + 1) * kv_half] = found[:, q_half + kv_half :].astype(BF)
+        found = nn(normed, wa[j, :, q_half:qkv])
+        k_pre[:, j * kv_half : (j + 1) * kv_half] = found[:, :kv_half]
+        kv[:loc, HD + j * kv_half : HD + (j + 1) * kv_half] = found[:, kv_half:].astype(BF)
     kv[:loc, :HD] = head_forward(k_pre[...], gk[...], cos[...], sin[...]).astype(BF)
     kv_first = [
         remote(kv.at[pl.ds(0, loc)], kv.at[pl.ds(slot * loc, loc)], kv_s.at[i], kv_r.at[i], device)
@@ -383,6 +382,8 @@
     for copy in kv_first:
         copy.start()
     hand_out(1)
+    for j in range(2):
+        q_pre[:, j * q_half : (j + 1) * q_half] = nn(normed, wa[j, :, :q_half])
     ct_copies = scatter(ct, ct_all, ct_s, ct_r)
     for h in range(head_count):
         cols = slice(h * HD, (h + 1) * HD)
@@ -558,7 +559,6 @@
 
     def forward(j, carry):
         got_chunk(j, pre_all, ag_s, ag_r)
-        acc[...] = jnp.zeros_like(acc)
         rows = chunk_rows(j)
         for n in range(tiles):
             at = slice(n * TILE, (n + 1) * TILE)
@@ -574,7 +574,7 @@
             aa[rows, at] = gelu.astype(BF)
             bb[rows, at] = (up * slope).astype(BF)
             hh[rows, at] = hidden
-            acc[...] += nt(hidden, wd[:, at])
+        acc[...] = nt(hh[rows, :], wd[...])
         store(0, j, hh, hh_out).start()
 
         @pl.when(j == 0)
@@ -608,7 +608,6 @@
     gathers2 = spread(gm_all.at[0], gm_all, gs_s, gs_r)
     def backward(j, carry):
         got_chunk(j, gm_all, gs_s, gs_r)
-        acc[...] = jnp.zeros_like(acc)
         rows = chunk_rows(j)
         for n in range(tiles):
             at = slice(n * TILE, (n + 1) * TILE)
@@ -617,7 +616,7 @@
             grad_up = (grad_hidden * aa[rows, at].astype(F32)).astype(BF)
             bb[rows, at] = grad_gate
             aa[rows, at] = grad_up
-            acc[...] += nt(grad_gate, wg[:, at]) + nt(grad_up, wu[:, at])
+        acc[...] = nt(bb[rows, :], wg[...]) + nt(aa[rows, :], wu[...])
         gm_t[:, rows] = gm_all[j].T
         store(1, j, bb, bb_out).start()
         store(2, j, aa, aa_out).start()

time: 423 us -> 415 us (0.981)
  the two profiles are of different devices: /device:TPU:30 before, /device:TPU:0 now
where the time goes in v6:
time: 415 us; the launch traced here: 407 us
  Pallas kernels  401 us (97%)
    pallas_call x1, Pallas kernels, attention_back(): pl.pallas_call(back_kernel, out_shape=(struct((depth, 2 * hh.shape[1]), B...  208 us
    pallas_call x1, Pallas kernels, mlp(): pl.pallas_call(mlp_kernel, out_shape=(struct((loc, width), BF), struct((1...  91.9 us
    pallas_call x1, Pallas kernels, attention_front(): pl.pallas_call(front_kernel, out_shape=(struct((3, width, slab), BF), str...  91.4 us
    pallas_call x1, Pallas kernels, finish(): pl.pallas_call(finish_kernel, grid=(steps,), in_specs=[rows(array.shape)...  10.1 us

profile of v6, /device:TPU:0, one launch (start us, length us, event | category | flops | bytes accessed | tf_op | source)
XLA Modules:
  0.0 407.3 jit_solution(9607184579140157519)
XLA Ops:
  0.6 1.3 select_maximum_fusion.gain_block
  2.6 91.4 %attention_front.1 = (bf16[3,1152,1792]{2,1,0:T(8,128)(2,1)}, bf16[2,1152,1280]{2,1,0:T(8,128)(2,1)}, bf16[2048,512]{1,0:T(8,128)(2,1)}, bf16[2048,256]{1,0:T(8,...) custom-call(bf16[144,2048]{1,0:T(8,128)(2,1)} %bitcast.21, ...), custom_call_target="tpu_custom_call" | custom-call | tf_op jit(solution)/shard_map/attention_front/pallas_call | solution.py:470
  94.1 91.9 %feed_forward.1 = (bf16[256,1152]{1,0:T(8,128)(2,1)}, f32[1,1152]{1,0:T(1,128)}, f32[256,1152]{1,0:T(8,128)}, bf16[3,256,1152]{2,1,0:T(8,128)(2,1)}, bf16[1152,1...) custom-call(bf16[256,1152]{1,0:T(8,128)(2,1)} %get-tuple-element.55., ...), custom_call_target="tpu_custom_call" | custom-call | tf_op jit(solution)/shard_map/feed_forward/pallas_call | solution.py:652
  186.0 207.7 %attention_back.1 = (bf16[288,3584]{1,0:T(8,128)(2,1)}, bf16[288,3584]{1,0:T(8,128)(2,1)}, bf16[288,3584]{1,0:T(8,128)(2,1)}, bf16[288,1280]{1,0:T(8,128)(2,1)},...) custom-call(bf16[3,256,1152]{2,1,0:T(8,128)(2,1)} %get-tuple-element.60.dparts, ...), custom_call_target="tpu_custom_call" | custom-call | tf_op jit(solution)/shard_map/attention_back/pallas_call | solution.py:1301
  393.6 0.0 copy-start
  393.6 10.1 %finish.1 = (f32[288,3456]{1,0:T(8,128)}, f32[288,3456]{1,0:T(8,128)}, f32[288,3456]{1,0:T(8,128)}, f32[288,512]{1,0:T(8,128)}, f32[288,128]{1,0:T(8,128)}, /*in...) custom-call(bf16[288,3584]{1,0:T(8,128)(2,1)} %get-tuple-element.81.gate_in, ...), custom_call_target="tpu_custom_call" | custom-call | tf_op jit(solution)/shard_map/finish/pallas_call | solution.py:1373
  403.7 0.0 copy-done
  403.7 0.7 fusion.1
  404.4 0.6 fusion
  405.0 1.9 copy.34
  (1 shorter events, 0.0 us)
Async XLA Ops:
  393.6 10.1 %copy-start = (f32[8,1152]{1,0:T(8,128)S(1)}, f32[8,1152]{1,0:T(8,128)}, u32[]{:S(2)}) copy-start(f32[8,1152]{1,0:T(8,128)} %get-tuple-element.94) | copy-start | bytes 110596

commit v7 on v6

--- a/solution.py
+++ b/solution.py
@@ -1021,8 +1021,8 @@
         for i in range(3 * n - 3, min(3 * n, AHEAD)):
             line.send(i)
         produce(n)
-        if n >= EARLY - 2:
-            line_step(n + 2 - EARLY)
+        if n >= EARLY - 3:
+            line_step(n + 3 - EARLY)
 
     here = pl.ds(pl.multiple_of(me * loc, 128), loc)
 
@@ -1053,7 +1053,6 @@
     k_t[...] = kv[:, :HD].T
     settle(EARLY - 1)
     produce(EARLY)
-    line_step(2)
     for copy in scatters:
         copy.wait()
     grad_pre = own[...] + rsr[0].astype(F32) + rsr[1].astype(F32) + rsr[2].astype(F32)
@@ -1364,7 +1363,7 @@
 
 def finish(gate, up, down, attn, tok, hidden, widths):
     depth, cut = gate.shape[0], tok.shape[0]
-    steps = cut // 16
+    steps = cut // 48
     outs = [(depth, hidden)] * 3 + [(depth, width) for width in widths] + [tok.shape]
 
     def rows(shape):

time: 415 us -> 413 us (level)
  no operation moved by 1% of the time
where the time goes in v7:
time: 413 us; the launch traced here: 405 us
  Pallas kernels  399 us (97%)
    pallas_call x1, Pallas kernels, attention_back(): pl.pallas_call(back_kernel, out_shape=(struct((depth, 2 * hh.shape[1]), B...  208 us
    pallas_call x1, Pallas kernels, mlp(): pl.pallas_call(mlp_kernel, out_shape=(struct((loc, width), BF), struct((1...  91.9 us
    pallas_call x1, Pallas kernels, attention_front(): pl.pallas_call(front_kernel, out_shape=(struct((3, width, slab), BF), str...  91.4 us

profile of v7, /device:TPU:0, one launch (start us, length us, event | category | flops | bytes accessed | tf_op | source)
XLA Modules:
  0.0 405.1 jit_solution(12124829049548607816)
XLA Ops:
  0.6 1.3 select_maximum_fusion.gain_block
  2.6 91.4 %attention_front.1 = (bf16[3,1152,1792]{2,1,0:T(8,128)(2,1)}, bf16[2,1152,1280]{2,1,0:T(8,128)(2,1)}, bf16[2048,512]{1,0:T(8,128)(2,1)}, bf16[2048,256]{1,0:T(8,...) custom-call(bf16[144,2048]{1,0:T(8,128)(2,1)} %bitcast.21, ...), custom_call_target="tpu_custom_call" | custom-call | tf_op jit(solution)/shard_map/attention_front/pallas_call | solution.py:470
  94.1 91.9 %feed_forward.1 = (bf16[256,1152]{1,0:T(8,128)(2,1)}, f32[1,1152]{1,0:T(1,128)}, f32[256,1152]{1,0:T(8,128)}, bf16[3,256,1152]{2,1,0:T(8,128)(2,1)}, bf16[1152,1...) custom-call(bf16[256,1152]{1,0:T(8,128)(2,1)} %get-tuple-element.55., ...), custom_call_target="tpu_custom_call" | custom-call | tf_op jit(solution)/shard_map/feed_forward/pallas_call | solution.py:652
  186.0 207.6 %attention_back.1 = (bf16[288,3584]{1,0:T(8,128)(2,1)}, bf16[288,3584]{1,0:T(8,128)(2,1)}, bf16[288,3584]{1,0:T(8,128)(2,1)}, bf16[288,1280]{1,0:T(8,128)(2,1)},...) custom-call(bf16[3,256,1152]{2,1,0:T(8,128)(2,1)} %get-tuple-element.60.dparts, ...), custom_call_target="tpu_custom_call" | custom-call | tf_op jit(solution)/shard_map/attention_back/pallas_call | solution.py:1300
  393.6 0.0 copy-start
  393.6 7.9 %finish.1 = (f32[288,3456]{1,0:T(8,128)}, f32[288,3456]{1,0:T(8,128)}, f32[288,3456]{1,0:T(8,128)}, f32[288,512]{1,0:T(8,128)}, f32[288,128]{1,0:T(8,128)}, /*in...) custom-call(bf16[288,3584]{1,0:T(8,128)(2,1)} %get-tuple-element.81.gate_in, ...), custom_call_target="tpu_custom_call" | custom-call | tf_op jit(solution)/shard_map/finish/pallas_call | solution.py:1372
  401.5 0.0 copy-done
  401.5 0.7 fusion.1
  402.2 0.6 fusion
  402.7 1.9 copy.34
  (1 shorter events, 0.0 us)
Async XLA Ops:
  393.6 7.9 %copy-start = (f32[8,1152]{1,0:T(8,128)S(1)}, f32[8,1152]{1,0:T(8,128)}, u32[]{:S(2)}) copy-start(f32[8,1152]{1,0:T(8,128)} %get-tuple-element.94) | copy-start | bytes 110596
